TPU v7x, 256 devices: a whole 4x4x8 slice. The times are simulated.
256 devices in a mesh: col: 16 (over y, x), height: 16 (over z, core).
Axes of the slice: x: 4, y: 4, z: 8, core: 2. Of those that a mesh axis runs over, the one named last changes fastest.
Arguments:
- orbitals: bfloat16 [192, 128, 256, 128], P('col', 'height'), may hold values from -6 to 6
- live_atoms: int32 [192, 128], P('col', 'height'), may hold values from 1 to 4
- pair_index: int32 [192, 128, 4, 4], P('col', 'height'), may hold values from 0 to 255
- density_blocks: bfloat16 [4096, 64, 64], P(('col', 'height')), may hold values from -0.0234375 to 0.0234375
Outputs:
- potential: float32 [192, 128, 128], P('col', 'height')
- hamiltonian: float32 [4096, 64, 64], P(('col', 'height'))
Inputs may be any that keep to these rules, and one draw needn't show every extreme that they name: A line's live atom blocks are its first live_atoms blocks. `pair_index`: indices are local to the column group: line x uses blocks x // 12 * 256 onward.
All inputs are finite; a program needn't handle non-finite values.
Results may differ from a plain program's by a relative error of at most 0.006.
Values may be sent and summed in bfloat16 or wider, within the bound.
No kernel may reach another device: no remote copies, remote signals or barrier semaphores. Data moves between devices by JAX's collectives and lax.ppermute only.
A program may use at most 128 MiB of HBM per device.

v0:
```python
import math

import jax
import jax.numpy as jnp
from jax import lax
from jax.sharding import PartitionSpec as P

XC_COEF = 0.7386
FOUR_PI = 12.566370614359172
KAPPA = 0.5


def cas_table(count):
    steps = jnp.arange(count, dtype=jnp.int32)
    wrapped = steps[:, None] * steps[None, :] % count
    angle = 2.0 * jnp.pi * wrapped.astype(jnp.float32) / count
    return jnp.cos(angle) + jnp.sin(angle)


def symbol(steps, count):
    return 2.0 - 2.0 * jnp.cos(2.0 * jnp.pi * steps.astype(jnp.float32) / count)


def screened_solve(density):
    highest = lax.Precision.HIGHEST
    cells_x, cells_z, line_cells = density.shape
    full_x = cells_x * lax.axis_size("col")
    full_z = cells_z * lax.axis_size("height")
    table_y = cas_table(line_cells)
    table_z = cas_table(full_z)
    table_x = cas_table(full_x)
    spectrum = jnp.einsum("xzy,yk->xzk", density, table_y, precision=highest)
    spectrum = lax.all_to_all(spectrum, "height", split_axis=2, concat_axis=1, tiled=True)
    spectrum = jnp.einsum("xzy,zk->xky", spectrum, table_z, precision=highest)
    spectrum = lax.all_to_all(spectrum, "col", split_axis=1, concat_axis=0, tiled=True)
    spectrum = jnp.einsum("xzy,xk->kzy", spectrum, table_x, precision=highest)
    z_piece = spectrum.shape[1]
    y_piece = spectrum.shape[2]
    z_index = lax.axis_index("col") * z_piece + jnp.arange(z_piece, dtype=jnp.int32)
    y_index = lax.axis_index("height") * y_piece + jnp.arange(y_piece, dtype=jnp.int32)
    symbol_sum = (
        symbol(jnp.arange(full_x, dtype=jnp.int32), full_x)[:, None, None]
        + symbol(z_index, full_z)[None, :, None]
        + symbol(y_index, line_cells)[None, None, :]
    )
    spectrum = spectrum * (FOUR_PI / (symbol_sum + KAPPA * KAPPA))
    spectrum = jnp.einsum("xzy,xk->kzy", spectrum, table_x, precision=highest)
    spectrum = lax.all_to_all(spectrum, "col", split_axis=0, concat_axis=1, tiled=True)
    spectrum = jnp.einsum("xzy,zk->xky", spectrum, table_z, precision=highest)
    spectrum = lax.all_to_all(spectrum, "height", split_axis=1, concat_axis=2, tiled=True)
    spectrum = jnp.einsum("xzy,yk->xzk", spectrum, table_y, precision=highest)
    return spectrum / (full_x * full_z * line_cells)


def per_device(orbitals, live_atoms, pair_index, density_blocks):
    cells_x, cells_z, orbital_width, line_cells = orbitals.shape
    atom_count = pair_index.shape[2]
    orbital_count = orbital_width // atom_count
    blocks = lax.all_gather(density_blocks, "height", axis=0, tiled=True)
    block_count = blocks.shape[0]
    tile_count = cells_x * cells_z
    group_size = math.gcd(tile_count, 16)
    groups = tile_count // group_size
    atom_of = jnp.arange(orbital_width, dtype=jnp.int32) // orbital_count
    live_mask = (atom_of[None, :] < live_atoms.reshape(tile_count)[:, None]).astype(jnp.bfloat16)
    masked = orbitals.reshape(tile_count, orbital_width, line_cells) * live_mask[:, :, None]
    atom_rows = masked.reshape(groups, group_size, atom_count, orbital_count, line_cells)
    pair_groups = pair_index.reshape(groups, group_size, atom_count, atom_count)

    def group_density(operands):
        orbital_row_values, pair_row_values = operands
        chosen = blocks[pair_row_values]
        product = jnp.einsum(
            "nabij,nbjy->naiy", chosen, orbital_row_values, preferred_element_type=jnp.float32
        )
        return jnp.sum(orbital_row_values.astype(jnp.float32) * product, axis=(1, 2))

    density = lax.map(group_density, (atom_rows, pair_groups)).reshape(cells_x, cells_z, line_cells)
    exchange_contribution = -XC_COEF * jnp.power(density * density + 1.0, 1.0 / 6.0)
    potential = screened_solve(density) + exchange_contribution
    potential_groups = potential.reshape(groups, group_size, line_cells)
    block_ids = jnp.arange(block_count, dtype=jnp.int32)

    def group_terms(summed, operands):
        orbital_row_values, pair_row_values, potential_rows = operands
        weight_applied = (
            orbital_row_values.astype(jnp.float32) * potential_rows[:, None, None, :]
        ).astype(jnp.bfloat16)
        full_block = jnp.einsum(
            "naiy,nbjy->nabij",
            weight_applied,
            orbital_row_values,
            preferred_element_type=jnp.float32,
        )
        pieces = full_block.reshape(
            group_size * atom_count * atom_count, orbital_count * orbital_count
        )
        high_part = pieces.astype(jnp.bfloat16)
        low_part = (pieces - high_part.astype(jnp.float32)).astype(jnp.bfloat16)
        selector = (pair_row_values.reshape(-1)[:, None] == block_ids[None, :]).astype(jnp.bfloat16)
        added = jnp.einsum("rp,rk->pk", selector, high_part, preferred_element_type=jnp.float32)
        added = added + jnp.einsum(
            "rp,rk->pk", selector, low_part, preferred_element_type=jnp.float32
        )
        return (summed + added, None)

    start = jnp.zeros((block_count, orbital_count * orbital_count), jnp.float32)
    partial_value, _ = lax.scan(group_terms, start, (atom_rows, pair_groups, potential_groups))
    share_rows = block_count // lax.axis_size("height")
    summed = lax.psum(partial_value, "height")
    local_block_list = lax.dynamic_slice_in_dim(
        summed, lax.axis_index("height") * share_rows, share_rows, 0
    )
    return (potential, local_block_list.reshape(share_rows, orbital_count, orbital_count))


def solution(mesh):
    placed = (
        P("col", "height", None, None),
        P("col", "height"),
        P("col", "height", None, None),
        P(("col", "height"), None, None),
    )
    return jax.shard_map(
        per_device,
        mesh=mesh,
        in_specs=placed,
        out_specs=(P("col", "height", None), P(("col", "height"), None, None)),
        check_vma=False,
    )
```

profile of v0, /device:TPU:1, one launch (start us, length us, event | category | flops | bytes accessed | tf_op | source)
XLA Modules:
  0.0 524.8 jit_solution(14922633698963997676)
XLA Ops:
  10.2 8.2 %broadcast_multiply_fusion = bf16[6,16,4,64,128]{4,3,2,1,0:T(8,128)(2,1)} fusion(bf16[6,16,4,64,128]{4,3,2,1,0:T(8,128)(2,1)} %bitcast.135, bf16[6,16,4,64]{3,2,1,0:T(4,128)(2,1)S(1)} %compare_convert_fusion), kind=kLoop, calls=%fused_computation.29 | loop fusion | flops 3145728 | bytes 12632064 | tf_op jit(solution)/shard_map/mul | solution.py:66
  18.4 37.8 %all-gather.2.cloned.1.call-done = bf16[256,64,64]{2,1,0:T(8,128)(2,1)} async-done(((bf16[16,64,64]{2,1,0:T(8,128)(2,1)}), bf16[256,64,64]{2,1,0:T(8,128)(2,1)}) %all-gather.2.cloned.1.call-update) | async-done | bytes 2097168 | tf_op jit(solution)/shard_map/all_gather | solution.py:59
  56.2 56.0 %while.21 = (s32[]{:T(128)}, f32[6,16,128]{2,1,0:T(8,128)S(1)}, bf16[6,16,4,64,128]{4,3,2,1,0:T(8,128)(2,1)}, s32[6,16,4,4]{3,2,1,0:T(4,128)S(1)}, bf16[256,64,64]{2,1,0:T(8,128)(2,1)}, /*index=5*/s32[]{:T(128)}) while((s32[]{:T(128)}, f32[6,16,128]{2,1,0:T(8,128)S(1)}, bf16[6,16,4,64,128]{4,3,2,1,0:T(8,128)(2,1)}, ...), condition=%wide.region_2.3_spmd, body=%wide.region_0.2_spmd.sunk | while | flops 270008064 | bytes 10521677 | solution.py:78
  148.9 9.6 %all_to_all.72 = f32[16,1,768]{2,1,0:T(1,128)S(1)} all-to-all(f32[16,1,768]{2,1,0:T(1,128)S(1)} %reshape.197), channel_id=1, replica_groups=mesh['col'=16,'height'=16] {'col'}, dimensions={0} | all-to-all | bytes 98304 | tf_op jit(solution)/shard_map/all_to_all | solution.py:48
  179.6 222.5 %while.22 = (s32[]{:T(128)}, f32[256,4096]{1,0:T(8,128)}, s32[6,16,4,4]{3,2,1,0:T(4,128)S(1)}, bf16[6,16,4,64,128]{4,3,2,1,0:T(8,128)(2,1)}, f32[6,16,128]{2,1,0:T(8,128)S(1)}, /*index=5*/s32[]{:T(128)}, s32[]{:T(128)}) while((s32[]{:T(128)}, f32[256,4096]{1,0:T(8,128)}, s32[6,16,4,4]{3,2,1,0:T(4,128)S(1)}, ...), condition=%wide.region_4.5_spmd.clone, body=%wide.region_3.4_spmd.clone.sunk | while | flops 1352269824 | bytes 48266332 | solution.py:108
  185.8 9.3 %copy.80 = f32[16,4,4,64,64]{4,3,2,1,0:T(8,128)} copy(f32[16,4,4,64,64]{3,4,1,2,0:T(8,128)} %convolution_bitcast_fusion.6) | data formatting | bytes 8388608 | tf_op jit(solution)/shard_map/while/body/eval_jaxpr/naiy,nbjy->nabij/transpose | solution.py:89
  195.0 7.9 %reshape.208 = f32[256,4096]{1,0:T(8,128)} reshape(f32[16,4,4,64,64]{4,3,2,1,0:T(8,128)} %copy.80) | data formatting | bytes 8388608 | tf_op jit(solution)/shard_map/while/body/eval_jaxpr/reshape | solution.py:95
  208.0 7.8 %fusion.89 = f32[256,4096]{1,0:T(8,128)} fusion(f32[256,4096]{1,0:T(8,128)} %fusion.88, f32[256,4096]{1,0:T(8,128)} %get-tuple-element.221, f32[256,4096]{1,0:T(8,128)} %reshape.208, pred[]{:T(512)S(6)} %compare.8, s32[256]{0:T(256)S(1)} %eq.44), kind=kOutput, calls=%fused_computation.11.clone.1 | convolution fusion | flops 544276480 | bytes 16778240 | tf_op jit(solution)/shard_map/while/body/eval_jaxpr/rp,rk->pk/dot_general | solution.py:102
  221.9 9.3 %copy.80 = f32[16,4,4,64,64]{4,3,2,1,0:T(8,128)} copy(f32[16,4,4,64,64]{3,4,1,2,0:T(8,128)} %convolution_bitcast_fusion.6) | data formatting | bytes 8388608 | tf_op jit(solution)/shard_map/while/body/eval_jaxpr/naiy,nbjy->nabij/transpose | solution.py:89
  231.2 7.9 %reshape.208 = f32[256,4096]{1,0:T(8,128)} reshape(f32[16,4,4,64,64]{4,3,2,1,0:T(8,128)} %copy.80) | data formatting | bytes 8388608 | tf_op jit(solution)/shard_map/while/body/eval_jaxpr/reshape | solution.py:95
  244.1 9.0 %fusion.89 = f32[256,4096]{1,0:T(8,128)} fusion(f32[256,4096]{1,0:T(8,128)} %fusion.88, f32[256,4096]{1,0:T(8,128)} %get-tuple-element.221, f32[256,4096]{1,0:T(8,128)} %reshape.208, pred[]{:T(512)S(6)} %compare.8, s32[256]{0:T(256)S(1)} %eq.44), kind=kOutput, calls=%fused_computation.11.clone.1 | convolution fusion | flops 544276480 | bytes 16778240 | tf_op jit(solution)/shard_map/while/body/eval_jaxpr/rp,rk->pk/dot_general | solution.py:102
  259.2 9.3 %copy.80 = f32[16,4,4,64,64]{4,3,2,1,0:T(8,128)} copy(f32[16,4,4,64,64]{3,4,1,2,0:T(8,128)} %convolution_bitcast_fusion.6) | data formatting | bytes 8388608 | tf_op jit(solution)/shard_map/while/body/eval_jaxpr/naiy,nbjy->nabij/transpose | solution.py:89
  268.4 7.9 %reshape.208 = f32[256,4096]{1,0:T(8,128)} reshape(f32[16,4,4,64,64]{4,3,2,1,0:T(8,128)} %copy.80) | data formatting | bytes 8388608 | tf_op jit(solution)/shard_map/while/body/eval_jaxpr/reshape | solution.py:95
  281.4 9.0 %fusion.89 = f32[256,4096]{1,0:T(8,128)} fusion(f32[256,4096]{1,0:T(8,128)} %fusion.88, f32[256,4096]{1,0:T(8,128)} %get-tuple-element.221, f32[256,4096]{1,0:T(8,128)} %reshape.208, pred[]{:T(512)S(6)} %compare.8, s32[256]{0:T(256)S(1)} %eq.44), kind=kOutput, calls=%fused_computation.11.clone.1 | convolution fusion | flops 544276480 | bytes 16778240 | tf_op jit(solution)/shard_map/while/body/eval_jaxpr/rp,rk->pk/dot_general | solution.py:102
  296.4 9.3 %copy.80 = f32[16,4,4,64,64]{4,3,2,1,0:T(8,128)} copy(f32[16,4,4,64,64]{3,4,1,2,0:T(8,128)} %convolution_bitcast_fusion.6) | data formatting | bytes 8388608 | tf_op jit(solution)/shard_map/while/body/eval_jaxpr/naiy,nbjy->nabij/transpose | solution.py:89
  305.7 7.9 %reshape.208 = f32[256,4096]{1,0:T(8,128)} reshape(f32[16,4,4,64,64]{4,3,2,1,0:T(8,128)} %copy.80) | data formatting | bytes 8388608 | tf_op jit(solution)/shard_map/while/body/eval_jaxpr/reshape | solution.py:95
  318.7 9.0 %fusion.89 = f32[256,4096]{1,0:T(8,128)} fusion(f32[256,4096]{1,0:T(8,128)} %fusion.88, f32[256,4096]{1,0:T(8,128)} %get-tuple-element.221, f32[256,4096]{1,0:T(8,128)} %reshape.208, pred[]{:T(512)S(6)} %compare.8, s32[256]{0:T(256)S(1)} %eq.44), kind=kOutput, calls=%fused_computation.11.clone.1 | convolution fusion | flops 544276480 | bytes 16778240 | tf_op jit(solution)/shard_map/while/body/eval_jaxpr/rp,rk->pk/dot_general | solution.py:102
  333.7 9.3 %copy.80 = f32[16,4,4,64,64]{4,3,2,1,0:T(8,128)} copy(f32[16,4,4,64,64]{3,4,1,2,0:T(8,128)} %convolution_bitcast_fusion.6) | data formatting | bytes 8388608 | tf_op jit(solution)/shard_map/while/body/eval_jaxpr/naiy,nbjy->nabij/transpose | solution.py:89
  342.9 7.9 %reshape.208 = f32[256,4096]{1,0:T(8,128)} reshape(f32[16,4,4,64,64]{4,3,2,1,0:T(8,128)} %copy.80) | data formatting | bytes 8388608 | tf_op jit(solution)/shard_map/while/body/eval_jaxpr/reshape | solution.py:95
  355.9 9.0 %fusion.89 = f32[256,4096]{1,0:T(8,128)} fusion(f32[256,4096]{1,0:T(8,128)} %fusion.88, f32[256,4096]{1,0:T(8,128)} %get-tuple-element.221, f32[256,4096]{1,0:T(8,128)} %reshape.208, pred[]{:T(512)S(6)} %compare.8, s32[256]{0:T(256)S(1)} %eq.44), kind=kOutput, calls=%fused_computation.11.clone.1 | convolution fusion | flops 544276480 | bytes 16778240 | tf_op jit(solution)/shard_map/while/body/eval_jaxpr/rp,rk->pk/dot_general | solution.py:102
  370.9 9.3 %copy.80 = f32[16,4,4,64,64]{4,3,2,1,0:T(8,128)} copy(f32[16,4,4,64,64]{3,4,1,2,0:T(8,128)} %convolution_bitcast_fusion.6) | data formatting | bytes 8388608 | tf_op jit(solution)/shard_map/while/body/eval_jaxpr/naiy,nbjy->nabij/transpose | solution.py:89
  380.2 7.9 %reshape.208 = f32[256,4096]{1,0:T(8,128)} reshape(f32[16,4,4,64,64]{4,3,2,1,0:T(8,128)} %copy.80) | data formatting | bytes 8388608 | tf_op jit(solution)/shard_map/while/body/eval_jaxpr/reshape | solution.py:95
  393.2 9.0 %fusion.89 = f32[256,4096]{1,0:T(8,128)} fusion(f32[256,4096]{1,0:T(8,128)} %fusion.88, f32[256,4096]{1,0:T(8,128)} %get-tuple-element.221, f32[256,4096]{1,0:T(8,128)} %reshape.208, pred[]{:T(512)S(6)} %compare.8, s32[256]{0:T(256)S(1)} %eq.44), kind=kOutput, calls=%fused_computation.11.clone.1 | convolution fusion | flops 544276480 | bytes 16778240 | tf_op jit(solution)/shard_map/while/body/eval_jaxpr/rp,rk->pk/dot_general | solution.py:102
  402.2 113.7 %all-reduce.2.cloned.1.call-done = f32[256,4096]{1,0:T(8,128)} async-done(((f32[256,4096]{1,0:T(8,128)}), f32[256,4096]{1,0:T(8,128)}) %all-reduce.2.cloned.1.call-update) | async-done | bytes 4194320 | tf_op jit(solution)/shard_map/psum | solution.py:110
  (122 shorter events, 185.3 us)
Async XLA Ops:
  7.2 49.0 %all-gather.2.cloned.1.call-start = ((), (), s32[]{:S(2)}) async-start(), calls=%async_computation.4 | async-start | bytes 4456448 | tf_op jit(solution)/shard_map/all_gather | solution.py:59
  114.0 12.0 %all-to-all-start = ((f32[16,1,768]{2,1,0:T(1,128)}), f32[16,1,768]{2,1,0:T(1,128)S(1)}, u32[]{:S(2)}, u32[]{:S(2)}) async-start(f32[16,1,768]{2,1,0:T(1,128)} %reshape.193), calls=%async_computation | async-start | bytes 98304 | tf_op jit(solution)/shard_map/all_to_all | solution.py:33
  131.1 13.0 %all-to-all-start.1 = ((f32[16,1,768]{2,1,0:T(1,128)}), f32[16,1,768]{2,1,0:T(1,128)S(1)}, u32[]{:S(2)}, u32[]{:S(2)}) async-start(f32[16,1,768]{2,1,0:T(1,128)} %reshape.195), calls=%async_computation.1 | async-start | bytes 98304 | tf_op jit(solution)/shard_map/all_to_all | solution.py:35
  162.6 13.7 %all-to-all-start.3 = ((f32[16,1,768]{2,1,0:T(1,128)}), f32[16,1,768]{2,1,0:T(1,128)S(1)}, u32[]{:S(2)}, u32[]{:S(2)}) async-start(f32[16,1,768]{2,1,0:T(1,128)} %reshape.199), calls=%async_computation.3 | async-start | bytes 98304 | tf_op jit(solution)/shard_map/all_to_all | solution.py:50
  168.8 347.2 %all-reduce.2.cloned.1.call-start = ((), (), s32[]{:S(2)}) async-start(), calls=%async_computation.5 | async-start | bytes 8388608 | tf_op jit(solution)/shard_map/psum | solution.py:110
  402.2 115.8 %copy-start = (f32[6,16,128]{2,1,0:T(8,128)}, f32[6,16,128]{2,1,0:T(8,128)S(1)}, u32[]{:S(2)}) copy-start(f32[6,16,128]{2,1,0:T(8,128)S(1)} %get-tuple-element.246) | copy-start | bytes 147460
Sparse Core Ops, SparseCore 0:
  9.8 46.3 all-gather.1
  402.3 113.5 all-reduce.1
where the time goes:
time: 527 us; the launch traced here: 525 us
  waiting for transfers between devices  174 us (33%)
  local copies, waits for them, and re-layouts  151 us (29%)
  matrix products  146 us (28%)
  starting transfers between devices  17.4 us (3%)
  between operations  14.3 us (3%)
  other arithmetic  11.9 us (2%)
  blocking collectives  9.6 us (2%)
    psum x1, waiting for transfers between devices, per_device(): summed = lax.psum(partial_value, 'height')  114 us
    transpose x6, local copies, waits for them, and re-layouts, group_terms(): jnp.einsum('naiy,nbjy->nabij', weight_applied, orbital_row_values, prefer...  55.6 us
    dot_general x6, matrix products, group_terms(): jnp.einsum('rp,rk->pk', selector, low_part, preferred_element_type=jnp.fl...  52.6 us
    reshape x6, local copies, waits for them, and re-layouts, group_terms(): full_block.reshape(group_size * atom_count * atom_count, orbital_count *...  47.3 us
    all_gather x1, waiting for transfers between devices, per_device(): blocks = lax.all_gather(density_blocks, 'height', axis=0, tiled=True)  37.8 us
    dot_general x6, matrix products, group_terms(): jnp.einsum('naiy,nbjy->nabij', weight_applied, orbital_row_values, prefer...  36.3 us
    gather x6, local copies, waits for them, and re-layouts, group_density(): chosen = blocks[pair_row_values]  31.5 us
    dot_general x6, matrix products, group_terms(): jnp.einsum('rp,rk->pk', selector, high_part, preferred_element_type=jnp.f...  29.9 us
  transfers between devices with their start and end apart: 5, of which 5 were waited for; matrix products, arithmetic and copies ran while one was open for 2% of the time, Pallas kernels for 0%

commit v1 on v0

v1 whole, which is shorter than its diff:
```python
import math

import jax
import jax.numpy as jnp
import numpy as np
from jax import lax
from jax.experimental import pallas as pl
from jax.experimental.pallas import tpu as pltpu
from jax.sharding import PartitionSpec as P

XC_COEF = 0.7386
FOUR_PI = 12.566370614359172
KAPPA = 0.5
LANES = 128
F32 = jnp.float32
BF16 = jnp.bfloat16
HIGHEST = lax.Precision.HIGHEST
VMEM_LIMIT = 56 * 1024 * 1024


def cas_table(count):
    steps = np.arange(count)
    angle = 2.0 * np.pi * (steps[:, None] * steps[None, :] % count) / count
    return (np.cos(angle) + np.sin(angle)).astype(np.float32)


def symbol(count):
    return (2.0 - 2.0 * np.cos(2.0 * np.pi * np.arange(count) / count)).astype(np.float32)


def density_kernel(pair_ref, live_ref, base_ref, orb_ref, *refs):
    pieces, (cas_ref, dens_ref, spec_ref, table_ref) = refs[:-4], refs[-4:]
    step = pl.program_id(0)
    group = orb_ref.shape[0]
    packed_rows = table_ref.shape[0] // 2

    @pl.when(step == 0)
    def _():
        at = 0
        for piece in pieces:
            for first in range(0, piece.shape[0], 8):
                base = base_ref[at]
                at += 1
                both = piece[first : first + 8]
                table_ref[pl.ds(base, 8)] = both
                table_ref[pl.ds(packed_rows + base, 8)] = jnp.concatenate(
                    [both[:, :, 64:], both[:, :, :64]], axis=2
                )

    left_lanes = lax.broadcasted_iota(jnp.int32, (64, LANES), 1) < 64

    def place(p, side):
        row = (p >> 4) * 8 + (p & 7)
        other = (p >> 3) & 1
        return row + (other if side == 0 else 1 - other) * packed_rows

    rows_out = []
    for l in range(group):
        line = step * group + l
        live = live_ref[line]
        phi = jnp.concatenate(
            [
                jnp.where(a < live, orb_ref[l, a * 64 : (a + 1) * 64, :], jnp.zeros((), BF16))
                for a in range(4)
            ],
            axis=0,
        )
        strips = []
        for a in range(4):
            halves = []
            for b in (0, 2):
                p0 = pair_ref[line * 16 + a * 4 + b]
                p1 = pair_ref[line * 16 + a * 4 + b + 1]
                halves.append(jnp.where(left_lanes, table_ref[place(p0, 0)], table_ref[place(p1, 1)]))
            strips.append(jnp.concatenate(halves, axis=1))
        matrix = jnp.concatenate(strips, axis=0)
        product = jnp.dot(matrix, phi, preferred_element_type=F32)
        rows_out.append(jnp.sum(phi.astype(F32) * product, axis=0, keepdims=True))
    dens_ref[pl.ds(pl.multiple_of(step * group, group), group), :] = jnp.concatenate(rows_out, axis=0)

    @pl.when(step == pl.num_programs(0) - 1)
    def _():
        spectrum = jnp.dot(dens_ref[...], cas_ref[...], precision=HIGHEST, preferred_element_type=F32)
        lines = spectrum.shape[0]
        wide = jnp.concatenate([spectrum, jnp.zeros((LANES - lines, spectrum.shape[1]), F32)], axis=0)
        spec_ref[...] = wide.T


def solve_kernel(part_ref, in_ref, cx_ref, cxt_ref, cz_ref, sx_ref, sz_ref, sy_ref, out_ref, *, cells_x, cells_z, cols, heights):
    core = part_ref[0]
    plane = part_ref[1]
    lane = lax.broadcasted_iota(jnp.int32, (cols, LANES), 1)
    group_of = lane // cells_z
    slots = LANES // cells_z
    skewed = [
        pltpu.roll(in_ref[pl.ds(h, cols, stride=heights), :], cells_z * h, 1) if h else in_ref[pl.ds(h, cols, stride=heights), :]
        for h in range(heights)
    ]
    rows = []
    for x in range(cells_x):
        mixed = jnp.zeros((cols, LANES), F32)
        for g in range(slots):
            mixed = jnp.where(group_of == g, skewed[(g - x) % slots], mixed)
        rows.append(pltpu.roll(mixed, LANES - cells_z * x, 1) if x else mixed)
    field = jnp.concatenate(rows, axis=0)
    forward = cx_ref[core]
    spec = jnp.dot(forward, field, precision=HIGHEST, preferred_element_type=F32)
    spec = jnp.dot(spec, cz_ref[...], precision=HIGHEST, preferred_element_type=F32)
    scale = sx_ref[core] + sz_ref[...] + sy_ref[plane]
    spec = spec / scale
    spec = jnp.dot(spec, cz_ref[...], precision=HIGHEST, preferred_element_type=F32)
    back = jnp.dot(cxt_ref[core], spec, precision=HIGHEST, preferred_element_type=F32)
    skewed = []
    for x in range(cells_x):
        part = back[x * cols : (x + 1) * cols]
        skewed.append(pltpu.roll(part, cells_z * x, 1) if x else part)
    for h in range(heights):
        mixed = jnp.zeros((cols, LANES), F32)
        for x in range(cells_x):
            mixed = jnp.where(group_of == (h + x) % slots, skewed[x], mixed)
        mixed = pltpu.roll(mixed, LANES - cells_z * h, 1) if h else mixed
        out_ref[pl.ds(h, cols, stride=heights), :] = mixed


def hamiltonian_kernel(
    pair_ref, live_ref, base_ref, orb_ref, dens_ref, back_ref, cas_ref, pot_ref, keep_ref, first_ref, rest_ref, acc_ref
):
    step = pl.program_id(0)
    group = orb_ref.shape[0]
    lines = dens_ref.shape[0]

    @pl.when(step == 0)
    def _():
        hartree = lax.dot_general(
            back_ref[...].T, cas_ref[...], (((1,), (0,)), ((), ())), precision=HIGHEST, preferred_element_type=F32
        )
        dens = dens_ref[...]
        pot_ref[...] = hartree[:lines] - XC_COEF * jnp.exp(jnp.log(dens * dens + 1.0) * (1.0 / 6.0))

        def clear(i, carry):
            acc_ref[pl.ds(i * 8, 8)] = jnp.zeros((8, 64, LANES), F32)
            return carry

        lax.fori_loop(0, acc_ref.shape[0] // 8, clear, 0)

    potential = pot_ref[pl.ds(pl.multiple_of(step * group, group), group), :]
    for l in range(group):
        line = step * group + l
        live = live_ref[line]
        phi = jnp.concatenate(
            [
                jnp.where(a < live, orb_ref[l, a * 64 : (a + 1) * 64, :], jnp.zeros((), BF16))
                for a in range(4)
            ],
            axis=0,
        )
        weighted = (phi.astype(F32) * potential[l : l + 1, :]).astype(BF16)
        full = lax.dot_general(weighted, phi, (((1,), (1,)), ((), ())), preferred_element_type=F32)
        for a in range(4):
            for b in (0, 2):
                p0 = pair_ref[line * 16 + a * 4 + b]
                p1 = pair_ref[line * 16 + a * 4 + b + 1]
                both = full[a * 64 : (a + 1) * 64, b * 64 : b * 64 + LANES]
                acc_ref[p0] += both
                acc_ref[p1] += pltpu.roll(both, 64, 1)

    @pl.when(step == pl.num_programs(0) - 1)
    def _():
        left_lanes = lax.broadcasted_iota(jnp.int32, (8, 64, LANES), 2) < 64
        at = 0
        for out in (keep_ref, first_ref, rest_ref):
            for first in range(0, out.shape[0], 8):
                base = base_ref[at]
                at += 1
                low = acc_ref[pl.ds(base, 8)]
                high = acc_ref[pl.ds(base + 8, 8)]
                out[first : first + 8] = jnp.where(left_lanes, low, pltpu.roll(high, 64, 2)).astype(out.dtype)


def per_device(orbitals, live_atoms, pair_index, density_blocks):
    cells_x, cells_z, width, line_cells = orbitals.shape
    cols = lax.axis_size("col")
    heights = lax.axis_size("height")
    full_x = cells_x * cols
    full_z = cells_z * heights
    lines = cells_x * cells_z
    share = density_blocks.shape[0]
    devices = cols * heights
    copies = devices // line_cells
    group = 8
    block_rows = share * heights // 2

    cas_y = cas_table(line_cells)
    cas_y2 = np.repeat(cas_y, copies, axis=1)
    cas_x = cas_table(full_x)
    order = np.arange(full_x).reshape(cols, cells_x).T.reshape(-1)
    half_x = full_x // copies
    forward_x = cas_x.reshape(copies, half_x, full_x)[:, :, order]
    back_x = forward_x.transpose(0, 2, 1).copy()
    cas_z = cas_table(full_z)
    norm = 1.0 / (full_x * full_z * line_cells)
    unit = FOUR_PI * norm
    sym_x = np.broadcast_to(symbol(full_x).reshape(copies, half_x, 1) / unit, (copies, half_x, LANES)).astype(np.float32)
    sym_z = ((symbol(full_z) + KAPPA * KAPPA) / unit).reshape(1, full_z).astype(np.float32)
    sym_y = (symbol(line_cells) / unit).astype(np.float32)

    orb = orbitals.reshape(lines, width, line_cells)
    live = live_atoms.reshape(lines)
    pairs = pair_index.reshape(lines * 16)
    packed = jnp.concatenate([density_blocks[: share // 2], density_blocks[share // 2 :]], axis=2)
    chips = heights // 2
    far = chips // 2
    height = lax.axis_index("height")
    chip, core = height // 2, height % 2
    turn = 1 - 2 * core
    twin = [(h, h ^ 1) for h in range(heights)]
    ring = [(h, (h + 2 - 4 * (h % 2)) % heights) for h in range(heights)]

    def across(values):
        return lax.ppermute(values, "height", twin)

    def onward(values):
        return lax.ppermute(values, "height", ring)

    def place_of(distance, owner):
        return ((chip + distance) % chips) * 2 + owner

    moving = jnp.concatenate([packed, across(packed)], axis=0)
    pieces = [moving]
    heights_of = [place_of(0, core), place_of(0, 1 - core)]
    for d in range(1, far + 1):
        moving = onward(moving if d < far else moving[: share // 2])
        pieces += [moving, across(moving)]
        if d < far:
            heights_of += [place_of(-turn * d, core), place_of(-turn * d, 1 - core)]
            heights_of += [place_of(turn * d, 1 - core), place_of(turn * d, core)]
        else:
            heights_of += [place_of(d, core), place_of(d, 1 - core)]
    table_rows = (jnp.stack(heights_of) * (share // 2)).astype(jnp.int32)
    keep_of, give_of = [], []
    for d in range(far, -1, -1):
        keep_of.append(place_of(turn * d, core))
        give_of.append(place_of(-turn * d, 1 - core))
        if 0 < d < far:
            keep_of.append(place_of(turn * d, 1 - core))
            give_of.append(place_of(-turn * d, core))
    sum_rows = (jnp.stack(keep_of + give_of) * share).astype(jnp.int32)

    def whole(*shape):
        return pl.BlockSpec(shape, lambda i, *_: (0,) * len(shape))

    params = pltpu.CompilerParams(dimension_semantics=("arbitrary",), vmem_limit_bytes=VMEM_LIMIT)
    density, spectrum = pl.pallas_call(
        density_kernel,
        grid_spec=pltpu.PrefetchScalarGridSpec(
            num_scalar_prefetch=3,
            grid=(lines // group,),
            in_specs=[
                pl.BlockSpec((group, width, line_cells), lambda i, *_: (i, 0, 0)),
                *[whole(*piece.shape) for piece in pieces],
                whole(line_cells, devices),
            ],
            out_specs=[whole(lines, line_cells), whole(devices, LANES)],
            scratch_shapes=[pltpu.VMEM((2 * block_rows, 64, LANES), BF16)],
        ),
        out_shape=[
            jax.ShapeDtypeStruct((lines, line_cells), F32),
            jax.ShapeDtypeStruct((devices, LANES), F32),
        ],
        compiler_params=params,
        name="density",
    )(pairs, live, table_rows, orb, *pieces, jnp.asarray(cas_y2))

    def exchange(values):
        out = lax.all_to_all(values.reshape(devices, 1, LANES), ("col", "height"), split_axis=0, concat_axis=0, tiled=True)
        return out.reshape(devices, LANES)

    device = lax.axis_index("col") * heights + height
    part = jnp.stack([device % copies, device // copies]).astype(jnp.int32)
    smem = pl.BlockSpec(memory_space=pltpu.SMEM)
    vmem = pl.BlockSpec(memory_space=pltpu.VMEM)
    solved = pl.pallas_call(
        lambda *refs: solve_kernel(*refs, cells_x=cells_x, cells_z=cells_z, cols=cols, heights=heights),
        in_specs=[smem, vmem, vmem, vmem, vmem, vmem, vmem, smem],
        out_specs=vmem,
        out_shape=jax.ShapeDtypeStruct((devices, LANES), F32),
        compiler_params=pltpu.CompilerParams(vmem_limit_bytes=VMEM_LIMIT),
        name="solve",
    )(
        part,
        exchange(spectrum),
        jnp.asarray(forward_x),
        jnp.asarray(back_x),
        jnp.asarray(cas_z),
        jnp.asarray(sym_x),
        jnp.asarray(sym_z),
        jnp.asarray(sym_y),
    )
    returned = exchange(solved)

    half_rows = block_rows // 2
    potential, keep, give_first, give_rest = pl.pallas_call(
        hamiltonian_kernel,
        grid_spec=pltpu.PrefetchScalarGridSpec(
            num_scalar_prefetch=3,
            grid=(lines // group,),
            in_specs=[
                pl.BlockSpec((group, width, line_cells), lambda i, *_: (i, 0, 0)),
                whole(lines, line_cells),
                whole(devices, LANES),
                whole(devices, line_cells),
            ],
            out_specs=[
                whole(lines, line_cells),
                whole(half_rows, 64, LANES),
                whole(share // 2, 64, LANES),
                whole(half_rows - share // 2, 64, LANES),
            ],
            scratch_shapes=[pltpu.VMEM((2 * block_rows, 64, LANES), F32)],
        ),
        out_shape=[
            jax.ShapeDtypeStruct((lines, line_cells), F32),
            jax.ShapeDtypeStruct((half_rows, 64, LANES), F32),
            jax.ShapeDtypeStruct((share // 2, 64, LANES), BF16),
            jax.ShapeDtypeStruct((half_rows - share // 2, 64, LANES), BF16),
        ],
        compiler_params=params,
        name="hamiltonian",
    )(pairs, live, sum_rows, orb, density, returned, jnp.asarray(cas_y2.T.copy()))

    half = share // 2
    got_first = across(give_first)
    got_rest = across(give_rest)
    moving = onward((keep[:half] + got_first.astype(F32)).astype(BF16)).astype(F32)
    for i, d in enumerate(range(far - 1, 0, -1)):
        at = half + share * i
        terms = keep[at : at + share] + got_rest[at - half : at - half + share].astype(F32)
        if i == 0:
            moving = jnp.concatenate([moving, jnp.zeros_like(moving)], axis=0)
        moving = onward((terms + moving).astype(BF16)).astype(F32)
    other = across(moving[half:].astype(BF16)).astype(F32)
    summed = keep[half_rows - half :] + got_rest[-half:].astype(F32) + moving[:half] + other
    hamiltonian = jnp.concatenate([summed[:, :, :64], summed[:, :, 64:]], axis=0)
    return potential.reshape(cells_x, cells_z, line_cells), hamiltonian


def solution(mesh):
    placed = (
        P("col", "height", None, None),
        P("col", "height"),
        P("col", "height", None, None),
        P(("col", "height"), None, None),
    )
    return jax.shard_map(
        per_device,
        mesh=mesh,
        in_specs=placed,
        out_specs=(P("col", "height", None), P(("col", "height"), None, None)),
        check_vma=False,
    )
```

time: 527 us -> 161 us (0.31)
  matrix products: 146 us -> 0 us
  local copies, waits for them, and re-layouts: 151 us -> 5.23 us
  waiting for transfers between devices: 174 us -> 53.8 us
  starting transfers between devices: 17.4 us -> 55.7 us
  Pallas kernels: 0 us -> 36.1 us
  between operations: 14.3 us -> 0.9 us
  blocking collectives: 9.6 us -> 0 us
    dot_general x28 -> x0, matrix products: 144 us -> none  [the longest x6 52.6 us: group_terms(): jnp.einsum('rp,rk->pk', selector, low_part, preferred_element_type=jnp.fl...]
    psum x1 -> x0, waiting for transfers between devices: 114 us -> none  [per_device(): summed = lax.psum(partial_value, 'height')]
    transpose x8 -> x0, local copies, waits for them, and re-layouts: 56.1 us -> none  [the longest x6 55.6 us: group_terms(): jnp.einsum('naiy,nbjy->nabij', weight_applied, orbital_row_values, prefer...]
    reshape x7 -> x2, local copies, waits for them, and re-layouts: 48.3 us -> 1.41 us  [the longest x1 0.81 us: per_device(): pairs = pair_index.reshape(lines * 16)]
    ppermute x0 -> x16, starting transfers between devices: none -> 37.9 us  [the longest x8 20.4 us: onward(): return lax.ppermute(values, 'height', ring)]
    all_gather x1 -> x0, waiting for transfers between devices: 37.8 us -> none  [per_device(): blocks = lax.all_gather(density_blocks, 'height', axis=0, tiled=True)]
    pallas_call x0 -> x3, Pallas kernels: none -> 36.1 us  [the longest x1 18.8 us: per_device(): pl.pallas_call(hamiltonian_kernel, grid_spec=pltpu.PrefetchScalarGridSpec...]
    gather x6 -> x0, local copies, waits for them, and re-layouts: 31.5 us -> none  [group_density(): chosen = blocks[pair_row_values]]
  transfers between devices with their start and end apart: 5 -> 18, of which waited for: 5 -> 13; matrix products, arithmetic and copies ran while one was open for 2% -> 3% of each run, Pallas kernels for 0% -> 0%
where the time goes in v1:
time: 161 us; the launch traced here: 160 us
  starting transfers between devices  55.7 us (35%)
  waiting for transfers between devices  53.8 us (33%)
  Pallas kernels  36.1 us (22%)
  other arithmetic  8.12 us (5%)
  local copies, waits for them, and re-layouts  5.23 us (3%)
    all_to_all x2, waiting for transfers between devices, exchange(): lax.all_to_all(values.reshape(devices, 1, LANES), ('col', 'height'), spli...  24.5 us
    ppermute x8, waiting for transfers between devices, onward(): return lax.ppermute(values, 'height', ring)  24.4 us
    ppermute x8, starting transfers between devices, onward(): return lax.ppermute(values, 'height', ring)  20.4 us
    pallas_call x1, Pallas kernels, per_device(): pl.pallas_call(hamiltonian_kernel, grid_spec=pltpu.PrefetchScalarGridSpec...  18.8 us
    all_to_all x2, starting transfers between devices, exchange(): lax.all_to_all(values.reshape(devices, 1, LANES), ('col', 'height'), spli...  17.8 us
    ppermute x8, starting transfers between devices, across(): return lax.ppermute(values, 'height', twin)  17.5 us
    pallas_call x1, Pallas kernels, per_device(): pl.pallas_call(density_kernel, grid_spec=pltpu.PrefetchScalarGridSpec(num...  14.2 us
    ppermute x8, waiting for transfers between devices, across(): return lax.ppermute(values, 'height', twin)  4.93 us
  transfers between devices with their start and end apart: 18, of which 13 were waited for; matrix products, arithmetic and copies ran while one was open for 3% of the time, Pallas kernels for 0%

profile of v1, /device:TPU:1, one launch (start us, length us, event | category | flops | bytes accessed | tf_op | source)
XLA Modules:
  0.0 159.9 jit_solution(10377583877704481763)
XLA Ops:
  1.8 3.3 %collective-permute-start = (bf16[8,64,128]{2,1,0:T(8,128)(2,1)S(1)}, bf16[8,64,128]{2,1,0:T(8,128)(2,1)S(1)}, u32[]{:S(2)}, u32[]{:S(2)}) collective-permute-start(bf16[8,64,128]{2,1,0:T(8,128)(2,1)S(1)} %pad_maximum_fusion.2), channel_id=1, source_target_pairs={{0,1},{1,0},{2,3},{3,2},{4,5},{5,4},{6,7},{7,6},{8,9},{9,8},{10,11... | collective-permute-start | bytes 393224 | tf_op jit(solution)/shard_map/ppermute | solution.py:220
  6.2 3.9 %collective-permute-start.1 = (bf16[16,64,128]{2,1,0:T(8,128)(2,1)S(1)}, bf16[16,64,128]{2,1,0:T(8,128)(2,1)S(1)}, u32[]{:S(2)}, u32[]{:S(2)}) collective-permute-start(bf16[16,64,128]{2,1,0:T(8,128)(2,1)S(1)} %pad_maximum_fusion.1.refs_0_), channel_id=1, source_target_pairs={{0,2},{1,15},{2,4},{3,1},{4,6},{5,3},{6,8},{7,5},{8,10},{9,7},{10,... | collective-permute-start | bytes 786440 | tf_op jit(solution)/shard_map/ppermute | solution.py:223
  10.1 3.3 %collective-permute-done.1.refs_1_ = bf16[16,64,128]{2,1,0:T(8,128)(2,1)S(1)} collective-permute-done((bf16[16,64,128]{2,1,0:T(8,128)(2,1)S(1)}, bf16[16,64,128]{2,1,0:T(8,128)(2,1)S(1)}, u32[]{:S(2)}, u32[]{:S(2)}) %collective-permute-start.1) | collective-permute-done | bytes 262176 | tf_op jit(solution)/shard_map/ppermute | solution.py:223
  13.5 3.1 %collective-permute-start.3 = (bf16[16,64,128]{2,1,0:T(8,128)(2,1)S(1)}, bf16[16,64,128]{2,1,0:T(8,128)(2,1)S(1)}, u32[]{:S(2)}, u32[]{:S(2)}) collective-permute-start(bf16[16,64,128]{2,1,0:T(8,128)(2,1)S(1)} %collective-permute-done.1.refs_1_), channel_id=1, source_target_pairs={{0,2},{1,15},{2,4},{3,1},{4,6},{5,3},{6,8},{7,5},{8,10},{9,7},{10,... | collective-permute-start | bytes 786440 | tf_op jit(solution)/shard_map/ppermute | solution.py:223
  16.6 3.3 %collective-permute-done.3.refs_3_ = bf16[16,64,128]{2,1,0:T(8,128)(2,1)S(1)} collective-permute-done((bf16[16,64,128]{2,1,0:T(8,128)(2,1)S(1)}, bf16[16,64,128]{2,1,0:T(8,128)(2,1)S(1)}, u32[]{:S(2)}, u32[]{:S(2)}) %collective-permute-start.3) | collective-permute-done | bytes 262176 | tf_op jit(solution)/shard_map/ppermute | solution.py:223
  19.9 3.1 %collective-permute-start.5 = (bf16[16,64,128]{2,1,0:T(8,128)(2,1)S(1)}, bf16[16,64,128]{2,1,0:T(8,128)(2,1)S(1)}, u32[]{:S(2)}, u32[]{:S(2)}) collective-permute-start(bf16[16,64,128]{2,1,0:T(8,128)(2,1)S(1)} %collective-permute-done.3.refs_3_), channel_id=1, source_target_pairs={{0,2},{1,15},{2,4},{3,1},{4,6},{5,3},{6,8},{7,5},{8,10},{9,7},{10,... | collective-permute-start | bytes 786440 | tf_op jit(solution)/shard_map/ppermute | solution.py:223
  23.0 3.3 %collective-permute-done.5.refs_5_ = bf16[16,64,128]{2,1,0:T(8,128)(2,1)S(1)} collective-permute-done((bf16[16,64,128]{2,1,0:T(8,128)(2,1)S(1)}, bf16[16,64,128]{2,1,0:T(8,128)(2,1)S(1)}, u32[]{:S(2)}, u32[]{:S(2)}) %collective-permute-start.5) | collective-permute-done | bytes 262176 | tf_op jit(solution)/shard_map/ppermute | solution.py:223
  26.3 3.2 %collective-permute-start.7 = (bf16[8,64,128]{2,1,0:T(8,128)(2,1)S(1)}, bf16[8,64,128]{2,1,0:T(8,128)(2,1)S(1)}, u32[]{:S(2)}, u32[]{:S(2)}) collective-permute-start(bf16[8,64,128]{2,1,0:T(8,128)(2,1)S(1)} %slice.69), channel_id=1, source_target_pairs={{0,2},{1,15},{2,4},{3,1},{4,6},{5,3},{6,8},{7,5},{8,10},{9,7},{10,... | collective-permute-start | bytes 393224 | tf_op jit(solution)/shard_map/ppermute | solution.py:223
  33.0 3.6 %collective-permute-start.8 = (bf16[8,64,128]{2,1,0:T(8,128)(2,1)S(1)}, bf16[8,64,128]{2,1,0:T(8,128)(2,1)S(1)}, u32[]{:S(2)}, u32[]{:S(2)}) collective-permute-start(bf16[8,64,128]{2,1,0:T(8,128)(2,1)S(1)} %collective-permute-done.7.refs_7_), channel_id=1, source_target_pairs={{0,1},{1,0},{2,3},{3,2},{4,5},{5,4},{6,7},{7,6},{8,9},{9,8},{10,11... | collective-permute-start | bytes 393224 | tf_op jit(solution)/shard_map/ppermute | solution.py:220
  38.3 14.2 %density.1 = (f32[96,128]{1,0:T(8,128)}, f32[256,128]{1,0:T(8,128)}) custom-call(s32[1536]{0:T(1024)} %reshape.28.pair_ref, s32[96]{0:T(128)} %reshape.29.live_ref, s32[16]{0:T(128)} %broadcast_multiply_fusion.base_ref, bf16[96,256,128]{2,1,0:T(8,128)(2,1)} %bitcast.30, bf16[16,64,128]{2,1,0:T(8,128)(2,1)} %copy-done, bf16[16,64,128]{2,1,0:T(8,128)(2,1)} %copy-done.4, ...), custom_call_target="tpu_custom_call" | custom-call | tf_op jit(solution)/shard_map/density/pallas_call | solution.py:253
  52.5 11.9 %all-to-all-start = ((f32[256,1,128]{2,1,0:T(1,128)}), f32[256,1,128]{2,1,0:T(1,128)S(1)}, u32[]{:S(2)}, u32[]{:S(2)}) async-start(f32[256,1,128]{2,1,0:T(1,128)} %bitcast.35), calls=%async_computation | async-start | bytes 262144 | tf_op jit(solution)/shard_map/all_to_all | solution.py:275
  65.0 12.3 %all-to-all-done = f32[256,1,128]{2,1,0:T(1,128)S(1)} async-done(((f32[256,1,128]{2,1,0:T(1,128)}), f32[256,1,128]{2,1,0:T(1,128)S(1)}, u32[]{:S(2)}, u32[]{:S(2)}) %all-to-all-start) | async-done | bytes 131104 | tf_op jit(solution)/shard_map/all_to_all | solution.py:275
  77.9 3.1 %solve.1 = f32[256,128]{1,0:T(8,128)} custom-call(s32[2]{0:T(128)} %pad_add_fusion.refs_0_, f32[256,128]{1,0:T(8,128)} %bitcast.34, f32[2,96,192]{2,1,0:T(8,128)} %constant.161.clone.refs_2_, f32[2,192,96]{2,1,0:T(8,128)} %constant.162.clone.refs_3_, f32[128,128]{1,0:T(8,128)} %constant.163.clone.refs_4_, f32[2,96,128]{2,1,0:T(8,128)} %constant.164.clone.refs_5_, ...), custom_call_target="tpu_custom_call" | custom-call | tf_op jit(solution)/shard_map/solve/pallas_call | solution.py:282
  81.0 5.9 %all-to-all-start.1 = ((f32[256,1,128]{2,1,0:T(1,128)}), f32[256,1,128]{2,1,0:T(1,128)S(1)}, u32[]{:S(2)}, u32[]{:S(2)}) async-start(f32[256,1,128]{2,1,0:T(1,128)} %bitcast.33), calls=%async_computation.1 | async-start | bytes 262144 | tf_op jit(solution)/shard_map/all_to_all | solution.py:275
  87.7 12.3 %all-to-all-done.1 = f32[256,1,128]{2,1,0:T(1,128)S(1)} async-done(((f32[256,1,128]{2,1,0:T(1,128)}), f32[256,1,128]{2,1,0:T(1,128)S(1)}, u32[]{:S(2)}, u32[]{:S(2)}) %all-to-all-start.1) | async-done | bytes 131104 | tf_op jit(solution)/shard_map/all_to_all | solution.py:275
  100.7 18.8 %hamiltonian.1 = (f32[96,128]{1,0:T(8,128)}, f32[64,64,128]{2,1,0:T(8,128)}, bf16[8,64,128]{2,1,0:T(8,128)(2,1)}, bf16[56,64,128]{2,1,0:T(8,128)(2,1)}) custom-call(s32[1536]{0:T(1024)} %reshape.28.pair_ref, s32[96]{0:T(128)} %reshape.29.live_ref, s32[16]{0:T(128)} %broadcast_multiply_fusion.1.base_ref, bf16[96,256,128]{2,1,0:T(8,128)(2,1)} %bitcast.31, ...), custom_call_target="tpu_custom_call" | custom-call | tf_op jit(solution)/shard_map/hamiltonian/pallas_call | solution.py:302
  120.3 2.5 %collective-permute-done.10 = bf16[8,64,128]{2,1,0:T(8,128)(2,1)S(1)} collective-permute-done((bf16[8,64,128]{2,1,0:T(8,128)(2,1)}, bf16[8,64,128]{2,1,0:T(8,128)(2,1)S(1)}, u32[]{:S(2)}, u32[]{:S(2)}) %collective-permute-start.10) | collective-permute-done | bytes 131104 | tf_op jit(solution)/shard_map/ppermute | solution.py:220
  123.9 3.8 %collective-permute-done.11 = bf16[8,64,128]{2,1,0:T(8,128)(2,1)S(1)} collective-permute-done((bf16[8,64,128]{2,1,0:T(8,128)(2,1)S(1)}, bf16[8,64,128]{2,1,0:T(8,128)(2,1)S(1)}, u32[]{:S(2)}, u32[]{:S(2)}) %collective-permute-start.11) | collective-permute-done | bytes 131104 | tf_op jit(solution)/shard_map/ppermute | solution.py:223
  130.1 4.0 %collective-permute-done.12 = bf16[16,64,128]{2,1,0:T(8,128)(2,1)S(1)} collective-permute-done((bf16[16,64,128]{2,1,0:T(8,128)(2,1)S(1)}, bf16[16,64,128]{2,1,0:T(8,128)(2,1)S(1)}, u32[]{:S(2)}, u32[]{:S(2)}) %collective-permute-start.12) | collective-permute-done | bytes 262176 | tf_op jit(solution)/shard_map/ppermute | solution.py:223
  135.2 2.5 %collective-permute-start.13 = (bf16[16,64,128]{2,1,0:T(8,128)(2,1)S(1)}, bf16[16,64,128]{2,1,0:T(8,128)(2,1)S(1)}, u32[]{:S(2)}, u32[]{:S(2)}) collective-permute-start(bf16[16,64,128]{2,1,0:T(8,128)(2,1)S(1)} %add_convert_fusion.1), channel_id=1, source_target_pairs={{0,2},{1,15},{2,4},{3,1},{4,6},{5,3},{6,8},{7,5},{8,10},{9,7},{10,... | collective-permute-start | bytes 786440 | tf_op jit(solution)/shard_map/ppermute | solution.py:223
  137.8 3.3 %collective-permute-done.13 = bf16[16,64,128]{2,1,0:T(8,128)(2,1)S(1)} collective-permute-done((bf16[16,64,128]{2,1,0:T(8,128)(2,1)S(1)}, bf16[16,64,128]{2,1,0:T(8,128)(2,1)S(1)}, u32[]{:S(2)}, u32[]{:S(2)}) %collective-permute-start.13) | collective-permute-done | bytes 262176 | tf_op jit(solution)/shard_map/ppermute | solution.py:223
  142.2 3.2 %collective-permute-start.14 = (bf16[16,64,128]{2,1,0:T(8,128)(2,1)S(1)}, bf16[16,64,128]{2,1,0:T(8,128)(2,1)S(1)}, u32[]{:S(2)}, u32[]{:S(2)}) collective-permute-start(bf16[16,64,128]{2,1,0:T(8,128)(2,1)S(1)} %add_convert_fusion), channel_id=1, source_target_pairs={{0,2},{1,15},{2,4},{3,1},{4,6},{5,3},{6,8},{7,5},{8,10},{9,7},{10,... | collective-permute-start | bytes 786440 | tf_op jit(solution)/shard_map/ppermute | solution.py:223
  145.4 3.3 %collective-permute-done.14 = bf16[16,64,128]{2,1,0:T(8,128)(2,1)S(1)} collective-permute-done((bf16[16,64,128]{2,1,0:T(8,128)(2,1)S(1)}, bf16[16,64,128]{2,1,0:T(8,128)(2,1)S(1)}, u32[]{:S(2)}, u32[]{:S(2)}) %collective-permute-start.14) | collective-permute-done | bytes 262176 | tf_op jit(solution)/shard_map/ppermute | solution.py:223
  148.7 8.2 %collective-permute-start.15 = (bf16[8,64,128]{2,1,0:T(8,128)(2,1)S(1)}, bf16[8,64,128]{2,1,0:T(8,128)(2,1)S(1)}, u32[]{:S(2)}, u32[]{:S(2)}) collective-permute-start(bf16[8,64,128]{2,1,0:T(8,128)(2,1)S(1)} %slice.75), channel_id=1, source_target_pairs={{0,1},{1,0},{2,3},{3,2},{4,5},{5,4},{6,7},{7,6},{8,9},{9,8},{10,11... | collective-permute-start | bytes 393224 | tf_op jit(solution)/shard_map/ppermute | solution.py:220
  (62 shorter events, 19.5 us)
Async XLA Ops:
  0.6 30.4 %copy-start.12 = (s32[12,8]{0,1:T(8,128)S(1)}, s32[12,8]{0,1:T(8,128)}, u32[]{:S(2)}) copy-start(s32[12,8]{0,1:T(8,128)} %param.13) | copy-start | bytes 1156
  0.6 31.1 %copy-start.11 = (s32[12,8,4,4]{0,3,2,1:T(4,128)S(1)}, s32[12,8,4,4]{0,3,2,1:T(4,128)}, u32[]{:S(2)}) copy-start(s32[12,8,4,4]{0,3,2,1:T(4,128)} %param.14) | copy-start | bytes 18436
  1.8 4.3 %collective-permute-start = (bf16[8,64,128]{2,1,0:T(8,128)(2,1)S(1)}, bf16[8,64,128]{2,1,0:T(8,128)(2,1)S(1)}, u32[]{:S(2)}, u32[]{:S(2)}) collective-permute-start(bf16[8,64,128]{2,1,0:T(8,128)(2,1)S(1)} %pad_maximum_fusion.2), channel_id=1, source_target_pairs={{0,1},{1,0},{2,3},{3,2},{4,5},{5,4},{6,7},{7,6},{8,9},{9,8},{10,11... | collective-permute-start | bytes 393224 | tf_op jit(solution)/shard_map/ppermute | solution.py:220
  6.2 31.4 %copy-start = (bf16[16,64,128]{2,1,0:T(8,128)(2,1)}, bf16[16,64,128]{2,1,0:T(8,128)(2,1)S(1)}, u32[]{:S(2)}) copy-start(bf16[16,64,128]{2,1,0:T(8,128)(2,1)S(1)} %pad_maximum_fusion.1.refs_0_) | copy-start | bytes 786436
  6.2 7.2 %collective-permute-start.1 = (bf16[16,64,128]{2,1,0:T(8,128)(2,1)S(1)}, bf16[16,64,128]{2,1,0:T(8,128)(2,1)S(1)}, u32[]{:S(2)}, u32[]{:S(2)}) collective-permute-start(bf16[16,64,128]{2,1,0:T(8,128)(2,1)S(1)} %pad_maximum_fusion.1.refs_0_), channel_id=1, source_target_pairs={{0,2},{1,15},{2,4},{3,1},{4,6},{5,3},{6,8},{7,5},{8,10},{9,7},{10,... | collective-permute-start | bytes 786440 | tf_op jit(solution)/shard_map/ppermute | solution.py:223
  13.5 24.1 %copy-start.4 = (bf16[16,64,128]{2,1,0:T(8,128)(2,1)}, bf16[16,64,128]{2,1,0:T(8,128)(2,1)S(1)}, u32[]{:S(2)}) copy-start(bf16[16,64,128]{2,1,0:T(8,128)(2,1)S(1)} %collective-permute-done.1.refs_1_) | copy-start | bytes 786436
  13.5 6.4 %collective-permute-start.3 = (bf16[16,64,128]{2,1,0:T(8,128)(2,1)S(1)}, bf16[16,64,128]{2,1,0:T(8,128)(2,1)S(1)}, u32[]{:S(2)}, u32[]{:S(2)}) collective-permute-start(bf16[16,64,128]{2,1,0:T(8,128)(2,1)S(1)} %collective-permute-done.1.refs_1_), channel_id=1, source_target_pairs={{0,2},{1,15},{2,4},{3,1},{4,6},{5,3},{6,8},{7,5},{8,10},{9,7},{10,... | collective-permute-start | bytes 786440 | tf_op jit(solution)/shard_map/ppermute | solution.py:223
  19.9 17.7 %copy-start.5 = (bf16[16,64,128]{2,1,0:T(8,128)(2,1)}, bf16[16,64,128]{2,1,0:T(8,128)(2,1)S(1)}, u32[]{:S(2)}) copy-start(bf16[16,64,128]{2,1,0:T(8,128)(2,1)S(1)} %collective-permute-done.3.refs_3_) | copy-start | bytes 786436
  19.9 6.4 %collective-permute-start.5 = (bf16[16,64,128]{2,1,0:T(8,128)(2,1)S(1)}, bf16[16,64,128]{2,1,0:T(8,128)(2,1)S(1)}, u32[]{:S(2)}, u32[]{:S(2)}) collective-permute-start(bf16[16,64,128]{2,1,0:T(8,128)(2,1)S(1)} %collective-permute-done.3.refs_3_), channel_id=1, source_target_pairs={{0,2},{1,15},{2,4},{3,1},{4,6},{5,3},{6,8},{7,5},{8,10},{9,7},{10,... | collective-permute-start | bytes 786440 | tf_op jit(solution)/shard_map/ppermute | solution.py:223
  26.3 11.3 %copy-start.1 = (bf16[16,64,128]{2,1,0:T(8,128)(2,1)}, bf16[16,64,128]{2,1,0:T(8,128)(2,1)S(1)}, u32[]{:S(2)}) copy-start(bf16[16,64,128]{2,1,0:T(8,128)(2,1)S(1)} %collective-permute-done.5.refs_5_) | copy-start | bytes 786436
  26.3 6.6 %collective-permute-start.7 = (bf16[8,64,128]{2,1,0:T(8,128)(2,1)S(1)}, bf16[8,64,128]{2,1,0:T(8,128)(2,1)S(1)}, u32[]{:S(2)}, u32[]{:S(2)}) collective-permute-start(bf16[8,64,128]{2,1,0:T(8,128)(2,1)S(1)} %slice.69), channel_id=1, source_target_pairs={{0,2},{1,15},{2,4},{3,1},{4,6},{5,3},{6,8},{7,5},{8,10},{9,7},{10,... | collective-permute-start | bytes 393224 | tf_op jit(solution)/shard_map/ppermute | solution.py:223
  29.5 7.6 %collective-permute-start.2 = (bf16[16,64,128]{2,1,0:T(8,128)(2,1)S(1)}, bf16[16,64,128]{2,1,0:T(8,128)(2,1)S(1)}, u32[]{:S(2)}, u32[]{:S(2)}) collective-permute-start(bf16[16,64,128]{2,1,0:T(8,128)(2,1)S(1)} %collective-permute-done.1.refs_1_), channel_id=1, source_target_pairs={{0,1},{1,0},{2,3},{3,2},{4,5},{5,4},{6,7},{7,6},{8,9},{9,8},{10,11... | collective-permute-start | bytes 786440 | tf_op jit(solution)/shard_map/ppermute | solution.py:220
  30.5 6.6 %collective-permute-start.4 = (bf16[16,64,128]{2,1,0:T(8,128)(2,1)S(1)}, bf16[16,64,128]{2,1,0:T(8,128)(2,1)S(1)}, u32[]{:S(2)}, u32[]{:S(2)}) collective-permute-start(bf16[16,64,128]{2,1,0:T(8,128)(2,1)S(1)} %collective-permute-done.3.refs_3_), channel_id=1, source_target_pairs={{0,1},{1,0},{2,3},{3,2},{4,5},{5,4},{6,7},{7,6},{8,9},{9,8},{10,11... | collective-permute-start | bytes 786440 | tf_op jit(solution)/shard_map/ppermute | solution.py:220
  30.6 7.0 %collective-permute-start.6 = (bf16[16,64,128]{2,1,0:T(8,128)(2,1)S(1)}, bf16[16,64,128]{2,1,0:T(8,128)(2,1)S(1)}, u32[]{:S(2)}, u32[]{:S(2)}) collective-permute-start(bf16[16,64,128]{2,1,0:T(8,128)(2,1)S(1)} %collective-permute-done.5.refs_5_), channel_id=1, source_target_pairs={{0,1},{1,0},{2,3},{3,2},{4,5},{5,4},{6,7},{7,6},{8,9},{9,8},{10,11... | collective-permute-start | bytes 786440 | tf_op jit(solution)/shard_map/ppermute | solution.py:220
  33.0 4.6 %collective-permute-start.8 = (bf16[8,64,128]{2,1,0:T(8,128)(2,1)S(1)}, bf16[8,64,128]{2,1,0:T(8,128)(2,1)S(1)}, u32[]{:S(2)}, u32[]{:S(2)}) collective-permute-start(bf16[8,64,128]{2,1,0:T(8,128)(2,1)S(1)} %collective-permute-done.7.refs_7_), channel_id=1, source_target_pairs={{0,1},{1,0},{2,3},{3,2},{4,5},{5,4},{6,7},{7,6},{8,9},{9,8},{10,11... | collective-permute-start | bytes 393224 | tf_op jit(solution)/shard_map/ppermute | solution.py:220
  52.5 24.7 %all-to-all-start = ((f32[256,1,128]{2,1,0:T(1,128)}), f32[256,1,128]{2,1,0:T(1,128)S(1)}, u32[]{:S(2)}, u32[]{:S(2)}) async-start(f32[256,1,128]{2,1,0:T(1,128)} %bitcast.35), calls=%async_computation | async-start | bytes 262144 | tf_op jit(solution)/shard_map/all_to_all | solution.py:275
  81.0 19.0 %all-to-all-start.1 = ((f32[256,1,128]{2,1,0:T(1,128)}), f32[256,1,128]{2,1,0:T(1,128)S(1)}, u32[]{:S(2)}, u32[]{:S(2)}) async-start(f32[256,1,128]{2,1,0:T(1,128)} %bitcast.33), calls=%async_computation.1 | async-start | bytes 262144 | tf_op jit(solution)/shard_map/all_to_all | solution.py:275
  119.4 8.2 %collective-permute-start.9 = (bf16[56,64,128]{2,1,0:T(8,128)(2,1)}, bf16[56,64,128]{2,1,0:T(8,128)(2,1)S(1)}, u32[]{:S(2)}, u32[]{:S(2)}) collective-permute-start(bf16[56,64,128]{2,1,0:T(8,128)(2,1)} %get-tuple-element.12), channel_id=1, source_target_pairs={{0,1},{1,0},{2,3},{3,2},{4,5},{5,4},{6,7},{7,6},{8,9},{9,8},{10,11... | collective-permute-start | bytes 2752520 | tf_op jit(solution)/shard_map/ppermute | solution.py:220
  120.3 2.5 %collective-permute-start.10 = (bf16[8,64,128]{2,1,0:T(8,128)(2,1)}, bf16[8,64,128]{2,1,0:T(8,128)(2,1)S(1)}, u32[]{:S(2)}, u32[]{:S(2)}) collective-permute-start(bf16[8,64,128]{2,1,0:T(8,128)(2,1)} %get-tuple-element.13), channel_id=1, source_target_pairs={{0,1},{1,0},{2,3},{3,2},{4,5},{5,4},{6,7},{7,6},{8,9},{9,8},{10,11... | collective-permute-start | bytes 393224 | tf_op jit(solution)/shard_map/ppermute | solution.py:220
  123.8 3.9 %collective-permute-start.11 = (bf16[8,64,128]{2,1,0:T(8,128)(2,1)S(1)}, bf16[8,64,128]{2,1,0:T(8,128)(2,1)S(1)}, u32[]{:S(2)}, u32[]{:S(2)}) collective-permute-start(bf16[8,64,128]{2,1,0:T(8,128)(2,1)S(1)} %add_convert_fusion.3), channel_id=1, source_target_pairs={{0,2},{1,15},{2,4},{3,1},{4,6},{5,3},{6,8},{7,5},{8,10},{9,7},{10,... | collective-permute-start | bytes 393224 | tf_op jit(solution)/shard_map/ppermute | solution.py:223
  128.8 5.3 %collective-permute-start.12 = (bf16[16,64,128]{2,1,0:T(8,128)(2,1)S(1)}, bf16[16,64,128]{2,1,0:T(8,128)(2,1)S(1)}, u32[]{:S(2)}, u32[]{:S(2)}) collective-permute-start(bf16[16,64,128]{2,1,0:T(8,128)(2,1)S(1)} %add_convert_fusion.2), channel_id=1, source_target_pairs={{0,2},{1,15},{2,4},{3,1},{4,6},{5,3},{6,8},{7,5},{8,10},{9,7},{10,... | collective-permute-start | bytes 786440 | tf_op jit(solution)/shard_map/ppermute | solution.py:223
  135.2 5.8 %collective-permute-start.13 = (bf16[16,64,128]{2,1,0:T(8,128)(2,1)S(1)}, bf16[16,64,128]{2,1,0:T(8,128)(2,1)S(1)}, u32[]{:S(2)}, u32[]{:S(2)}) collective-permute-start(bf16[16,64,128]{2,1,0:T(8,128)(2,1)S(1)} %add_convert_fusion.1), channel_id=1, source_target_pairs={{0,2},{1,15},{2,4},{3,1},{4,6},{5,3},{6,8},{7,5},{8,10},{9,7},{10,... | collective-permute-start | bytes 786440 | tf_op jit(solution)/shard_map/ppermute | solution.py:223
  142.2 6.5 %collective-permute-start.14 = (bf16[16,64,128]{2,1,0:T(8,128)(2,1)S(1)}, bf16[16,64,128]{2,1,0:T(8,128)(2,1)S(1)}, u32[]{:S(2)}, u32[]{:S(2)}) collective-permute-start(bf16[16,64,128]{2,1,0:T(8,128)(2,1)S(1)} %add_convert_fusion), channel_id=1, source_target_pairs={{0,2},{1,15},{2,4},{3,1},{4,6},{5,3},{6,8},{7,5},{8,10},{9,7},{10,... | collective-permute-start | bytes 786440 | tf_op jit(solution)/shard_map/ppermute | solution.py:223
  148.7 9.2 %collective-permute-start.15 = (bf16[8,64,128]{2,1,0:T(8,128)(2,1)S(1)}, bf16[8,64,128]{2,1,0:T(8,128)(2,1)S(1)}, u32[]{:S(2)}, u32[]{:S(2)}) collective-permute-start(bf16[8,64,128]{2,1,0:T(8,128)(2,1)S(1)} %slice.75), channel_id=1, source_target_pairs={{0,1},{1,0},{2,3},{3,2},{4,5},{5,4},{6,7},{7,6},{8,9},{9,8},{10,11... | collective-permute-start | bytes 393224 | tf_op jit(solution)/shard_map/ppermute | solution.py:220
  (7 other events, 8.9 us)

commit v2 on v1

v2 whole, which is shorter than its diff:
```python
import functools

import jax
import jax.numpy as jnp
import numpy as np
from jax import lax
from jax.experimental import pallas as pl
from jax.experimental.pallas import tpu as pltpu
from jax.sharding import PartitionSpec as P

XC_COEF = 0.7386
FOUR_PI = 12.566370614359172
KAPPA = 0.5
LANES = 128
F32 = jnp.float32
BF16 = jnp.bfloat16
HIGHEST = lax.Precision.HIGHEST
VMEM_LIMIT = 56 * 1024 * 1024


def cas_table(count):
    steps = np.arange(count)
    angle = 2.0 * np.pi * (steps[:, None] * steps[None, :] % count) / count
    return (np.cos(angle) + np.sin(angle)).astype(np.float32)


def symbol(count):
    return (2.0 - 2.0 * np.cos(2.0 * np.pi * np.arange(count) / count)).astype(np.float32)


def masked_line(orb_ref, line, live):
    parts = []
    for a in range(4):
        rows = orb_ref[line, a * 64 : (a + 1) * 64, :]
        parts.append(rows if a == 0 else jnp.where(a < live, rows, jnp.zeros((), BF16)))
    return jnp.concatenate(parts, axis=0)


def orbital_copies(orb_hbm, orb_ref, sems, chunk):
    return [
        pltpu.make_async_copy(orb_hbm.at[pl.ds(i * chunk, chunk)], orb_ref.at[pl.ds(i * chunk, chunk)], sems.at[i])
        for i in range(orb_ref.shape[0] // chunk)
    ]


def density_kernel(index_ref, live_ref, base_ref, orb_hbm, *refs, chunk):
    pieces, (cas_ref, dens_ref, spec_ref, orb_ref, table_ref, orb_sems, table_sems) = refs[:-7], refs[-7:]
    packed_rows = table_ref.shape[0] // 2
    copies = []
    for piece in pieces:
        for first in range(0, piece.shape[0], 8):
            i = len(copies)
            rows = table_ref.at[pl.ds(base_ref[i], 8)]
            copies.append(pltpu.make_async_copy(piece.at[pl.ds(first, 8)], rows, table_sems.at[i]))
    for copy in copies:
        copy.start()
    for copy in orbital_copies(orb_hbm, orb_ref, orb_sems, chunk):
        copy.start()
    for copy in copies:
        copy.wait()

    def fill(i, carry):
        both = table_ref[pl.ds(i * 8, 8)]
        table_ref[pl.ds(packed_rows + i * 8, 8)] = pltpu.roll(both, 64, 2)
        return carry

    lax.fori_loop(0, packed_rows // 8, fill, 0)
    left_lanes = lax.broadcasted_iota(jnp.int32, (64, LANES), 1) < 64

    def body(i, carry):
        first = i * chunk
        pltpu.make_async_copy(orb_hbm.at[pl.ds(first, chunk)], orb_ref.at[pl.ds(first, chunk)], orb_sems.at[i]).wait()
        rows_out = []
        for l in range(chunk):
            line = first + l
            phi = masked_line(orb_ref, line, live_ref[line])
            strips = []
            for a in range(4):
                halves = []
                for b in (0, 2):
                    at = line * 16 + a * 4 + b
                    halves.append(jnp.where(left_lanes, table_ref[index_ref[at]], table_ref[index_ref[at + 1]]))
                strips.append(jnp.concatenate(halves, axis=1))
            matrix = jnp.concatenate(strips, axis=0)
            product = jnp.dot(matrix, phi, preferred_element_type=F32)
            rows_out.append(jnp.sum(phi.astype(F32) * product, axis=0, keepdims=True))
        dens_ref[pl.ds(pl.multiple_of(first, 8), chunk), :] = jnp.concatenate(rows_out, axis=0)
        return carry

    lax.fori_loop(0, orb_ref.shape[0] // chunk, body, 0)
    spectrum = jnp.dot(dens_ref[...], cas_ref[...], precision=HIGHEST, preferred_element_type=F32)
    lines = spectrum.shape[0]
    wide = jnp.concatenate([spectrum, jnp.zeros((LANES - lines, spectrum.shape[1]), F32)], axis=0)
    spec_ref[...] = wide.T


def solve_kernel(part_ref, in_ref, cx_ref, cxt_ref, cz_ref, sx_ref, sz_ref, sy_ref, out_ref, *, cells_x, cells_z, cols, heights):
    core = part_ref[0]
    plane = part_ref[1]
    lane = lax.broadcasted_iota(jnp.int32, (cols, LANES), 1)
    group_of = lane // cells_z
    slots = LANES // cells_z
    skewed = [
        pltpu.roll(in_ref[pl.ds(h, cols, stride=heights), :], cells_z * h, 1) if h else in_ref[pl.ds(h, cols, stride=heights), :]
        for h in range(heights)
    ]
    rows = []
    for x in range(cells_x):
        mixed = jnp.zeros((cols, LANES), F32)
        for g in range(slots):
            mixed = jnp.where(group_of == g, skewed[(g - x) % slots], mixed)
        rows.append(pltpu.roll(mixed, LANES - cells_z * x, 1) if x else mixed)
    field = jnp.concatenate(rows, axis=0)
    forward = cx_ref[core]
    spec = jnp.dot(forward, field, precision=HIGHEST, preferred_element_type=F32)
    spec = jnp.dot(spec, cz_ref[...], precision=HIGHEST, preferred_element_type=F32)
    scale = sx_ref[core] + sz_ref[...] + sy_ref[plane]
    spec = spec / scale
    spec = jnp.dot(spec, cz_ref[...], precision=HIGHEST, preferred_element_type=F32)
    back = jnp.dot(cxt_ref[core], spec, precision=HIGHEST, preferred_element_type=F32)
    skewed = []
    for x in range(cells_x):
        part = back[x * cols : (x + 1) * cols]
        skewed.append(pltpu.roll(part, cells_z * x, 1) if x else part)
    for h in range(heights):
        mixed = jnp.zeros((cols, LANES), F32)
        for x in range(cells_x):
            mixed = jnp.where(group_of == (h + x) % slots, skewed[x], mixed)
        mixed = pltpu.roll(mixed, LANES - cells_z * h, 1) if h else mixed
        out_ref[pl.ds(h, cols, stride=heights), :] = mixed


def hamiltonian_kernel(
    pair_ref,
    live_ref,
    base_ref,
    orb_hbm,
    dens_ref,
    back_ref,
    cas_ref,
    pot_ref,
    keep_hbm,
    first_hbm,
    rest_hbm,
    orb_ref,
    left_ref,
    right_ref,
    keep_ref,
    give_ref,
    orb_sems,
    out_sems,
    *,
    chunk,
):
    lines = dens_ref.shape[0]
    for copy in orbital_copies(orb_hbm, orb_ref, orb_sems, chunk):
        copy.start()

    def clear(i, carry):
        left_ref[pl.ds(i * 8, 8)] = jnp.zeros((8, 64, LANES), F32)
        right_ref[pl.ds(i * 8, 8)] = jnp.zeros((8, 64, LANES), F32)
        return carry

    lax.fori_loop(0, left_ref.shape[0] // 8, clear, 0)
    hartree = lax.dot_general(
        back_ref[...].T, cas_ref[...], (((1,), (0,)), ((), ())), precision=HIGHEST, preferred_element_type=F32
    )
    dens = dens_ref[...]
    pot_ref[...] = hartree[:lines] - XC_COEF * jnp.exp(jnp.log(dens * dens + 1.0) * (1.0 / 6.0))

    def body(i, carry):
        first = i * chunk
        pltpu.make_async_copy(orb_hbm.at[pl.ds(first, chunk)], orb_ref.at[pl.ds(first, chunk)], orb_sems.at[i]).wait()
        potential = pot_ref[pl.ds(pl.multiple_of(first, 8), chunk), :]
        for l in range(chunk):
            line = first + l
            phi = masked_line(orb_ref, line, live_ref[line])
            weighted = (phi.astype(F32) * potential[l : l + 1, :]).astype(BF16)
            full = lax.dot_general(weighted, phi, (((1,), (1,)), ((), ())), preferred_element_type=F32)
            for a in range(4):
                for b in (0, 2):
                    at = line * 16 + a * 4 + b
                    both = full[a * 64 : (a + 1) * 64, b * 64 : b * 64 + LANES]
                    left_ref[pair_ref[at]] += both
                    right_ref[pair_ref[at + 1]] += both
        return carry

    lax.fori_loop(0, lines // chunk, body, 0)
    left_lanes = lax.broadcasted_iota(jnp.int32, (8, 64, LANES), 2) < 64

    def emit(base):
        low, high = pl.ds(base, 8), pl.ds(base + 8, 8)
        crossed = jnp.where(left_lanes, left_ref[high], right_ref[low])
        return jnp.where(left_lanes, left_ref[low], right_ref[high]) + pltpu.roll(crossed, 64, 2)

    kept = keep_ref.shape[0] // 8
    given = give_ref.shape[0] // 8
    copies = []
    for i in range(given):
        give_ref[i * 8 : i * 8 + 8] = emit(base_ref[kept + i]).astype(BF16)
        target = first_hbm.at[pl.ds(i * 8, 8)] if i < 3 else rest_hbm.at[pl.ds(i * 8 - 24, 8)]
        copies.append(pltpu.make_async_copy(give_ref.at[pl.ds(i * 8, 8)], target, out_sems.at[kept + i]))
        copies[-1].start()
    for i in range(kept):
        keep_ref[i * 8 : i * 8 + 8] = emit(base_ref[i])
        copies.append(pltpu.make_async_copy(keep_ref.at[pl.ds(i * 8, 8)], keep_hbm.at[pl.ds(i * 8, 8)], out_sems.at[i]))
        copies[-1].start()
    for copy in copies:
        copy.wait()


def per_device(orbitals, live_atoms, pair_index, density_blocks):
    cells_x, cells_z, width, line_cells = orbitals.shape
    cols = lax.axis_size("col")
    heights = lax.axis_size("height")
    full_x = cells_x * cols
    full_z = cells_z * heights
    lines = cells_x * cells_z
    share = density_blocks.shape[0]
    devices = cols * heights
    copies = devices // line_cells
    chunk = 16
    block_rows = share * heights // 2

    cas_y = cas_table(line_cells)
    cas_y2 = np.repeat(cas_y, copies, axis=1)
    cas_x = cas_table(full_x)
    order = np.arange(full_x).reshape(cols, cells_x).T.reshape(-1)
    half_x = full_x // copies
    forward_x = cas_x.reshape(copies, half_x, full_x)[:, :, order]
    back_x = forward_x.transpose(0, 2, 1).copy()
    cas_z = cas_table(full_z)
    norm = 1.0 / (full_x * full_z * line_cells)
    unit = FOUR_PI * norm
    sym_x = np.broadcast_to(symbol(full_x).reshape(copies, half_x, 1) / unit, (copies, half_x, LANES)).astype(np.float32)
    sym_z = ((symbol(full_z) + KAPPA * KAPPA) / unit).reshape(1, full_z).astype(np.float32)
    sym_y = (symbol(line_cells) / unit).astype(np.float32)

    orb = orbitals.reshape(lines, width, line_cells)
    live = live_atoms.reshape(lines)
    pairs = pair_index.reshape(lines * 16)
    packed = jnp.concatenate([density_blocks[: share // 2], density_blocks[share // 2 :]], axis=2)
    chips = heights // 2
    far = chips // 2
    height = lax.axis_index("height")
    chip, core = height // 2, height % 2
    turn = 1 - 2 * core
    twin = [(h, h ^ 1) for h in range(heights)]

    def across(values):
        return lax.ppermute(values, "height", twin)

    def onward(values, hops):
        shift = 2 * hops
        return lax.ppermute(values, "height", [(h, (h + shift * (1 - 2 * (h % 2))) % heights) for h in range(heights)])

    def place_of(distance, owner):
        return ((chip + distance) % chips) * 2 + owner

    whole_chip = jnp.concatenate([packed, across(packed)], axis=0)
    near = onward(whole_chip, 1)
    second = onward(whole_chip, 2)
    arrived = [near, second, onward(near, 2), onward(second[: share // 2], 2)]
    pieces = [whole_chip]
    heights_of = [place_of(0, core), place_of(0, 1 - core)]
    for d, piece in enumerate(arrived, 1):
        pieces += [piece, across(piece)]
        count = 2 if d < far else 1
        heights_of += [place_of(-turn * d, core), place_of(-turn * d, 1 - core)][:count]
        heights_of += [place_of(turn * d, 1 - core), place_of(turn * d, core)][:count]
    table_rows = (jnp.stack(heights_of) * (share // 2)).astype(jnp.int32)
    keep_of, give_of = [], []
    for d in range(far, -1, -1):
        keep_of.append(place_of(turn * d, core))
        give_of.append(place_of(-turn * d, 1 - core))
        if 0 < d < far:
            keep_of.append(place_of(turn * d, 1 - core))
            give_of.append(place_of(-turn * d, core))
    sum_rows = (jnp.stack(keep_of + give_of) * share).astype(jnp.int32)

    side = jnp.arange(lines * 16, dtype=jnp.int32) % 2
    table_index = (pairs // share) * (share // 2) + pairs % (share // 2)
    table_index = table_index + jnp.where((pairs // (share // 2)) % 2 == side, 0, block_rows)
    smem = pl.BlockSpec(memory_space=pltpu.SMEM)
    vmem = pl.BlockSpec(memory_space=pltpu.VMEM)
    hbm = pl.BlockSpec(memory_space=pl.ANY)
    params = pltpu.CompilerParams(vmem_limit_bytes=VMEM_LIMIT)
    density, spectrum = pl.pallas_call(
        functools.partial(density_kernel, chunk=chunk),
        in_specs=[smem, smem, smem, hbm] + [hbm] * len(pieces) + [vmem],
        out_specs=[vmem, vmem],
        out_shape=[
            jax.ShapeDtypeStruct((lines, line_cells), F32),
            jax.ShapeDtypeStruct((devices, LANES), F32),
        ],
        scratch_shapes=[
            pltpu.VMEM((lines, width, line_cells), BF16),
            pltpu.VMEM((2 * block_rows, 64, LANES), BF16),
            pltpu.SemaphoreType.DMA((lines // chunk,)),
            pltpu.SemaphoreType.DMA((heights,)),
        ],
        compiler_params=params,
        name="density",
    )(table_index, live, table_rows, orb, *pieces, jnp.asarray(cas_y2))

    def exchange(values):
        out = lax.all_to_all(values.reshape(devices, 1, LANES), ("col", "height"), split_axis=0, concat_axis=0, tiled=True)
        return out.reshape(devices, LANES)

    device = lax.axis_index("col") * heights + height
    part = jnp.stack([device % copies, device // copies]).astype(jnp.int32)
    solved = pl.pallas_call(
        lambda *refs: solve_kernel(*refs, cells_x=cells_x, cells_z=cells_z, cols=cols, heights=heights),
        in_specs=[smem, vmem, vmem, vmem, vmem, vmem, vmem, smem],
        out_specs=vmem,
        out_shape=jax.ShapeDtypeStruct((devices, LANES), F32),
        compiler_params=params,
        name="solve",
    )(
        part,
        exchange(spectrum),
        jnp.asarray(forward_x),
        jnp.asarray(back_x),
        jnp.asarray(cas_z),
        jnp.asarray(sym_x),
        jnp.asarray(sym_z),
        jnp.asarray(sym_y),
    )
    returned = exchange(solved)

    half_rows = block_rows // 2
    potential, keep, give_first, give_rest = pl.pallas_call(
        functools.partial(hamiltonian_kernel, chunk=chunk),
        in_specs=[smem, smem, smem, hbm, vmem, vmem, vmem],
        out_specs=[vmem, hbm, hbm, hbm],
        out_shape=[
            jax.ShapeDtypeStruct((lines, line_cells), F32),
            jax.ShapeDtypeStruct((half_rows, 64, LANES), F32),
            jax.ShapeDtypeStruct((3 * share // 2, 64, LANES), BF16),
            jax.ShapeDtypeStruct((half_rows - 3 * share // 2, 64, LANES), BF16),
        ],
        scratch_shapes=[
            pltpu.VMEM((lines, width, line_cells), BF16),
            pltpu.VMEM((2 * block_rows, 64, LANES), F32),
            pltpu.VMEM((2 * block_rows, 64, LANES), F32),
            pltpu.VMEM((half_rows, 64, LANES), F32),
            pltpu.VMEM((half_rows, 64, LANES), BF16),
            pltpu.SemaphoreType.DMA((lines // chunk,)),
            pltpu.SemaphoreType.DMA((heights,)),
        ],
        compiler_params=params,
        name="hamiltonian",
    )(pairs, live, sum_rows, orb, density, returned, jnp.asarray(cas_y2.T.copy()))

    half = share // 2
    got_first = across(give_first)
    got_rest = across(lax.optimization_barrier((give_rest, got_first))[0])
    inner = onward((keep[: 3 * half] + got_first.astype(F32)).astype(BF16), 2)
    local = keep[3 * half :] + got_rest.astype(F32)
    from_far = jnp.concatenate([inner[:half].astype(F32), jnp.zeros((half, 64, LANES), F32)], axis=0)
    by_two = onward((local[: 2 * half] + from_far).astype(BF16), 2)
    by_one = onward((local[2 * half : 4 * half] + inner[half:].astype(F32)).astype(BF16), 1)
    summed = local[4 * half :] + by_two[:half].astype(F32) + by_one[:half].astype(F32)
    summed = summed + across(by_two[half:]).astype(F32) + across(by_one[half:]).astype(F32)
    hamiltonian = jnp.concatenate([summed[:, :, :64], summed[:, :, 64:]], axis=0)
    return potential.reshape(cells_x, cells_z, line_cells), hamiltonian


def solution(mesh):
    placed = (
        P("col", "height", None, None),
        P("col", "height"),
        P("col", "height", None, None),
        P(("col", "height"), None, None),
    )
    return jax.shard_map(
        per_device,
        mesh=mesh,
        in_specs=placed,
        out_specs=(P("col", "height", None), P(("col", "height"), None, None)),
        check_vma=False,
    )
```

time: 161 us -> 139 us (0.86)
  starting transfers between devices: 55.7 us -> 42.7 us
  Pallas kernels: 36.1 us -> 27.6 us
  waiting for transfers between devices: 53.8 us -> 56.3 us
  other arithmetic: 8.12 us -> 6.36 us
    ppermute x8 -> x7, starting transfers between devices: 20.4 us -> 8.66 us  [onward(): lax.ppermute(values, 'height', [(h, (h + shift * (1 - 2 * (h % 2))) % hei...]
    pallas_call x2, Pallas kernels: 33 us -> 24.5 us  [the longest x1 12.4 us: per_device(): pl.pallas_call(functools.partial(hamiltonian_kernel, chunk=chunk), in_spe...]
    convert_element_type x4 -> x2, other arithmetic: 4.38 us -> 1.42 us  [the longest x1 1.24 us: per_device(): inner = onward((keep[:3 * half] + got_first.astype(F32)).astype(BF16), 2)]
    ppermute x8 -> x7, waiting for transfers between devices: 24.4 us -> 27 us  [onward(): lax.ppermute(values, 'height', [(h, (h + shift * (1 - 2 * (h % 2))) % hei...]
    ppermute x8 -> x9, waiting for transfers between devices: 4.93 us -> 4.73 us  [across(): return lax.ppermute(values, 'height', twin)]
    ppermute x8 -> x9, starting transfers between devices: 17.5 us -> 17.4 us  [across(): return lax.ppermute(values, 'height', twin)]
  transfers between devices with their start and end apart: 18 -> 18, of which waited for: 13 -> 12; matrix products, arithmetic and copies ran while one was open for 3% -> 5% of each run, Pallas kernels for 0% -> 0%
where the time goes in v2:
time: 139 us
  waiting for transfers between devices  56.3 us (41%)
  starting transfers between devices  42.7 us (31%)
  Pallas kernels  27.6 us (20%)
  other arithmetic  6.36 us (5%)
  local copies, waits for them, and re-layouts  4.82 us (3%)
    ppermute x7, waiting for transfers between devices, onward(): lax.ppermute(values, 'height', [(h, (h + shift * (1 - 2 * (h % 2))) % hei...  27 us
    all_to_all x2, waiting for transfers between devices, exchange(): lax.all_to_all(values.reshape(devices, 1, LANES), ('col', 'height'), spli...  24.6 us
    ppermute x9, starting transfers between devices, across(): return lax.ppermute(values, 'height', twin)  17.4 us
    all_to_all x2, starting transfers between devices, exchange(): lax.all_to_all(values.reshape(devices, 1, LANES), ('col', 'height'), spli...  16.6 us
    pallas_call x1, Pallas kernels, per_device(): pl.pallas_call(functools.partial(hamiltonian_kernel, chunk=chunk), in_spe...  12.4 us
    pallas_call x1, Pallas kernels, per_device(): pl.pallas_call(functools.partial(density_kernel, chunk=chunk), in_specs=[...  12.1 us
    ppermute x7, starting transfers between devices, onward(): lax.ppermute(values, 'height', [(h, (h + shift * (1 - 2 * (h % 2))) % hei...  8.66 us
    ppermute x9, waiting for transfers between devices, across(): return lax.ppermute(values, 'height', twin)  4.73 us
  transfers between devices with their start and end apart: 18, of which 12 were waited for; matrix products, arithmetic and copies ran while one was open for 5% of the time, Pallas kernels for 0%

profile of v2, /device:TPU:1, one launch (start us, length us, event | category | flops | bytes accessed | tf_op | source)
XLA Modules:
  0.0 138.7 jit_solution(13528750252693307725)
XLA Ops:
  0.7 1.0 fusion.17
  1.8 3.3 %collective-permute-start = (bf16[8,64,128]{2,1,0:T(8,128)(2,1)S(1)}, bf16[8,64,128]{2,1,0:T(8,128)(2,1)S(1)}, u32[]{:S(2)}, u32[]{:S(2)}) collective-permute-start(bf16[8,64,128]{2,1,0:T(8,128)(2,1)S(1)} %pad_maximum_fusion.2), channel_id=1, source_target_pairs={{0,1},{1,0},{2,3},{3,2},{4,5},{5,4},{6,7},{7,6},{8,9},{9,8},{10,11... | collective-permute-start | bytes 393224 | tf_op jit(solution)/shard_map/ppermute | solution.py:251
  5.1 1.0 collective-permute-done
  6.2 3.9 %collective-permute-start.1 = (bf16[16,64,128]{2,1,0:T(8,128)(2,1)S(1)}, bf16[16,64,128]{2,1,0:T(8,128)(2,1)S(1)}, u32[]{:S(2)}, u32[]{:S(2)}) collective-permute-start(bf16[16,64,128]{2,1,0:T(8,128)(2,1)S(1)} %pad_maximum_fusion.1.refs_0_), channel_id=1, source_target_pairs={{0,2},{1,15},{2,4},{3,1},{4,6},{5,3},{6,8},{7,5},{8,10},{9,7},{10,... | collective-permute-start | bytes 786440 | tf_op jit(solution)/shard_map/ppermute | solution.py:255
  10.1 1.2 collective-permute-start.3
  11.3 4.6 %collective-permute-done.1.refs_1_ = bf16[16,64,128]{2,1,0:T(8,128)(2,1)S(1)} collective-permute-done((bf16[16,64,128]{2,1,0:T(8,128)(2,1)S(1)}, bf16[16,64,128]{2,1,0:T(8,128)(2,1)S(1)}, u32[]{:S(2)}, u32[]{:S(2)}) %collective-permute-start.1) | collective-permute-done | bytes 262176 | tf_op jit(solution)/shard_map/ppermute | solution.py:255
  16.7 4.8 %collective-permute-done.3.refs_3_ = bf16[16,64,128]{2,1,0:T(8,128)(2,1)S(1)} collective-permute-done((bf16[16,64,128]{2,1,0:T(8,128)(2,1)S(1)}, bf16[16,64,128]{2,1,0:T(8,128)(2,1)S(1)}, u32[]{:S(2)}, u32[]{:S(2)}) %collective-permute-start.3) | collective-permute-done | bytes 262176 | tf_op jit(solution)/shard_map/ppermute | solution.py:255
  21.5 1.8 %collective-permute-start.7 = (bf16[8,64,128]{2,1,0:T(8,128)(2,1)S(1)}, bf16[8,64,128]{2,1,0:T(8,128)(2,1)S(1)}, u32[]{:S(2)}, u32[]{:S(2)}) collective-permute-start(bf16[8,64,128]{2,1,0:T(8,128)(2,1)S(1)} %slice.65), channel_id=1, source_target_pairs={{0,4},{1,13},{2,6},{3,15},{4,8},{5,1},{6,10},{7,3},{8,12},{9,5},{1... | collective-permute-start | bytes 393224 | tf_op jit(solution)/shard_map/ppermute | solution.py:255
  24.3 4.5 %collective-permute-start.6 = (bf16[16,64,128]{2,1,0:T(8,128)(2,1)S(1)}, bf16[16,64,128]{2,1,0:T(8,128)(2,1)S(1)}, u32[]{:S(2)}, u32[]{:S(2)}) collective-permute-start(bf16[16,64,128]{2,1,0:T(8,128)(2,1)S(1)} %collective-permute-done.5.refs_5_), channel_id=1, source_target_pairs={{0,1},{1,0},{2,3},{3,2},{4,5},{5,4},{6,7},{7,6},{8,9},{9,8},{10,11... | collective-permute-start | bytes 786440 | tf_op jit(solution)/shard_map/ppermute | solution.py:251
  32.6 12.1 %density.1 = (f32[96,128]{1,0:T(8,128)}, f32[256,128]{1,0:T(8,128)}) custom-call(s32[1536]{0:T(1024)} %fusion.8.index_ref, s32[96]{0:T(128)} %reshape.29.live_ref, s32[16]{0:T(128)} %broadcast_multiply_fusion.base_ref, bf16[96,256,128]{2,1,0:T(8,128)(2,1)} %bitcast.30, bf16[16,64,128]{2,1,0:T(8,128)(2,1)} %copy-done, bf16[16,64,128]{2,1,0:T(8,128)(2,1)} %copy-done.4, ...), custom_call_target="tpu_custom_call" | custom-call | tf_op jit(solution)/shard_map/density/pallas_call | solution.py:288
  44.7 10.8 %all-to-all-start = ((f32[256,1,128]{2,1,0:T(1,128)}), f32[256,1,128]{2,1,0:T(1,128)S(1)}, u32[]{:S(2)}, u32[]{:S(2)}) async-start(f32[256,1,128]{2,1,0:T(1,128)} %bitcast.35), calls=%async_computation | async-start | bytes 262144 | tf_op jit(solution)/shard_map/all_to_all | solution.py:307
  56.1 12.3 %all-to-all-done = f32[256,1,128]{2,1,0:T(1,128)S(1)} async-done(((f32[256,1,128]{2,1,0:T(1,128)}), f32[256,1,128]{2,1,0:T(1,128)S(1)}, u32[]{:S(2)}, u32[]{:S(2)}) %all-to-all-start) | async-done | bytes 131104 | tf_op jit(solution)/shard_map/all_to_all | solution.py:307
  69.0 3.1 %solve.1 = f32[256,128]{1,0:T(8,128)} custom-call(s32[2]{0:T(128)} %pad_add_fusion.refs_0_, f32[256,128]{1,0:T(8,128)} %bitcast.33, f32[2,96,192]{2,1,0:T(8,128)} %constant.203.clone.refs_2_, f32[2,192,96]{2,1,0:T(8,128)} %constant.204.clone.refs_3_, f32[128,128]{1,0:T(8,128)} %constant.205.clone.refs_4_, f32[2,96,128]{2,1,0:T(8,128)} %constant.206.clone.refs_5_, ...), custom_call_target="tpu_custom_call" | custom-call | tf_op jit(solution)/shard_map/solve/pallas_call | solution.py:312
  72.1 5.9 %all-to-all-start.1 = ((f32[256,1,128]{2,1,0:T(1,128)}), f32[256,1,128]{2,1,0:T(1,128)S(1)}, u32[]{:S(2)}, u32[]{:S(2)}) async-start(f32[256,1,128]{2,1,0:T(1,128)} %bitcast.34), calls=%async_computation.1 | async-start | bytes 262144 | tf_op jit(solution)/shard_map/all_to_all | solution.py:307
  78.6 12.3 %all-to-all-done.1 = f32[256,1,128]{2,1,0:T(1,128)S(1)} async-done(((f32[256,1,128]{2,1,0:T(1,128)}), f32[256,1,128]{2,1,0:T(1,128)S(1)}, u32[]{:S(2)}, u32[]{:S(2)}) %all-to-all-start.1) | async-done | bytes 131104 | tf_op jit(solution)/shard_map/all_to_all | solution.py:307
  91.6 12.4 %hamiltonian.1 = (f32[96,128]{1,0:T(8,128)}, f32[64,64,128]{2,1,0:T(8,128)}, bf16[24,64,128]{2,1,0:T(8,128)(2,1)}, bf16[40,64,128]{2,1,0:T(8,128)(2,1)}) custom-call(s32[1536]{0:T(1024)} %copy-done.11, s32[96]{0:T(128)} %reshape.29.live_ref, s32[16]{0:T(128)} %broadcast_multiply_fusion.1.base_ref, bf16[96,256,128]{2,1,0:T(8,128)(2,1)} %bitcast.31, ...), custom_call_target="tpu_custom_call" | custom-call | tf_op jit(solution)/shard_map/hamiltonian/pallas_call | solution.py:332
  105.0 1.6 %collective-permute-done.9 = bf16[24,64,128]{2,1,0:T(8,128)(2,1)S(1)} collective-permute-done((bf16[24,64,128]{2,1,0:T(8,128)(2,1)}, bf16[24,64,128]{2,1,0:T(8,128)(2,1)S(1)}, u32[]{:S(2)}, u32[]{:S(2)}) %collective-permute-start.9) | collective-permute-done | bytes 393248 | tf_op jit(solution)/shard_map/ppermute | solution.py:251
  107.0 1.2 add_convert_fusion
  108.9 1.5 %convert_add_fusion = f32[40,64,128]{2,1,0:T(8,128)S(1)} fusion(bf16[40,64,128]{2,1,0:T(8,128)(2,1)S(1)} %collective-permute-done.10, f32[64,64,128]{2,1,0:T(8,128)} %get-tuple-element.12), kind=kLoop, calls=%fused_computation | loop fusion | flops 655360 | bytes 3276800 | tf_op jit(solution)/shard_map/add | solution.py:359
  110.4 9.9 %collective-permute-done.11 = bf16[24,64,128]{2,1,0:T(8,128)(2,1)S(1)} collective-permute-done((bf16[24,64,128]{2,1,0:T(8,128)(2,1)S(1)}, bf16[24,64,128]{2,1,0:T(8,128)(2,1)S(1)}, u32[]{:S(2)}, u32[]{:S(2)}) %collective-permute-start.11) | collective-permute-done | bytes 393248 | tf_op jit(solution)/shard_map/ppermute | solution.py:255
  120.5 1.2 collective-permute-start.12
  121.7 7.3 %collective-permute-done.12 = bf16[16,64,128]{2,1,0:T(8,128)(2,1)S(1)} collective-permute-done((bf16[16,64,128]{2,1,0:T(8,128)(2,1)S(1)}, bf16[16,64,128]{2,1,0:T(8,128)(2,1)S(1)}, u32[]{:S(2)}, u32[]{:S(2)}) %collective-permute-start.12) | collective-permute-done | bytes 262176 | tf_op jit(solution)/shard_map/ppermute | solution.py:255
  129.0 4.8 %collective-permute-start.14 = (bf16[8,64,128]{2,1,0:T(8,128)(2,1)S(1)}, bf16[8,64,128]{2,1,0:T(8,128)(2,1)S(1)}, u32[]{:S(2)}, u32[]{:S(2)}) collective-permute-start(bf16[8,64,128]{2,1,0:T(8,128)(2,1)S(1)} %slice.73), channel_id=1, source_target_pairs={{0,1},{1,0},{2,3},{3,2},{4,5},{5,4},{6,7},{7,6},{8,9},{9,8},{10,11... | collective-permute-start | bytes 393224 | tf_op jit(solution)/shard_map/ppermute | solution.py:251
  133.8 2.8 %collective-permute-start.15 = (bf16[8,64,128]{2,1,0:T(8,128)(2,1)S(1)}, bf16[8,64,128]{2,1,0:T(8,128)(2,1)S(1)}, u32[]{:S(2)}, u32[]{:S(2)}) collective-permute-start(bf16[8,64,128]{2,1,0:T(8,128)(2,1)S(1)} %slice.74), channel_id=1, source_target_pairs={{0,1},{1,0},{2,3},{3,2},{4,5},{5,4},{6,7},{7,6},{8,9},{9,8},{10,11... | collective-permute-start | bytes 393224 | tf_op jit(solution)/shard_map/ppermute | solution.py:251
  (67 shorter events, 12.6 us)
Async XLA Ops:
  0.6 15.5 %copy-start.12 = (s32[12,8,4,4]{0,3,2,1:T(4,128)S(1)}, s32[12,8,4,4]{0,3,2,1:T(4,128)}, u32[]{:S(2)}) copy-start(s32[12,8,4,4]{0,3,2,1:T(4,128)} %param.14) | copy-start | bytes 18436
  0.6 28.8 %copy-start.13 = (s32[12,8]{0,1:T(8,128)S(1)}, s32[12,8]{0,1:T(8,128)}, u32[]{:S(2)}) copy-start(s32[12,8]{0,1:T(8,128)} %param.13) | copy-start | bytes 1156
  1.8 4.3 %collective-permute-start = (bf16[8,64,128]{2,1,0:T(8,128)(2,1)S(1)}, bf16[8,64,128]{2,1,0:T(8,128)(2,1)S(1)}, u32[]{:S(2)}, u32[]{:S(2)}) collective-permute-start(bf16[8,64,128]{2,1,0:T(8,128)(2,1)S(1)} %pad_maximum_fusion.2), channel_id=1, source_target_pairs={{0,1},{1,0},{2,3},{3,2},{4,5},{5,4},{6,7},{7,6},{8,9},{9,8},{10,11... | collective-permute-start | bytes 393224 | tf_op jit(solution)/shard_map/ppermute | solution.py:251
  6.2 25.5 %copy-start = (bf16[16,64,128]{2,1,0:T(8,128)(2,1)}, bf16[16,64,128]{2,1,0:T(8,128)(2,1)S(1)}, u32[]{:S(2)}) copy-start(bf16[16,64,128]{2,1,0:T(8,128)(2,1)S(1)} %pad_maximum_fusion.1.refs_0_) | copy-start | bytes 786436
  6.2 9.6 %collective-permute-start.1 = (bf16[16,64,128]{2,1,0:T(8,128)(2,1)S(1)}, bf16[16,64,128]{2,1,0:T(8,128)(2,1)S(1)}, u32[]{:S(2)}, u32[]{:S(2)}) collective-permute-start(bf16[16,64,128]{2,1,0:T(8,128)(2,1)S(1)} %pad_maximum_fusion.1.refs_0_), channel_id=1, source_target_pairs={{0,2},{1,15},{2,4},{3,1},{4,6},{5,3},{6,8},{7,5},{8,10},{9,7},{10,... | collective-permute-start | bytes 786440 | tf_op jit(solution)/shard_map/ppermute | solution.py:255
  10.1 11.3 %collective-permute-start.3 = (bf16[16,64,128]{2,1,0:T(8,128)(2,1)S(1)}, bf16[16,64,128]{2,1,0:T(8,128)(2,1)S(1)}, u32[]{:S(2)}, u32[]{:S(2)}) collective-permute-start(bf16[16,64,128]{2,1,0:T(8,128)(2,1)S(1)} %pad_maximum_fusion.1.refs_0_), channel_id=1, source_target_pairs={{0,4},{1,13},{2,6},{3,15},{4,8},{5,1},{6,10},{7,3},{8,12},{9,5},{1... | collective-permute-start | bytes 786440 | tf_op jit(solution)/shard_map/ppermute | solution.py:255
  15.9 15.8 %copy-start.4 = (bf16[16,64,128]{2,1,0:T(8,128)(2,1)}, bf16[16,64,128]{2,1,0:T(8,128)(2,1)S(1)}, u32[]{:S(2)}) copy-start(bf16[16,64,128]{2,1,0:T(8,128)(2,1)S(1)} %collective-permute-done.1.refs_1_) | copy-start | bytes 786436
  15.9 8.4 %collective-permute-start.5 = (bf16[16,64,128]{2,1,0:T(8,128)(2,1)S(1)}, bf16[16,64,128]{2,1,0:T(8,128)(2,1)S(1)}, u32[]{:S(2)}, u32[]{:S(2)}) collective-permute-start(bf16[16,64,128]{2,1,0:T(8,128)(2,1)S(1)} %collective-permute-done.1.refs_1_), channel_id=1, source_target_pairs={{0,4},{1,13},{2,6},{3,15},{4,8},{5,1},{6,10},{7,3},{8,12},{9,5},{1... | collective-permute-start | bytes 786440 | tf_op jit(solution)/shard_map/ppermute | solution.py:255
  16.7 28.0 %copy-start.11 = (s32[1536]{0:T(1024)}, s32[1536]{0:T(1024)S(1)}, u32[]{:S(2)}) copy-start(s32[1536]{0:T(1024)S(1)} %reshape.28.pair_ref) | copy-start | bytes 18436
  21.5 8.7 %collective-permute-start.7 = (bf16[8,64,128]{2,1,0:T(8,128)(2,1)S(1)}, bf16[8,64,128]{2,1,0:T(8,128)(2,1)S(1)}, u32[]{:S(2)}, u32[]{:S(2)}) collective-permute-start(bf16[8,64,128]{2,1,0:T(8,128)(2,1)S(1)} %slice.65), channel_id=1, source_target_pairs={{0,4},{1,13},{2,6},{3,15},{4,8},{5,1},{6,10},{7,3},{8,12},{9,5},{1... | collective-permute-start | bytes 393224 | tf_op jit(solution)/shard_map/ppermute | solution.py:255
  23.3 8.4 %collective-permute-start.4 = (bf16[16,64,128]{2,1,0:T(8,128)(2,1)S(1)}, bf16[16,64,128]{2,1,0:T(8,128)(2,1)S(1)}, u32[]{:S(2)}, u32[]{:S(2)}) collective-permute-start(bf16[16,64,128]{2,1,0:T(8,128)(2,1)S(1)} %collective-permute-done.3.refs_3_), channel_id=1, source_target_pairs={{0,1},{1,0},{2,3},{3,2},{4,5},{5,4},{6,7},{7,6},{8,9},{9,8},{10,11... | collective-permute-start | bytes 786440 | tf_op jit(solution)/shard_map/ppermute | solution.py:251
  23.3 8.4 %collective-permute-start.2 = (bf16[16,64,128]{2,1,0:T(8,128)(2,1)S(1)}, bf16[16,64,128]{2,1,0:T(8,128)(2,1)S(1)}, u32[]{:S(2)}, u32[]{:S(2)}) collective-permute-start(bf16[16,64,128]{2,1,0:T(8,128)(2,1)S(1)} %collective-permute-done.1.refs_1_), channel_id=1, source_target_pairs={{0,1},{1,0},{2,3},{3,2},{4,5},{5,4},{6,7},{7,6},{8,9},{9,8},{10,11... | collective-permute-start | bytes 786440 | tf_op jit(solution)/shard_map/ppermute | solution.py:251
  24.3 7.4 %collective-permute-start.6 = (bf16[16,64,128]{2,1,0:T(8,128)(2,1)S(1)}, bf16[16,64,128]{2,1,0:T(8,128)(2,1)S(1)}, u32[]{:S(2)}, u32[]{:S(2)}) collective-permute-start(bf16[16,64,128]{2,1,0:T(8,128)(2,1)S(1)} %collective-permute-done.5.refs_5_), channel_id=1, source_target_pairs={{0,1},{1,0},{2,3},{3,2},{4,5},{5,4},{6,7},{7,6},{8,9},{9,8},{10,11... | collective-permute-start | bytes 786440 | tf_op jit(solution)/shard_map/ppermute | solution.py:251
  30.2 1.4 %collective-permute-start.8 = (bf16[8,64,128]{2,1,0:T(8,128)(2,1)S(1)}, bf16[8,64,128]{2,1,0:T(8,128)(2,1)S(1)}, u32[]{:S(2)}, u32[]{:S(2)}) collective-permute-start(bf16[8,64,128]{2,1,0:T(8,128)(2,1)S(1)} %collective-permute-done.7.refs_7_), channel_id=1, source_target_pairs={{0,1},{1,0},{2,3},{3,2},{4,5},{5,4},{6,7},{7,6},{8,9},{9,8},{10,11... | collective-permute-start | bytes 393224 | tf_op jit(solution)/shard_map/ppermute | solution.py:251
  44.7 23.6 %all-to-all-start = ((f32[256,1,128]{2,1,0:T(1,128)}), f32[256,1,128]{2,1,0:T(1,128)S(1)}, u32[]{:S(2)}, u32[]{:S(2)}) async-start(f32[256,1,128]{2,1,0:T(1,128)} %bitcast.35), calls=%async_computation | async-start | bytes 262144 | tf_op jit(solution)/shard_map/all_to_all | solution.py:307
  72.1 18.9 %all-to-all-start.1 = ((f32[256,1,128]{2,1,0:T(1,128)}), f32[256,1,128]{2,1,0:T(1,128)S(1)}, u32[]{:S(2)}, u32[]{:S(2)}) async-start(f32[256,1,128]{2,1,0:T(1,128)} %bitcast.34), calls=%async_computation.1 | async-start | bytes 262144 | tf_op jit(solution)/shard_map/all_to_all | solution.py:307
  104.1 2.5 %collective-permute-start.9 = (bf16[24,64,128]{2,1,0:T(8,128)(2,1)}, bf16[24,64,128]{2,1,0:T(8,128)(2,1)S(1)}, u32[]{:S(2)}, u32[]{:S(2)}) collective-permute-start(bf16[24,64,128]{2,1,0:T(8,128)(2,1)} %get-tuple-element.14), channel_id=1, source_target_pairs={{0,1},{1,0},{2,3},{3,2},{4,5},{5,4},{6,7},{7,6},{8,9},{9,8},{10,11... | collective-permute-start | bytes 1179656 | tf_op jit(solution)/shard_map/ppermute | solution.py:251
  106.6 2.3 %collective-permute-start.10 = (bf16[40,64,128]{2,1,0:T(8,128)(2,1)}, bf16[40,64,128]{2,1,0:T(8,128)(2,1)S(1)}, u32[]{:S(2)}, u32[]{:S(2)}) collective-permute-start(bf16[40,64,128]{2,1,0:T(8,128)(2,1)} %get-tuple-element.15), channel_id=1, source_target_pairs={{0,1},{1,0},{2,3},{3,2},{4,5},{5,4},{6,7},{7,6},{8,9},{9,8},{10,11... | collective-permute-start | bytes 1966088 | tf_op jit(solution)/shard_map/ppermute | solution.py:251
  108.2 12.1 %copy-start.14 = (pred[16]{0:T(512)(128)(4,1)S(1)}, pred[16]{0:T(512)(128)(4,1)}, u32[]{:S(2)}) copy-start(pred[16]{0:T(512)(128)(4,1)} %constant.200.clone.1) | copy-start | bytes 52
  108.2 12.1 %collective-permute-start.11 = (bf16[24,64,128]{2,1,0:T(8,128)(2,1)S(1)}, bf16[24,64,128]{2,1,0:T(8,128)(2,1)S(1)}, u32[]{:S(2)}, u32[]{:S(2)}) collective-permute-start(bf16[24,64,128]{2,1,0:T(8,128)(2,1)S(1)} %add_convert_fusion), channel_id=1, source_target_pairs={{0,4},{1,13},{2,6},{3,15},{4,8},{5,1},{6,10},{7,3},{8,12},{9,5},{1... | collective-permute-start | bytes 1179656 | tf_op jit(solution)/shard_map/ppermute | solution.py:255
  120.5 8.5 %collective-permute-start.12 = (bf16[16,64,128]{2,1,0:T(8,128)(2,1)S(1)}, bf16[16,64,128]{2,1,0:T(8,128)(2,1)S(1)}, u32[]{:S(2)}, u32[]{:S(2)}) collective-permute-start(bf16[16,64,128]{2,1,0:T(8,128)(2,1)S(1)} %get-tuple-element.16), channel_id=1, source_target_pairs={{0,4},{1,13},{2,6},{3,15},{4,8},{5,1},{6,10},{7,3},{8,12},{9,5},{1... | collective-permute-start | bytes 786440 | tf_op jit(solution)/shard_map/ppermute | solution.py:255
  121.7 12.0 %collective-permute-start.13 = (bf16[16,64,128]{2,1,0:T(8,128)(2,1)S(1)}, bf16[16,64,128]{2,1,0:T(8,128)(2,1)S(1)}, u32[]{:S(2)}, u32[]{:S(2)}) collective-permute-start(bf16[16,64,128]{2,1,0:T(8,128)(2,1)S(1)} %get-tuple-element.17), channel_id=1, source_target_pairs={{0,2},{1,15},{2,4},{3,1},{4,6},{5,3},{6,8},{7,5},{8,10},{9,7},{10,... | collective-permute-start | bytes 786440 | tf_op jit(solution)/shard_map/ppermute | solution.py:255
  129.0 7.6 %collective-permute-start.14 = (bf16[8,64,128]{2,1,0:T(8,128)(2,1)S(1)}, bf16[8,64,128]{2,1,0:T(8,128)(2,1)S(1)}, u32[]{:S(2)}, u32[]{:S(2)}) collective-permute-start(bf16[8,64,128]{2,1,0:T(8,128)(2,1)S(1)} %slice.73), channel_id=1, source_target_pairs={{0,1},{1,0},{2,3},{3,2},{4,5},{5,4},{6,7},{7,6},{8,9},{9,8},{10,11... | collective-permute-start | bytes 393224 | tf_op jit(solution)/shard_map/ppermute | solution.py:251
  133.8 3.8 %collective-permute-start.15 = (bf16[8,64,128]{2,1,0:T(8,128)(2,1)S(1)}, bf16[8,64,128]{2,1,0:T(8,128)(2,1)S(1)}, u32[]{:S(2)}, u32[]{:S(2)}) collective-permute-start(bf16[8,64,128]{2,1,0:T(8,128)(2,1)S(1)} %slice.74), channel_id=1, source_target_pairs={{0,1},{1,0},{2,3},{3,2},{4,5},{5,4},{6,7},{7,6},{8,9},{9,8},{10,11... | collective-permute-start | bytes 393224 | tf_op jit(solution)/shard_map/ppermute | solution.py:251
  (9 other events, 23.7 us)

commit v3 on v2

--- a/solution.py
+++ b/solution.py
@@ -15,7 +15,7 @@
 F32 = jnp.float32
 BF16 = jnp.bfloat16
 HIGHEST = lax.Precision.HIGHEST
-VMEM_LIMIT = 56 * 1024 * 1024
+VMEM_LIMIT = 32 * 1024 * 1024
 
 
 def cas_table(count):
@@ -36,40 +36,29 @@
     return jnp.concatenate(parts, axis=0)
 
 
-def orbital_copies(orb_hbm, orb_ref, sems, chunk):
-    return [
-        pltpu.make_async_copy(orb_hbm.at[pl.ds(i * chunk, chunk)], orb_ref.at[pl.ds(i * chunk, chunk)], sems.at[i])
-        for i in range(orb_ref.shape[0] // chunk)
-    ]
-
-
-def density_kernel(index_ref, live_ref, base_ref, orb_hbm, *refs, chunk):
-    pieces, (cas_ref, dens_ref, spec_ref, orb_ref, table_ref, orb_sems, table_sems) = refs[:-7], refs[-7:]
+def density_kernel(index_ref, live_ref, part_ref, base_ref, orb_hbm, *refs, chunk):
+    pieces, (cas_ref, dens_ref, spec_ref, table_ref, orb_ref, sems) = refs[:-6], refs[-6:]
     packed_rows = table_ref.shape[0] // 2
-    copies = []
+
+    def fetch(i):
+        rows = pl.ds(i * chunk, chunk)
+        return pltpu.make_async_copy(orb_hbm.at[rows], orb_ref.at[rows], sems.at[i])
+
+    for i in range(orb_ref.shape[0] // chunk):
+        fetch(i).start()
+    at = 0
     for piece in pieces:
         for first in range(0, piece.shape[0], 8):
-            i = len(copies)
-            rows = table_ref.at[pl.ds(base_ref[i], 8)]
-            copies.append(pltpu.make_async_copy(piece.at[pl.ds(first, 8)], rows, table_sems.at[i]))
-    for copy in copies:
-        copy.start()
-    for copy in orbital_copies(orb_hbm, orb_ref, orb_sems, chunk):
-        copy.start()
-    for copy in copies:
-        copy.wait()
-
-    def fill(i, carry):
-        both = table_ref[pl.ds(i * 8, 8)]
-        table_ref[pl.ds(packed_rows + i * 8, 8)] = pltpu.roll(both, 64, 2)
-        return carry
-
-    lax.fori_loop(0, packed_rows // 8, fill, 0)
+            base = base_ref[part_ref[2], at]
+            at += 1
+            both = piece[first : first + 8]
+            table_ref[pl.ds(base, 8)] = both
+            table_ref[pl.ds(packed_rows + base, 8)] = pltpu.roll(both, 64, 2)
     left_lanes = lax.broadcasted_iota(jnp.int32, (64, LANES), 1) < 64
 
     def body(i, carry):
         first = i * chunk
-        pltpu.make_async_copy(orb_hbm.at[pl.ds(first, chunk)], orb_ref.at[pl.ds(first, chunk)], orb_sems.at[i]).wait()
+        fetch(i).wait()
         rows_out = []
         for l in range(chunk):
             line = first + l
@@ -133,28 +122,22 @@
 def hamiltonian_kernel(
     pair_ref,
     live_ref,
+    part_ref,
     base_ref,
-    orb_hbm,
+    orb_ref,
     dens_ref,
     back_ref,
     cas_ref,
     pot_ref,
-    keep_hbm,
-    first_hbm,
-    rest_hbm,
-    orb_ref,
+    keep_ref,
+    first_ref,
+    rest_ref,
     left_ref,
     right_ref,
-    keep_ref,
-    give_ref,
-    orb_sems,
-    out_sems,
     *,
     chunk,
 ):
     lines = dens_ref.shape[0]
-    for copy in orbital_copies(orb_hbm, orb_ref, orb_sems, chunk):
-        copy.start()
 
     def clear(i, carry):
         left_ref[pl.ds(i * 8, 8)] = jnp.zeros((8, 64, LANES), F32)
@@ -170,7 +153,6 @@
 
     def body(i, carry):
         first = i * chunk
-        pltpu.make_async_copy(orb_hbm.at[pl.ds(first, chunk)], orb_ref.at[pl.ds(first, chunk)], orb_sems.at[i]).wait()
         potential = pot_ref[pl.ds(pl.multiple_of(first, 8), chunk), :]
         for l in range(chunk):
             line = first + l
@@ -193,20 +175,21 @@
         crossed = jnp.where(left_lanes, left_ref[high], right_ref[low])
         return jnp.where(left_lanes, left_ref[low], right_ref[high]) + pltpu.roll(crossed, 64, 2)
 
-    kept = keep_ref.shape[0] // 8
-    given = give_ref.shape[0] // 8
-    copies = []
-    for i in range(given):
-        give_ref[i * 8 : i * 8 + 8] = emit(base_ref[kept + i]).astype(BF16)
-        target = first_hbm.at[pl.ds(i * 8, 8)] if i < 3 else rest_hbm.at[pl.ds(i * 8 - 24, 8)]
-        copies.append(pltpu.make_async_copy(give_ref.at[pl.ds(i * 8, 8)], target, out_sems.at[kept + i]))
-        copies[-1].start()
-    for i in range(kept):
-        keep_ref[i * 8 : i * 8 + 8] = emit(base_ref[i])
-        copies.append(pltpu.make_async_copy(keep_ref.at[pl.ds(i * 8, 8)], keep_hbm.at[pl.ds(i * 8, 8)], out_sems.at[i]))
-        copies[-1].start()
-    for copy in copies:
-        copy.wait()
+    at = 0
+    for out in (keep_ref, first_ref, rest_ref):
+        for first in range(0, out.shape[0], 8):
+            out[first : first + 8] = emit(base_ref[part_ref[2], at]).astype(out.dtype)
+            at += 1
+
+
+def finish_kernel(keep_ref, got_ref, one_ref, two_ref, twin_one_ref, twin_two_ref, out_ref):
+    rows = out_ref.shape[0] // 2
+    for i in range(rows):
+        total = keep_ref[keep_ref.shape[0] - rows + i] + got_ref[got_ref.shape[0] - rows + i].astype(F32)
+        total = total + one_ref[i].astype(F32) + two_ref[i].astype(F32)
+        total = total + twin_one_ref[i].astype(F32) + twin_two_ref[i].astype(F32)
+        out_ref[i] = total[:, :64]
+        out_ref[rows + i] = total[:, 64:]
 
 
 def per_device(orbitals, live_atoms, pair_index, density_blocks):
@@ -243,8 +226,8 @@
     chips = heights // 2
     far = chips // 2
     height = lax.axis_index("height")
-    chip, core = height // 2, height % 2
-    turn = 1 - 2 * core
+    device = lax.axis_index("col") * heights + height
+    part = jnp.stack([device % copies, device // copies, height]).astype(jnp.int32)
     twin = [(h, h ^ 1) for h in range(heights)]
 
     def across(values):
@@ -254,61 +237,64 @@
         shift = 2 * hops
         return lax.ppermute(values, "height", [(h, (h + shift * (1 - 2 * (h % 2))) % heights) for h in range(heights)])
 
-    def place_of(distance, owner):
-        return ((chip + distance) % chips) * 2 + owner
-
+    gather_rows, keep_rows, give_rows = [], [], []
+    for h in range(heights):
+        core, turn = h % 2, 1 - 2 * (h % 2)
+
+        def place_of(distance, owner):
+            return ((h // 2 + distance) % chips) * 2 + owner
+
+        places = [place_of(0, core), place_of(0, 1 - core)]
+        for d in (2, 1, 3, far):
+            count = 2 if d < far else 1
+            places += [place_of(-turn * d, core), place_of(-turn * d, 1 - core)][:count]
+            places += [place_of(turn * d, 1 - core), place_of(turn * d, core)][:count]
+        gather_rows.append(places)
+        keep, give = [], []
+        for d in (far, 3, 1, 2, 0):
+            count = 2 if 0 < d < far else 1
+            keep += [place_of(turn * d, core), place_of(turn * d, 1 - core)][:count]
+            give += [place_of(-turn * d, 1 - core), place_of(-turn * d, core)][:count]
+        keep_rows.append(keep)
+        give_rows.append(give)
+    half = share // 2
+    table_rows = np.array(gather_rows, np.int32) * half
+    sum_rows = np.concatenate([np.array(keep_rows, np.int32), np.array(give_rows, np.int32)], axis=1) * share
+
+    side = jnp.arange(lines * 16, dtype=jnp.int32) % 2
+    table_index = (pairs // share) * half + pairs % half
+    table_index = table_index + jnp.where((pairs // half) % 2 == side, 0, block_rows)
     whole_chip = jnp.concatenate([packed, across(packed)], axis=0)
+    second = onward(whole_chip, 2)
     near = onward(whole_chip, 1)
-    second = onward(whole_chip, 2)
-    arrived = [near, second, onward(near, 2), onward(second[: share // 2], 2)]
+    near, table_index, live, part, pairs = lax.optimization_barrier((near, table_index, live, part, pairs))
     pieces = [whole_chip]
-    heights_of = [place_of(0, core), place_of(0, 1 - core)]
-    for d, piece in enumerate(arrived, 1):
+    for piece in (second, near, onward(second, 1), onward(second[:half], 2)):
         pieces += [piece, across(piece)]
-        count = 2 if d < far else 1
-        heights_of += [place_of(-turn * d, core), place_of(-turn * d, 1 - core)][:count]
-        heights_of += [place_of(turn * d, 1 - core), place_of(turn * d, core)][:count]
-    table_rows = (jnp.stack(heights_of) * (share // 2)).astype(jnp.int32)
-    keep_of, give_of = [], []
-    for d in range(far, -1, -1):
-        keep_of.append(place_of(turn * d, core))
-        give_of.append(place_of(-turn * d, 1 - core))
-        if 0 < d < far:
-            keep_of.append(place_of(turn * d, 1 - core))
-            give_of.append(place_of(-turn * d, core))
-    sum_rows = (jnp.stack(keep_of + give_of) * share).astype(jnp.int32)
-
-    side = jnp.arange(lines * 16, dtype=jnp.int32) % 2
-    table_index = (pairs // share) * (share // 2) + pairs % (share // 2)
-    table_index = table_index + jnp.where((pairs // (share // 2)) % 2 == side, 0, block_rows)
     smem = pl.BlockSpec(memory_space=pltpu.SMEM)
     vmem = pl.BlockSpec(memory_space=pltpu.VMEM)
-    hbm = pl.BlockSpec(memory_space=pl.ANY)
     params = pltpu.CompilerParams(vmem_limit_bytes=VMEM_LIMIT)
     density, spectrum = pl.pallas_call(
         functools.partial(density_kernel, chunk=chunk),
-        in_specs=[smem, smem, smem, hbm] + [hbm] * len(pieces) + [vmem],
+        in_specs=[smem] * 4 + [pl.BlockSpec(memory_space=pl.ANY)] + [vmem] * (len(pieces) + 1),
         out_specs=[vmem, vmem],
         out_shape=[
             jax.ShapeDtypeStruct((lines, line_cells), F32),
             jax.ShapeDtypeStruct((devices, LANES), F32),
         ],
         scratch_shapes=[
+            pltpu.VMEM((2 * block_rows, 64, LANES), BF16),
             pltpu.VMEM((lines, width, line_cells), BF16),
-            pltpu.VMEM((2 * block_rows, 64, LANES), BF16),
             pltpu.SemaphoreType.DMA((lines // chunk,)),
-            pltpu.SemaphoreType.DMA((heights,)),
         ],
         compiler_params=params,
         name="density",
-    )(table_index, live, table_rows, orb, *pieces, jnp.asarray(cas_y2))
+    )(table_index, live, part, jnp.asarray(table_rows), orb, *pieces, jnp.asarray(cas_y2))
 
     def exchange(values):
         out = lax.all_to_all(values.reshape(devices, 1, LANES), ("col", "height"), split_axis=0, concat_axis=0, tiled=True)
         return out.reshape(devices, LANES)
 
-    device = lax.axis_index("col") * heights + height
-    part = jnp.stack([device % copies, device // copies]).astype(jnp.int32)
     solved = pl.pallas_call(
         lambda *refs: solve_kernel(*refs, cells_x=cells_x, cells_z=cells_z, cols=cols, heights=heights),
         in_specs=[smem, vmem, vmem, vmem, vmem, vmem, vmem, smem],
@@ -331,38 +317,36 @@
     half_rows = block_rows // 2
     potential, keep, give_first, give_rest = pl.pallas_call(
         functools.partial(hamiltonian_kernel, chunk=chunk),
-        in_specs=[smem, smem, smem, hbm, vmem, vmem, vmem],
-        out_specs=[vmem, hbm, hbm, hbm],
+        in_specs=[smem] * 4 + [vmem] * 4,
+        out_specs=[vmem] * 4,
         out_shape=[
             jax.ShapeDtypeStruct((lines, line_cells), F32),
             jax.ShapeDtypeStruct((half_rows, 64, LANES), F32),
             jax.ShapeDtypeStruct((3 * share // 2, 64, LANES), BF16),
             jax.ShapeDtypeStruct((half_rows - 3 * share // 2, 64, LANES), BF16),
         ],
-        scratch_shapes=[
-            pltpu.VMEM((lines, width, line_cells), BF16),
-            pltpu.VMEM((2 * block_rows, 64, LANES), F32),
-            pltpu.VMEM((2 * block_rows, 64, LANES), F32),
-            pltpu.VMEM((half_rows, 64, LANES), F32),
-            pltpu.VMEM((half_rows, 64, LANES), BF16),
-            pltpu.SemaphoreType.DMA((lines // chunk,)),
-            pltpu.SemaphoreType.DMA((heights,)),
-        ],
+        scratch_shapes=[pltpu.VMEM((2 * block_rows, 64, LANES), F32)] * 2,
         compiler_params=params,
         name="hamiltonian",
-    )(pairs, live, sum_rows, orb, density, returned, jnp.asarray(cas_y2.T.copy()))
-
-    half = share // 2
+    )(pairs, live, part, jnp.asarray(sum_rows), orb, density, returned, jnp.asarray(cas_y2.T.copy()))
+
     got_first = across(give_first)
     got_rest = across(lax.optimization_barrier((give_rest, got_first))[0])
-    inner = onward((keep[: 3 * half] + got_first.astype(F32)).astype(BF16), 2)
+    begin = (keep[: 3 * half] + got_first.astype(F32)).astype(BF16)
+    from_far = onward(begin[:half], 2).astype(F32)
+    from_third = onward(begin[half:], 1).astype(F32)
     local = keep[3 * half :] + got_rest.astype(F32)
-    from_far = jnp.concatenate([inner[:half].astype(F32), jnp.zeros((half, 64, LANES), F32)], axis=0)
-    by_two = onward((local[: 2 * half] + from_far).astype(BF16), 2)
-    by_one = onward((local[2 * half : 4 * half] + inner[half:].astype(F32)).astype(BF16), 1)
-    summed = local[4 * half :] + by_two[:half].astype(F32) + by_one[:half].astype(F32)
-    summed = summed + across(by_two[half:]).astype(F32) + across(by_one[half:]).astype(F32)
-    hamiltonian = jnp.concatenate([summed[:, :, :64], summed[:, :, 64:]], axis=0)
+    by_one = onward(local[: 2 * half].astype(BF16), 1)
+    from_far = jnp.concatenate([from_far, jnp.zeros_like(from_far)], axis=0)
+    by_two = onward((local[2 * half : 4 * half] + from_third + from_far).astype(BF16), 2)
+    hamiltonian = pl.pallas_call(
+        finish_kernel,
+        in_specs=[vmem] * 6,
+        out_specs=vmem,
+        out_shape=jax.ShapeDtypeStruct(density_blocks.shape, F32),
+        compiler_params=params,
+        name="finish",
+    )(keep, got_rest, by_one, by_two, across(by_one[half:]), across(by_two[half:]))
     return potential.reshape(cells_x, cells_z, line_cells), hamiltonian
 
 

time: 139 us -> 123 us (0.88)
  blocking collectives: 0 us -> 44 us
  waiting for transfers between devices: 56.3 us -> 24.8 us
  starting transfers between devices: 42.7 us -> 26.9 us
  Pallas kernels: 27.6 us -> 20.8 us
  other arithmetic: 6.36 us -> 0.72 us
    all_to_all x0 -> x2, blocking collectives: none -> 44 us  [exchange(): lax.all_to_all(values.reshape(devices, 1, LANES), ('col', 'height'), spli...]
    all_to_all x2 -> x0, waiting for transfers between devices: 24.6 us -> none  [exchange(): lax.all_to_all(values.reshape(devices, 1, LANES), ('col', 'height'), spli...]
    all_to_all x2 -> x0, starting transfers between devices: 16.6 us -> none  [exchange(): lax.all_to_all(values.reshape(devices, 1, LANES), ('col', 'height'), spli...]
    ppermute x7 -> x8, waiting for transfers between devices: 27 us -> 19.4 us  [onward(): lax.ppermute(values, 'height', [(h, (h + shift * (1 - 2 * (h % 2))) % hei...]
    pallas_call x1, Pallas kernels: 12.1 us -> 7.27 us  [per_device(): pl.pallas_call(functools.partial(density_kernel, chunk=chunk), in_specs=[...]
    ppermute x7 -> x8, starting transfers between devices: 8.66 us -> 11.5 us  [onward(): lax.ppermute(values, 'height', [(h, (h + shift * (1 - 2 * (h % 2))) % hei...]
    ppermute x9, starting transfers between devices: 17.4 us -> 15.5 us  [across(): return lax.ppermute(values, 'height', twin)]
    pallas_call x1, Pallas kernels: 12.4 us -> 10.7 us  [per_device(): pl.pallas_call(functools.partial(hamiltonian_kernel, chunk=chunk), in_spe...]
  transfers between devices with their start and end apart: 18 -> 17, of which waited for: 12 -> 12; matrix products, arithmetic and copies ran while one was open for 5% -> 1% of each run, Pallas kernels for 0% -> 0%
where the time goes in v3:
time: 123 us
  blocking collectives  44 us (36%)
  starting transfers between devices  26.9 us (22%)
  waiting for transfers between devices  24.8 us (20%)
  Pallas kernels  20.8 us (17%)
  local copies, waits for them, and re-layouts  4.72 us (4%)
    all_to_all x2, blocking collectives, exchange(): lax.all_to_all(values.reshape(devices, 1, LANES), ('col', 'height'), spli...  44 us
    ppermute x8, waiting for transfers between devices, onward(): lax.ppermute(values, 'height', [(h, (h + shift * (1 - 2 * (h % 2))) % hei...  19.4 us
    ppermute x9, starting transfers between devices, across(): return lax.ppermute(values, 'height', twin)  15.5 us
    ppermute x8, starting transfers between devices, onward(): lax.ppermute(values, 'height', [(h, (h + shift * (1 - 2 * (h % 2))) % hei...  11.5 us
    pallas_call x1, Pallas kernels, per_device(): pl.pallas_call(functools.partial(hamiltonian_kernel, chunk=chunk), in_spe...  10.7 us
    pallas_call x1, Pallas kernels, per_device(): pl.pallas_call(functools.partial(density_kernel, chunk=chunk), in_specs=[...  7.27 us
    ppermute x9, waiting for transfers between devices, across(): return lax.ppermute(values, 'height', twin)  5.47 us
    unnamed x30, local copies, waits for them, and re-layouts  3.28 us
  transfers between devices with their start and end apart: 17, of which 12 were waited for; matrix products, arithmetic and copies ran while one was open for 1% of the time, Pallas kernels for 0%

profile of v3, /device:TPU:1, one launch (start us, length us, event | category | flops | bytes accessed | tf_op | source)
XLA Modules:
  0.0 122.9 jit_solution(12039090926628719733)
XLA Ops:
  0.7 1.1 fusion.13
  1.8 3.3 %collective-permute-start = (bf16[8,64,128]{2,1,0:T(8,128)(2,1)S(1)}, bf16[8,64,128]{2,1,0:T(8,128)(2,1)S(1)}, u32[]{:S(2)}, u32[]{:S(2)}) collective-permute-start(bf16[8,64,128]{2,1,0:T(8,128)(2,1)S(1)} %pad_maximum_fusion.1), channel_id=1, source_target_pairs={{0,1},{1,0},{2,3},{3,2},{4,5},{5,4},{6,7},{7,6},{8,9},{9,8},{10,11... | collective-permute-start | bytes 393224 | tf_op jit(solution)/shard_map/ppermute | solution.py:234
  5.2 1.0 collective-permute-done
  6.3 4.4 %collective-permute-start.2 = (bf16[16,64,128]{2,1,0:T(8,128)(2,1)S(1)}, bf16[16,64,128]{2,1,0:T(8,128)(2,1)S(1)}, u32[]{:S(2)}, u32[]{:S(2)}) collective-permute-start(bf16[16,64,128]{2,1,0:T(8,128)(2,1)S(1)} %pad_maximum_fusion.refs_0_), channel_id=1, source_target_pairs={{0,4},{1,13},{2,6},{3,15},{4,8},{5,1},{6,10},{7,3},{8,12},{9,5},{1... | collective-permute-start | bytes 786440 | tf_op jit(solution)/shard_map/ppermute | solution.py:238
  11.4 4.2 %collective-permute-done.2.refs_1_ = bf16[16,64,128]{2,1,0:T(8,128)(2,1)S(1)} collective-permute-done((bf16[16,64,128]{2,1,0:T(8,128)(2,1)S(1)}, bf16[16,64,128]{2,1,0:T(8,128)(2,1)S(1)}, u32[]{:S(2)}, u32[]{:S(2)}) %collective-permute-start.2) | collective-permute-done | bytes 262176 | tf_op jit(solution)/shard_map/ppermute | solution.py:238
  15.6 4.5 %collective-permute-start.5 = (bf16[16,64,128]{2,1,0:T(8,128)(2,1)S(1)}, bf16[16,64,128]{2,1,0:T(8,128)(2,1)S(1)}, u32[]{:S(2)}, u32[]{:S(2)}) collective-permute-start(bf16[16,64,128]{2,1,0:T(8,128)(2,1)S(1)} %collective-permute-done.2.refs_1_), channel_id=1, source_target_pairs={{0,2},{1,15},{2,4},{3,1},{4,6},{5,3},{6,8},{7,5},{8,10},{9,7},{10,... | collective-permute-start | bytes 786440 | tf_op jit(solution)/shard_map/ppermute | solution.py:238
  22.1 2.5 %collective-permute-done.5.refs_5_ = bf16[16,64,128]{2,1,0:T(8,128)(2,1)S(1)} collective-permute-done((bf16[16,64,128]{2,1,0:T(8,128)(2,1)S(1)}, bf16[16,64,128]{2,1,0:T(8,128)(2,1)S(1)}, u32[]{:S(2)}, u32[]{:S(2)}) %collective-permute-start.5) | collective-permute-done | bytes 262176 | tf_op jit(solution)/shard_map/ppermute | solution.py:238
  25.0 1.9 %collective-permute-done.7.refs_7_ = bf16[8,64,128]{2,1,0:T(8,128)(2,1)S(1)} collective-permute-done((bf16[8,64,128]{2,1,0:T(8,128)(2,1)S(1)}, bf16[8,64,128]{2,1,0:T(8,128)(2,1)S(1)}, u32[]{:S(2)}, u32[]{:S(2)}) %collective-permute-start.7) | collective-permute-done | bytes 131104 | tf_op jit(solution)/shard_map/ppermute | solution.py:238
  26.9 1.5 %collective-permute-start.8 = (bf16[8,64,128]{2,1,0:T(8,128)(2,1)S(1)}, bf16[8,64,128]{2,1,0:T(8,128)(2,1)S(1)}, u32[]{:S(2)}, u32[]{:S(2)}) collective-permute-start(bf16[8,64,128]{2,1,0:T(8,128)(2,1)S(1)} %collective-permute-done.7.refs_7_), channel_id=1, source_target_pairs={{0,1},{1,0},{2,3},{3,2},{4,5},{5,4},{6,7},{7,6},{8,9},{9,8},{10,11... | collective-permute-start | bytes 393224 | tf_op jit(solution)/shard_map/ppermute | solution.py:234
  28.5 1.0 collective-permute-done.8.refs_8_
  29.5 2.8 %copy-done = bf16[12,8,256,128]{3,2,1,0:T(8,128)(2,1)S(1)} copy-done((bf16[12,8,256,128]{3,2,1,0:T(8,128)(2,1)S(1)}, bf16[12,8,256,128]{3,2,1,0:T(8,128)(2,1)}, u32[]{:S(2)}) %copy-start) | copy-done | bytes 6291480
  32.3 7.3 %density.1 = (f32[96,128]{1,0:T(8,128)S(1)}, f32[256,128]{1,0:T(8,128)S(1)}) custom-call(s32[1536]{0:T(1024)S(1)} %fusion.5.index_ref, s32[96]{0:T(128)S(1)} %reshape.29.live_ref, s32[3]{0:T(128)S(1)} %pad_add_fusion.part_ref.refs_0_, s32[16,16]{1,0:T(8,128)S(1)} %copy-done.9, bf16[96,256,128]{2,1,0:T(8,128)(2,1)S(1)} %bitcast.13, ...), custom_call_target="tpu_custom_call" | custom-call | tf_op jit(solution)/shard_map/density/pallas_call | solution.py:277
  39.6 25.4 %all_to_all.10 = f32[256,1,128]{2,1,0:T(1,128)S(1)} all-to-all(f32[256,1,128]{2,1,0:T(1,128)S(1)} %bitcast.18), channel_id=1, replica_groups=mesh['col'=16,'height'=16] {'col','height'}, dimensions={0} | all-to-all | bytes 262144 | tf_op jit(solution)/shard_map/all_to_all | solution.py:295
  65.1 1.8 %solve.1 = f32[256,128]{1,0:T(8,128)S(1)} custom-call(s32[3]{0:T(128)S(1)} %pad_add_fusion.part_ref.refs_0_, f32[256,128]{1,0:T(8,128)S(1)} %bitcast.16, f32[2,96,192]{2,1,0:T(8,128)S(1)} %copy-done.3, f32[2,192,96]{2,1,0:T(8,128)S(1)} %copy-done.2, f32[128,128]{1,0:T(8,128)S(1)} %copy-done.7, f32[2,96,128]{2,1,0:T(8,128)S(1)} %copy-done.6, ...), custom_call_target="tpu_custom_call" | custom-call | tf_op jit(solution)/shard_map/solve/pallas_call | solution.py:298
  66.9 18.6 %all_to_all.11 = f32[256,1,128]{2,1,0:T(1,128)S(1)} all-to-all(f32[256,1,128]{2,1,0:T(1,128)S(1)} %bitcast.17), channel_id=1, replica_groups=mesh['col'=16,'height'=16] {'col','height'}, dimensions={0} | all-to-all | bytes 262144 | tf_op jit(solution)/shard_map/all_to_all | solution.py:295
  85.5 10.7 %hamiltonian.1 = (f32[96,128]{1,0:T(8,128)}, f32[64,64,128]{2,1,0:T(8,128)S(1)}, bf16[24,64,128]{2,1,0:T(8,128)(2,1)S(1)}, bf16[40,64,128]{2,1,0:T(8,128)(2,1)S(1)}) custom-call(s32[1536]{0:T(1024)S(1)} %reshape.28.pair_ref, s32[96]{0:T(128)S(1)} %reshape.29.live_ref, s32[3]{0:T(128)S(1)} %pad_add_fusion.part_ref.refs_0_, s32[16,16]{1,0:T(8,128)S(1)} %copy-done.8, ...), custom_call_target="tpu_custom_call" | custom-call | tf_op jit(solution)/shard_map/hamiltonian/pallas_call | solution.py:318
  97.2 1.3 %collective-permute-done.9 = bf16[24,64,128]{2,1,0:T(8,128)(2,1)S(1)} collective-permute-done((bf16[24,64,128]{2,1,0:T(8,128)(2,1)S(1)}, bf16[24,64,128]{2,1,0:T(8,128)(2,1)S(1)}, u32[]{:S(2)}, u32[]{:S(2)}) %collective-permute-start.9) | collective-permute-done | bytes 393248 | tf_op jit(solution)/shard_map/ppermute | solution.py:234
  99.4 1.2 collective-permute-done.10.got_ref
  100.9 4.6 %collective-permute-done.13 = bf16[8,64,128]{2,1,0:T(8,128)(2,1)S(1)} collective-permute-done((bf16[8,64,128]{2,1,0:T(8,128)(2,1)S(1)}, bf16[8,64,128]{2,1,0:T(8,128)(2,1)S(1)}, u32[]{:S(2)}, u32[]{:S(2)}) %collective-permute-start.13) | collective-permute-done | bytes 131104 | tf_op jit(solution)/shard_map/ppermute | solution.py:238
  105.5 1.3 %collective-permute-done.12 = bf16[16,64,128]{2,1,0:T(8,128)(2,1)S(1)} collective-permute-done((bf16[16,64,128]{2,1,0:T(8,128)(2,1)S(1)}, bf16[16,64,128]{2,1,0:T(8,128)(2,1)S(1)}, u32[]{:S(2)}, u32[]{:S(2)}) %collective-permute-start.12) | collective-permute-done | bytes 262176 | tf_op jit(solution)/shard_map/ppermute | solution.py:238
  107.7 2.1 %collective-permute-done.11.one_ref = bf16[16,64,128]{2,1,0:T(8,128)(2,1)S(1)} collective-permute-done((bf16[16,64,128]{2,1,0:T(8,128)(2,1)S(1)}, bf16[16,64,128]{2,1,0:T(8,128)(2,1)S(1)}, u32[]{:S(2)}, u32[]{:S(2)}) %collective-permute-start.11) | collective-permute-done | bytes 262176 | tf_op jit(solution)/shard_map/ppermute | solution.py:238
  109.9 3.3 %collective-permute-start.15 = (bf16[8,64,128]{2,1,0:T(8,128)(2,1)S(1)}, bf16[8,64,128]{2,1,0:T(8,128)(2,1)S(1)}, u32[]{:S(2)}, u32[]{:S(2)}) collective-permute-start(bf16[8,64,128]{2,1,0:T(8,128)(2,1)S(1)} %slice.50), channel_id=1, source_target_pairs={{0,1},{1,0},{2,3},{3,2},{4,5},{5,4},{6,7},{7,6},{8,9},{9,8},{10,11... | collective-permute-start | bytes 393224 | tf_op jit(solution)/shard_map/ppermute | solution.py:234
  113.2 2.7 %collective-permute-done.14.two_ref = bf16[16,64,128]{2,1,0:T(8,128)(2,1)S(1)} collective-permute-done((bf16[16,64,128]{2,1,0:T(8,128)(2,1)S(1)}, bf16[16,64,128]{2,1,0:T(8,128)(2,1)S(1)}, u32[]{:S(2)}, u32[]{:S(2)}) %collective-permute-start.14) | collective-permute-done | bytes 262176 | tf_op jit(solution)/shard_map/ppermute | solution.py:238
  115.9 5.1 %collective-permute-start.16 = (bf16[8,64,128]{2,1,0:T(8,128)(2,1)S(1)}, bf16[8,64,128]{2,1,0:T(8,128)(2,1)S(1)}, u32[]{:S(2)}, u32[]{:S(2)}) collective-permute-start(bf16[8,64,128]{2,1,0:T(8,128)(2,1)S(1)} %slice.51), channel_id=1, source_target_pairs={{0,1},{1,0},{2,3},{3,2},{4,5},{5,4},{6,7},{7,6},{8,9},{9,8},{10,11... | collective-permute-start | bytes 393224 | tf_op jit(solution)/shard_map/ppermute | solution.py:234
  (62 shorter events, 8.4 us)
Async XLA Ops:
  1.8 4.3 %collective-permute-start = (bf16[8,64,128]{2,1,0:T(8,128)(2,1)S(1)}, bf16[8,64,128]{2,1,0:T(8,128)(2,1)S(1)}, u32[]{:S(2)}, u32[]{:S(2)}) collective-permute-start(bf16[8,64,128]{2,1,0:T(8,128)(2,1)S(1)} %pad_maximum_fusion.1), channel_id=1, source_target_pairs={{0,1},{1,0},{2,3},{3,2},{4,5},{5,4},{6,7},{7,6},{8,9},{9,8},{10,11... | collective-permute-start | bytes 393224 | tf_op jit(solution)/shard_map/ppermute | solution.py:234
  6.3 9.3 %collective-permute-start.2 = (bf16[16,64,128]{2,1,0:T(8,128)(2,1)S(1)}, bf16[16,64,128]{2,1,0:T(8,128)(2,1)S(1)}, u32[]{:S(2)}, u32[]{:S(2)}) collective-permute-start(bf16[16,64,128]{2,1,0:T(8,128)(2,1)S(1)} %pad_maximum_fusion.refs_0_), channel_id=1, source_target_pairs={{0,4},{1,13},{2,6},{3,15},{4,8},{5,1},{6,10},{7,3},{8,12},{9,5},{1... | collective-permute-start | bytes 786440 | tf_op jit(solution)/shard_map/ppermute | solution.py:238
  10.6 10.9 %collective-permute-start.1 = (bf16[16,64,128]{2,1,0:T(8,128)(2,1)S(1)}, bf16[16,64,128]{2,1,0:T(8,128)(2,1)S(1)}, u32[]{:S(2)}, u32[]{:S(2)}) collective-permute-start(bf16[16,64,128]{2,1,0:T(8,128)(2,1)S(1)} %pad_maximum_fusion.refs_0_), channel_id=1, source_target_pairs={{0,2},{1,15},{2,4},{3,1},{4,6},{5,3},{6,8},{7,5},{8,10},{9,7},{10,... | collective-permute-start | bytes 786440 | tf_op jit(solution)/shard_map/ppermute | solution.py:238
  15.6 9.0 %collective-permute-start.5 = (bf16[16,64,128]{2,1,0:T(8,128)(2,1)S(1)}, bf16[16,64,128]{2,1,0:T(8,128)(2,1)S(1)}, u32[]{:S(2)}, u32[]{:S(2)}) collective-permute-start(bf16[16,64,128]{2,1,0:T(8,128)(2,1)S(1)} %collective-permute-done.2.refs_1_), channel_id=1, source_target_pairs={{0,2},{1,15},{2,4},{3,1},{4,6},{5,3},{6,8},{7,5},{8,10},{9,7},{10,... | collective-permute-start | bytes 786440 | tf_op jit(solution)/shard_map/ppermute | solution.py:238
  21.0 6.0 %collective-permute-start.7 = (bf16[8,64,128]{2,1,0:T(8,128)(2,1)S(1)}, bf16[8,64,128]{2,1,0:T(8,128)(2,1)S(1)}, u32[]{:S(2)}, u32[]{:S(2)}) collective-permute-start(bf16[8,64,128]{2,1,0:T(8,128)(2,1)S(1)} %slice.45), channel_id=1, source_target_pairs={{0,4},{1,13},{2,6},{3,15},{4,8},{5,1},{6,10},{7,3},{8,12},{9,5},{1... | collective-permute-start | bytes 393224 | tf_op jit(solution)/shard_map/ppermute | solution.py:238
  21.6 7.9 %collective-permute-start.4 = (bf16[16,64,128]{2,1,0:T(8,128)(2,1)S(1)}, bf16[16,64,128]{2,1,0:T(8,128)(2,1)S(1)}, u32[]{:S(2)}, u32[]{:S(2)}) collective-permute-start(bf16[16,64,128]{2,1,0:T(8,128)(2,1)S(1)} %collective-permute-done.1.refs_3_), channel_id=1, source_target_pairs={{0,1},{1,0},{2,3},{3,2},{4,5},{5,4},{6,7},{7,6},{8,9},{9,8},{10,11... | collective-permute-start | bytes 786440 | tf_op jit(solution)/shard_map/ppermute | solution.py:234
  21.6 7.9 %collective-permute-start.3 = (bf16[16,64,128]{2,1,0:T(8,128)(2,1)S(1)}, bf16[16,64,128]{2,1,0:T(8,128)(2,1)S(1)}, u32[]{:S(2)}, u32[]{:S(2)}) collective-permute-start(bf16[16,64,128]{2,1,0:T(8,128)(2,1)S(1)} %collective-permute-done.2.refs_1_), channel_id=1, source_target_pairs={{0,1},{1,0},{2,3},{3,2},{4,5},{5,4},{6,7},{7,6},{8,9},{9,8},{10,11... | collective-permute-start | bytes 786440 | tf_op jit(solution)/shard_map/ppermute | solution.py:234
  24.6 4.9 %collective-permute-start.6 = (bf16[16,64,128]{2,1,0:T(8,128)(2,1)S(1)}, bf16[16,64,128]{2,1,0:T(8,128)(2,1)S(1)}, u32[]{:S(2)}, u32[]{:S(2)}) collective-permute-start(bf16[16,64,128]{2,1,0:T(8,128)(2,1)S(1)} %collective-permute-done.5.refs_5_), channel_id=1, source_target_pairs={{0,1},{1,0},{2,3},{3,2},{4,5},{5,4},{6,7},{7,6},{8,9},{9,8},{10,11... | collective-permute-start | bytes 786440 | tf_op jit(solution)/shard_map/ppermute | solution.py:234
  26.9 2.5 %collective-permute-start.8 = (bf16[8,64,128]{2,1,0:T(8,128)(2,1)S(1)}, bf16[8,64,128]{2,1,0:T(8,128)(2,1)S(1)}, u32[]{:S(2)}, u32[]{:S(2)}) collective-permute-start(bf16[8,64,128]{2,1,0:T(8,128)(2,1)S(1)} %collective-permute-done.7.refs_7_), channel_id=1, source_target_pairs={{0,1},{1,0},{2,3},{3,2},{4,5},{5,4},{6,7},{7,6},{8,9},{9,8},{10,11... | collective-permute-start | bytes 393224 | tf_op jit(solution)/shard_map/ppermute | solution.py:234
  32.3 32.8 %copy-start.6 = (f32[2,96,128]{2,1,0:T(8,128)S(1)}, f32[2,96,128]{2,1,0:T(8,128)}, u32[]{:S(2)}) copy-start(f32[2,96,128]{2,1,0:T(8,128)} %constant.111.clone.refs_5_) | copy-start | bytes 294916
  32.3 32.8 %copy-start.7 = (f32[128,128]{1,0:T(8,128)S(1)}, f32[128,128]{1,0:T(8,128)}, u32[]{:S(2)}) copy-start(f32[128,128]{1,0:T(8,128)} %constant.110.clone.refs_4_) | copy-start | bytes 196612
  32.3 32.8 %copy-start.10 = (f32[128]{0:T(128)S(1)}, f32[128]{0:T(128)}, u32[]{:S(2)}) copy-start(f32[128]{0:T(128)} %constant.113.clone.refs_7_) | copy-start | bytes 1540
  32.3 32.8 %copy-start.11 = (f32[1,128]{1,0:T(1,128)S(1)}, f32[1,128]{1,0:T(1,128)}, u32[]{:S(2)}) copy-start(f32[1,128]{1,0:T(1,128)} %constant.112.clone.refs_6_) | copy-start | bytes 1540
  32.3 53.2 %copy-start.1 = (bf16[12,8,256,128]{3,2,1,0:T(8,128)(2,1)S(1)}, bf16[12,8,256,128]{3,2,1,0:T(8,128)(2,1)}, u32[]{:S(2)}) copy-start(bf16[12,8,256,128]{3,2,1,0:T(8,128)(2,1)} %param.14) | copy-start | bytes 18874372
  39.6 45.9 %copy-start.5 = (f32[256,128]{1,0:T(8,128)S(1)}, f32[256,128]{1,0:T(8,128)}, u32[]{:S(2)}) copy-start(f32[256,128]{1,0:T(8,128)} %constant.115.clone.cas_ref) | copy-start | bytes 393220
  39.6 45.9 %copy-start.8 = (s32[16,16]{1,0:T(8,128)S(1)}, s32[16,16]{1,0:T(8,128)}, u32[]{:S(2)}) copy-start(s32[16,16]{1,0:T(8,128)} %constant.114.clone.base_ref) | copy-start | bytes 3076
  96.3 2.2 %collective-permute-start.9 = (bf16[24,64,128]{2,1,0:T(8,128)(2,1)S(1)}, bf16[24,64,128]{2,1,0:T(8,128)(2,1)S(1)}, u32[]{:S(2)}, u32[]{:S(2)}) collective-permute-start(bf16[24,64,128]{2,1,0:T(8,128)(2,1)S(1)} %get-tuple-element.24), channel_id=1, source_target_pairs={{0,1},{1,0},{2,3},{3,2},{4,5},{5,4},{6,7},{7,6},{8,9},{9,8},{10,11... | collective-permute-start | bytes 1179656 | tf_op jit(solution)/shard_map/ppermute | solution.py:234
  98.5 2.1 %collective-permute-start.10 = (bf16[40,64,128]{2,1,0:T(8,128)(2,1)S(1)}, bf16[40,64,128]{2,1,0:T(8,128)(2,1)S(1)}, u32[]{:S(2)}, u32[]{:S(2)}) collective-permute-start(bf16[40,64,128]{2,1,0:T(8,128)(2,1)S(1)} %get-tuple-element.25), channel_id=1, source_target_pairs={{0,1},{1,0},{2,3},{3,2},{4,5},{5,4},{6,7},{7,6},{8,9},{9,8},{10,11... | collective-permute-start | bytes 1966088 | tf_op jit(solution)/shard_map/ppermute | solution.py:234
  99.1 6.5 %collective-permute-start.13 = (bf16[8,64,128]{2,1,0:T(8,128)(2,1)S(1)}, bf16[8,64,128]{2,1,0:T(8,128)(2,1)S(1)}, u32[]{:S(2)}, u32[]{:S(2)}) collective-permute-start(bf16[8,64,128]{2,1,0:T(8,128)(2,1)S(1)} %slice.49), channel_id=1, source_target_pairs={{0,4},{1,13},{2,6},{3,15},{4,8},{5,1},{6,10},{7,3},{8,12},{9,5},{1... | collective-permute-start | bytes 393224 | tf_op jit(solution)/shard_map/ppermute | solution.py:238
  99.3 7.5 %collective-permute-start.12 = (bf16[16,64,128]{2,1,0:T(8,128)(2,1)S(1)}, bf16[16,64,128]{2,1,0:T(8,128)(2,1)S(1)}, u32[]{:S(2)}, u32[]{:S(2)}) collective-permute-start(bf16[16,64,128]{2,1,0:T(8,128)(2,1)S(1)} %slice.48), channel_id=1, source_target_pairs={{0,2},{1,15},{2,4},{3,1},{4,6},{5,3},{6,8},{7,5},{8,10},{9,7},{10,... | collective-permute-start | bytes 786440 | tf_op jit(solution)/shard_map/ppermute | solution.py:238
  100.8 9.0 %collective-permute-start.11 = (bf16[16,64,128]{2,1,0:T(8,128)(2,1)S(1)}, bf16[16,64,128]{2,1,0:T(8,128)(2,1)S(1)}, u32[]{:S(2)}, u32[]{:S(2)}) collective-permute-start(bf16[16,64,128]{2,1,0:T(8,128)(2,1)S(1)} %slice.60), channel_id=1, source_target_pairs={{0,2},{1,15},{2,4},{3,1},{4,6},{5,3},{6,8},{7,5},{8,10},{9,7},{10,... | collective-permute-start | bytes 786440 | tf_op jit(solution)/shard_map/ppermute | solution.py:238
  107.0 8.9 %collective-permute-start.14 = (bf16[16,64,128]{2,1,0:T(8,128)(2,1)S(1)}, bf16[16,64,128]{2,1,0:T(8,128)(2,1)S(1)}, u32[]{:S(2)}, u32[]{:S(2)}) collective-permute-start(bf16[16,64,128]{2,1,0:T(8,128)(2,1)S(1)} %fusion.1), channel_id=1, source_target_pairs={{0,4},{1,13},{2,6},{3,15},{4,8},{5,1},{6,10},{7,3},{8,12},{9,5},{1... | collective-permute-start | bytes 786440 | tf_op jit(solution)/shard_map/ppermute | solution.py:238
  109.9 11.1 %collective-permute-start.15 = (bf16[8,64,128]{2,1,0:T(8,128)(2,1)S(1)}, bf16[8,64,128]{2,1,0:T(8,128)(2,1)S(1)}, u32[]{:S(2)}, u32[]{:S(2)}) collective-permute-start(bf16[8,64,128]{2,1,0:T(8,128)(2,1)S(1)} %slice.50), channel_id=1, source_target_pairs={{0,1},{1,0},{2,3},{3,2},{4,5},{5,4},{6,7},{7,6},{8,9},{9,8},{10,11... | collective-permute-start | bytes 393224 | tf_op jit(solution)/shard_map/ppermute | solution.py:234
  115.9 6.1 %collective-permute-start.16 = (bf16[8,64,128]{2,1,0:T(8,128)(2,1)S(1)}, bf16[8,64,128]{2,1,0:T(8,128)(2,1)S(1)}, u32[]{:S(2)}, u32[]{:S(2)}) collective-permute-start(bf16[8,64,128]{2,1,0:T(8,128)(2,1)S(1)} %slice.51), channel_id=1, source_target_pairs={{0,1},{1,0},{2,3},{3,2},{4,5},{5,4},{6,7},{7,6},{8,9},{9,8},{10,11... | collective-permute-start | bytes 393224 | tf_op jit(solution)/shard_map/ppermute | solution.py:234
  (7 other events, 165.2 us)

commit v4 on v3

--- a/solution.py
+++ b/solution.py
@@ -15,7 +15,8 @@
 F32 = jnp.float32
 BF16 = jnp.bfloat16
 HIGHEST = lax.Precision.HIGHEST
-VMEM_LIMIT = 32 * 1024 * 1024
+VMEM_LIMIT = 12 * 1024 * 1024
+STAGE_LIMIT = 12 * 1024 * 1024
 
 
 def cas_table(count):
@@ -26,6 +27,13 @@
 
 def symbol(count):
     return (2.0 - 2.0 * np.cos(2.0 * np.pi * np.arange(count) / count)).astype(np.float32)
+
+
+def block_base(height, chips, share, place):
+    distance, flip = place
+    core = lax.rem(height, 2)
+    chip = lax.rem(height // 2 + distance * (1 - 2 * core) + chips, chips)
+    return (chip * 2 + (1 - core if flip else core)) * share
 
 
 def masked_line(orb_ref, line, live):
@@ -36,20 +44,27 @@
     return jnp.concatenate(parts, axis=0)
 
 
-def density_kernel(index_ref, live_ref, part_ref, base_ref, orb_hbm, *refs, chunk):
-    pieces, (cas_ref, dens_ref, spec_ref, table_ref, orb_ref, sems) = refs[:-6], refs[-6:]
+def stage_kernel(orb_hbm, orb_ref, left_ref, right_ref, sem):
+    copy = pltpu.make_async_copy(orb_hbm, orb_ref, sem)
+    copy.start()
+
+    def clear(i, carry):
+        left_ref[pl.ds(i * 8, 8)] = jnp.zeros((8, 64, LANES), F32)
+        right_ref[pl.ds(i * 8, 8)] = jnp.zeros((8, 64, LANES), F32)
+        return carry
+
+    lax.fori_loop(0, left_ref.shape[0] // 8, clear, 0)
+    copy.wait()
+
+
+def density_kernel(index_ref, live_ref, part_ref, orb_ref, *refs, chunk, places, chips):
+    pieces, (cas_ref, dens_ref, spec_ref, table_ref) = refs[:-4], refs[-4:]
     packed_rows = table_ref.shape[0] // 2
 
-    def fetch(i):
-        rows = pl.ds(i * chunk, chunk)
-        return pltpu.make_async_copy(orb_hbm.at[rows], orb_ref.at[rows], sems.at[i])
-
-    for i in range(orb_ref.shape[0] // chunk):
-        fetch(i).start()
     at = 0
     for piece in pieces:
         for first in range(0, piece.shape[0], 8):
-            base = base_ref[part_ref[2], at]
+            base = block_base(part_ref[2], chips, 8, places[at])
             at += 1
             both = piece[first : first + 8]
             table_ref[pl.ds(base, 8)] = both
@@ -58,7 +73,6 @@
 
     def body(i, carry):
         first = i * chunk
-        fetch(i).wait()
         rows_out = []
         for l in range(chunk):
             line = first + l
@@ -123,11 +137,12 @@
     pair_ref,
     live_ref,
     part_ref,
-    base_ref,
     orb_ref,
     dens_ref,
     back_ref,
     cas_ref,
+    left_in,
+    right_in,
     pot_ref,
     keep_ref,
     first_ref,
@@ -136,18 +151,12 @@
     right_ref,
     *,
     chunk,
+    places,
+    chips,
 ):
     lines = dens_ref.shape[0]
 
-    def clear(i, carry):
-        left_ref[pl.ds(i * 8, 8)] = jnp.zeros((8, 64, LANES), F32)
-        right_ref[pl.ds(i * 8, 8)] = jnp.zeros((8, 64, LANES), F32)
-        return carry
-
-    lax.fori_loop(0, left_ref.shape[0] // 8, clear, 0)
-    hartree = lax.dot_general(
-        back_ref[...].T, cas_ref[...], (((1,), (0,)), ((), ())), precision=HIGHEST, preferred_element_type=F32
-    )
+    hartree = jnp.dot(cas_ref[...], back_ref[...], precision=HIGHEST, preferred_element_type=F32).T
     dens = dens_ref[...]
     pot_ref[...] = hartree[:lines] - XC_COEF * jnp.exp(jnp.log(dens * dens + 1.0) * (1.0 / 6.0))
 
@@ -178,7 +187,7 @@
     at = 0
     for out in (keep_ref, first_ref, rest_ref):
         for first in range(0, out.shape[0], 8):
-            out[first : first + 8] = emit(base_ref[part_ref[2], at]).astype(out.dtype)
+            out[first : first + 8] = emit(block_base(part_ref[2], chips, 16, places[at])).astype(out.dtype)
             at += 1
 
 
@@ -233,33 +242,23 @@
     def across(values):
         return lax.ppermute(values, "height", twin)
 
-    def onward(values, hops):
-        shift = 2 * hops
-        return lax.ppermute(values, "height", [(h, (h + shift * (1 - 2 * (h % 2))) % heights) for h in range(heights)])
-
-    gather_rows, keep_rows, give_rows = [], [], []
-    for h in range(heights):
-        core, turn = h % 2, 1 - 2 * (h % 2)
-
-        def place_of(distance, owner):
-            return ((h // 2 + distance) % chips) * 2 + owner
-
-        places = [place_of(0, core), place_of(0, 1 - core)]
-        for d in (2, 1, 3, far):
-            count = 2 if d < far else 1
-            places += [place_of(-turn * d, core), place_of(-turn * d, 1 - core)][:count]
-            places += [place_of(turn * d, 1 - core), place_of(turn * d, core)][:count]
-        gather_rows.append(places)
-        keep, give = [], []
-        for d in (far, 3, 1, 2, 0):
-            count = 2 if 0 < d < far else 1
-            keep += [place_of(turn * d, core), place_of(turn * d, 1 - core)][:count]
-            give += [place_of(-turn * d, 1 - core), place_of(-turn * d, core)][:count]
-        keep_rows.append(keep)
-        give_rows.append(give)
+    def onward(values, hops, sign=1, flip=0):
+        def target(h):
+            core = h % 2
+            return (h // 2 + sign * hops * (1 - 2 * core)) % chips * 2 + (core ^ flip)
+
+        return lax.ppermute(values, "height", [(h, target(h)) for h in range(heights)])
+
     half = share // 2
-    table_rows = np.array(gather_rows, np.int32) * half
-    sum_rows = np.concatenate([np.array(keep_rows, np.int32), np.array(give_rows, np.int32)], axis=1) * share
+    gather_places = [(0, 0), (0, 1)]
+    for d in (2, 1, 3):
+        gather_places += [(-d, 0), (-d, 1), (d, 1), (d, 0)]
+    gather_places += [(far, 0), (far, 1)]
+    keep_places, give_places = [(far, 0)], [(far, 1)]
+    for d in (3, 1, 2):
+        keep_places += [(d, 0), (d, 1)]
+        give_places += [(-d, 1), (-d, 0)]
+    sum_places = keep_places + [(0, 0)] + give_places + [(0, 1)]
 
     side = jnp.arange(lines * 16, dtype=jnp.int32) % 2
     table_index = (pairs // share) * half + pairs % half
@@ -267,29 +266,37 @@
     whole_chip = jnp.concatenate([packed, across(packed)], axis=0)
     second = onward(whole_chip, 2)
     near = onward(whole_chip, 1)
-    near, table_index, live, part, pairs = lax.optimization_barrier((near, table_index, live, part, pairs))
+    smem = pl.BlockSpec(memory_space=pltpu.SMEM)
+    vmem = pl.BlockSpec(memory_space=pltpu.VMEM)
+    params = pltpu.CompilerParams(vmem_limit_bytes=VMEM_LIMIT)
+    sums_shape = jax.ShapeDtypeStruct((2 * block_rows, 64, LANES), F32)
+    orb, left, right = pl.pallas_call(
+        stage_kernel,
+        in_specs=[pl.BlockSpec(memory_space=pl.ANY)],
+        out_specs=[vmem] * 3,
+        out_shape=[jax.ShapeDtypeStruct(orb.shape, BF16), sums_shape, sums_shape],
+        scratch_shapes=[pltpu.SemaphoreType.DMA(())],
+        compiler_params=pltpu.CompilerParams(vmem_limit_bytes=STAGE_LIMIT),
+        name="stage",
+    )(orb)
+    second, near, table_index, live, part, pairs, orb, left, right = lax.optimization_barrier(
+        (second, near, table_index, live, part, pairs, orb, left, right)
+    )
     pieces = [whole_chip]
     for piece in (second, near, onward(second, 1), onward(second[:half], 2)):
         pieces += [piece, across(piece)]
-    smem = pl.BlockSpec(memory_space=pltpu.SMEM)
-    vmem = pl.BlockSpec(memory_space=pltpu.VMEM)
-    params = pltpu.CompilerParams(vmem_limit_bytes=VMEM_LIMIT)
     density, spectrum = pl.pallas_call(
-        functools.partial(density_kernel, chunk=chunk),
-        in_specs=[smem] * 4 + [pl.BlockSpec(memory_space=pl.ANY)] + [vmem] * (len(pieces) + 1),
+        functools.partial(density_kernel, chunk=chunk, places=gather_places, chips=chips),
+        in_specs=[smem] * 3 + [vmem] * (len(pieces) + 2),
         out_specs=[vmem, vmem],
         out_shape=[
             jax.ShapeDtypeStruct((lines, line_cells), F32),
             jax.ShapeDtypeStruct((devices, LANES), F32),
         ],
-        scratch_shapes=[
-            pltpu.VMEM((2 * block_rows, 64, LANES), BF16),
-            pltpu.VMEM((lines, width, line_cells), BF16),
-            pltpu.SemaphoreType.DMA((lines // chunk,)),
-        ],
+        scratch_shapes=[pltpu.VMEM((2 * block_rows, 64, LANES), BF16)],
         compiler_params=params,
         name="density",
-    )(table_index, live, part, jnp.asarray(table_rows), orb, *pieces, jnp.asarray(cas_y2))
+    )(table_index, live, part, orb, *pieces, jnp.asarray(cas_y2))
 
     def exchange(values):
         out = lax.all_to_all(values.reshape(devices, 1, LANES), ("col", "height"), split_axis=0, concat_axis=0, tiled=True)
@@ -315,30 +322,40 @@
     returned = exchange(solved)
 
     half_rows = block_rows // 2
-    potential, keep, give_first, give_rest = pl.pallas_call(
-        functools.partial(hamiltonian_kernel, chunk=chunk),
-        in_specs=[smem] * 4 + [vmem] * 4,
-        out_specs=[vmem] * 4,
+    potential, keep, give_first, give_rest, _, _ = pl.pallas_call(
+        functools.partial(hamiltonian_kernel, chunk=chunk, places=sum_places, chips=chips),
+        in_specs=[smem] * 3 + [vmem] * 6,
+        out_specs=[vmem] * 6,
         out_shape=[
             jax.ShapeDtypeStruct((lines, line_cells), F32),
             jax.ShapeDtypeStruct((half_rows, 64, LANES), F32),
             jax.ShapeDtypeStruct((3 * share // 2, 64, LANES), BF16),
             jax.ShapeDtypeStruct((half_rows - 3 * share // 2, 64, LANES), BF16),
+            sums_shape,
+            sums_shape,
         ],
-        scratch_shapes=[pltpu.VMEM((2 * block_rows, 64, LANES), F32)] * 2,
+        input_output_aliases={7: 4, 8: 5},
         compiler_params=params,
         name="hamiltonian",
-    )(pairs, live, part, jnp.asarray(sum_rows), orb, density, returned, jnp.asarray(cas_y2.T.copy()))
+    )(pairs, live, part, orb, density, returned, jnp.asarray(cas_y2), left, right)
 
     got_first = across(give_first)
     got_rest = across(lax.optimization_barrier((give_rest, got_first))[0])
-    begin = (keep[: 3 * half] + got_first.astype(F32)).astype(BF16)
-    from_far = onward(begin[:half], 2).astype(F32)
-    from_third = onward(begin[half:], 1).astype(F32)
-    local = keep[3 * half :] + got_rest.astype(F32)
-    by_one = onward(local[: 2 * half].astype(BF16), 1)
-    from_far = jnp.concatenate([from_far, jnp.zeros_like(from_far)], axis=0)
-    by_two = onward((local[2 * half : 4 * half] + from_third + from_far).astype(BF16), 2)
+
+    def local(kept, i):
+        got = got_first[i * half : (i + 1) * half] if i < 3 else got_rest[(i - 3) * half : (i - 2) * half]
+        return kept[i * half : (i + 1) * half] + got.astype(F32)
+
+    begin = lax.optimization_barrier((keep, *[local(keep, i).astype(BF16) for i in range(3)]))
+    far_sum = onward(begin[1], 2)
+    third = onward(begin[2], 1)
+    third_twin = onward(begin[3], 1)
+    ones = lax.optimization_barrier((begin[0], local(begin[0], 3).astype(BF16), local(begin[0], 4).astype(BF16)))
+    by_one = onward(ones[1], 1)
+    by_one_twin = onward(ones[2], 1, 1, 1)
+    twos = lax.optimization_barrier((ones[0], (local(ones[0], 6) + third_twin.astype(F32)).astype(BF16)))
+    by_two_twin = onward(twos[1], 2, 1, 1)
+    by_two = onward((local(twos[0], 5) + far_sum.astype(F32) + third.astype(F32)).astype(BF16), 2)
     hamiltonian = pl.pallas_call(
         finish_kernel,
         in_specs=[vmem] * 6,
@@ -346,7 +363,7 @@
         out_shape=jax.ShapeDtypeStruct(density_blocks.shape, F32),
         compiler_params=params,
         name="finish",
-    )(keep, got_rest, by_one, by_two, across(by_one[half:]), across(by_two[half:]))
+    )(keep, got_rest, by_one, by_two, by_one_twin, by_two_twin)
     return potential.reshape(cells_x, cells_z, line_cells), hamiltonian
 
 

time: 123 us -> 119 us (0.967)
  waiting for transfers between devices: 24.8 us -> 20.2 us
  blocking collectives: 44 us -> 41.7 us
  starting transfers between devices: 26.9 us -> 29 us
  local copies, waits for them, and re-layouts: 4.72 us -> 6.09 us
    ppermute x8 -> x11, starting transfers between devices: 11.5 us -> 16.7 us  [onward(): lax.ppermute(values, 'height', [(h, target(h)) for h in range(heights)])]
    ppermute x9 -> x7, starting transfers between devices: 15.5 us -> 12.3 us  [across(): return lax.ppermute(values, 'height', twin)]
    ppermute x8 -> x11, waiting for transfers between devices: 19.4 us -> 16.8 us  [onward(): lax.ppermute(values, 'height', [(h, target(h)) for h in range(heights)])]
    all_to_all x2, blocking collectives: 44 us -> 41.7 us  [exchange(): lax.all_to_all(values.reshape(devices, 1, LANES), ('col', 'height'), spli...]
    ppermute x9 -> x7, waiting for transfers between devices: 5.47 us -> 3.46 us  [across(): return lax.ppermute(values, 'height', twin)]
    unnamed x30 -> x18, local copies, waits for them, and re-layouts: 3.28 us -> 4.77 us
    pallas_call x2 -> x3, Pallas kernels: 18 us -> 17.8 us  [the longest x1 9.61 us: per_device(): pl.pallas_call(functools.partial(hamiltonian_kernel, chunk=chunk, places=...]
  transfers between devices with their start and end apart: 17 -> 18, of which waited for: 12 -> 12; matrix products, arithmetic and copies ran while one was open for 1% -> 2% of each run, Pallas kernels for 0% -> 1%
where the time goes in v4:
time: 119 us
  blocking collectives  41.7 us (35%)
  starting transfers between devices  29 us (24%)
  Pallas kernels  20.5 us (17%)
  waiting for transfers between devices  20.2 us (17%)
  local copies, waits for them, and re-layouts  6.09 us (5%)
    all_to_all x2, blocking collectives, exchange(): lax.all_to_all(values.reshape(devices, 1, LANES), ('col', 'height'), spli...  41.7 us
    ppermute x11, waiting for transfers between devices, onward(): lax.ppermute(values, 'height', [(h, target(h)) for h in range(heights)])  16.8 us
    ppermute x11, starting transfers between devices, onward(): lax.ppermute(values, 'height', [(h, target(h)) for h in range(heights)])  16.7 us
    ppermute x7, starting transfers between devices, across(): return lax.ppermute(values, 'height', twin)  12.3 us
    pallas_call x1, Pallas kernels, per_device(): pl.pallas_call(functools.partial(hamiltonian_kernel, chunk=chunk, places=...  9.61 us
    pallas_call x1, Pallas kernels, per_device(): pl.pallas_call(functools.partial(density_kernel, chunk=chunk, places=gath...  6.62 us
    unnamed x18, local copies, waits for them, and re-layouts  4.77 us
    ppermute x7, waiting for transfers between devices, across(): return lax.ppermute(values, 'height', twin)  3.46 us
  transfers between devices with their start and end apart: 18, of which 12 were waited for; matrix products, arithmetic and copies ran while one was open for 2% of the time, Pallas kernels for 1%

profile of v4, /device:TPU:1, one launch (start us, length us, event | category | flops | bytes accessed | tf_op | source)
XLA Modules:
  0.0 119.0 jit_solution(12046374665678045400)
XLA Ops:
  0.6 1.0 fusion.11
  1.8 3.3 %collective-permute-start = (bf16[8,64,128]{2,1,0:T(8,128)(2,1)S(1)}, bf16[8,64,128]{2,1,0:T(8,128)(2,1)S(1)}, u32[]{:S(2)}, u32[]{:S(2)}) collective-permute-start(bf16[8,64,128]{2,1,0:T(8,128)(2,1)S(1)} %pad_maximum_fusion.1), channel_id=1, source_target_pairs={{0,1},{1,0},{2,3},{3,2},{4,5},{5,4},{6,7},{7,6},{8,9},{9,8},{10,11... | collective-permute-start | bytes 393224 | tf_op jit(solution)/shard_map/ppermute | solution.py:243
  6.2 3.9 %collective-permute-start.2 = (bf16[16,64,128]{2,1,0:T(8,128)(2,1)S(1)}, bf16[16,64,128]{2,1,0:T(8,128)(2,1)S(1)}, u32[]{:S(2)}, u32[]{:S(2)}) collective-permute-start(bf16[16,64,128]{2,1,0:T(8,128)(2,1)S(1)} %pad_maximum_fusion.refs_0_), channel_id=1, source_target_pairs={{0,2},{1,15},{2,4},{3,1},{4,6},{5,3},{6,8},{7,5},{8,10},{9,7},{10,... | collective-permute-start | bytes 786440 | tf_op jit(solution)/shard_map/ppermute | solution.py:250
  10.1 1.2 collective-permute-start.1
  12.2 1.2 copy.18
  13.6 2.8 %copy-done = bf16[12,8,256,128]{3,2,1,0:T(8,128)(2,1)S(1)} copy-done((bf16[12,8,256,128]{3,2,1,0:T(8,128)(2,1)S(1)}, bf16[12,8,256,128]{3,2,1,0:T(8,128)(2,1)}, u32[]{:S(2)}) %copy-start) | copy-done | bytes 6291480
  16.4 1.5 %stage.1 = (bf16[96,256,128]{2,1,0:T(8,128)(2,1)S(1)}, f32[256,64,128]{2,1,0:T(8,128)S(1)}, f32[256,64,128]{2,1,0:T(8,128)S(1)}) custom-call(bf16[96,256,128]{2,1,0:T(8,128)(2,1)S(1)} %bitcast.13), custom_call_target="tpu_custom_call" | custom-call | tf_op jit(solution)/shard_map/stage/pallas_call | solution.py:273
  18.0 1.0 collective-permute-done.1.refs_1_
  19.1 2.0 %collective-permute-start.5 = (bf16[16,64,128]{2,1,0:T(8,128)(2,1)S(1)}, bf16[16,64,128]{2,1,0:T(8,128)(2,1)S(1)}, u32[]{:S(2)}, u32[]{:S(2)}) collective-permute-start(bf16[16,64,128]{2,1,0:T(8,128)(2,1)S(1)} %collective-permute-done.1.refs_1_), channel_id=1, source_target_pairs={{0,2},{1,15},{2,4},{3,1},{4,6},{5,3},{6,8},{7,5},{8,10},{9,7},{10,... | collective-permute-start | bytes 786440 | tf_op jit(solution)/shard_map/ppermute | solution.py:250
  21.1 2.1 %collective-permute-start.7 = (bf16[8,64,128]{2,1,0:T(8,128)(2,1)S(1)}, bf16[8,64,128]{2,1,0:T(8,128)(2,1)S(1)}, u32[]{:S(2)}, u32[]{:S(2)}) collective-permute-start(bf16[8,64,128]{2,1,0:T(8,128)(2,1)S(1)} %slice.53), channel_id=1, source_target_pairs={{0,4},{1,13},{2,6},{3,15},{4,8},{5,1},{6,10},{7,3},{8,12},{9,5},{1... | collective-permute-start | bytes 393224 | tf_op jit(solution)/shard_map/ppermute | solution.py:250
  24.6 3.0 %collective-permute-start.6 = (bf16[16,64,128]{2,1,0:T(8,128)(2,1)S(1)}, bf16[16,64,128]{2,1,0:T(8,128)(2,1)S(1)}, u32[]{:S(2)}, u32[]{:S(2)}) collective-permute-start(bf16[16,64,128]{2,1,0:T(8,128)(2,1)S(1)} %collective-permute-done.5.refs_5_), channel_id=1, source_target_pairs={{0,1},{1,0},{2,3},{3,2},{4,5},{5,4},{6,7},{7,6},{8,9},{9,8},{10,11... | collective-permute-start | bytes 786440 | tf_op jit(solution)/shard_map/ppermute | solution.py:243
  27.6 4.3 %collective-permute-start.8 = (bf16[8,64,128]{2,1,0:T(8,128)(2,1)S(1)}, bf16[8,64,128]{2,1,0:T(8,128)(2,1)S(1)}, u32[]{:S(2)}, u32[]{:S(2)}) collective-permute-start(bf16[8,64,128]{2,1,0:T(8,128)(2,1)S(1)} %collective-permute-done.7.refs_7_), channel_id=1, source_target_pairs={{0,1},{1,0},{2,3},{3,2},{4,5},{5,4},{6,7},{7,6},{8,9},{9,8},{10,11... | collective-permute-start | bytes 393224 | tf_op jit(solution)/shard_map/ppermute | solution.py:243
  32.8 6.6 %density.1 = (f32[96,128]{1,0:T(8,128)S(1)}, f32[256,128]{1,0:T(8,128)S(1)}) custom-call(s32[1536]{0:T(1024)S(1)} %fusion.3.index_ref, s32[96]{0:T(128)S(1)} %reshape.29.live_ref, s32[3]{0:T(128)S(1)} %pad_add_fusion.part_ref.refs_0_, bf16[96,256,128]{2,1,0:T(8,128)(2,1)S(1)} %get-tuple-element.36.orb_ref, bf16[16,64,128]{2,1,0:T(8,128)(2,1)S(1)} %pad_maximum_fusion.refs_0_, ...), custom_call_target="tpu_custom_call" | custom-call | tf_op jit(solution)/shard_map/density/pallas_call | solution.py:288
  39.5 23.1 %all_to_all.10 = f32[256,1,128]{2,1,0:T(1,128)S(1)} all-to-all(f32[256,1,128]{2,1,0:T(1,128)S(1)} %bitcast.17), channel_id=1, replica_groups=mesh['col'=16,'height'=16] {'col','height'}, dimensions={0} | all-to-all | bytes 262144 | tf_op jit(solution)/shard_map/all_to_all | solution.py:302
  62.6 1.8 %solve.1 = f32[256,128]{1,0:T(8,128)S(1)} custom-call(s32[3]{0:T(128)S(1)} %pad_add_fusion.part_ref.refs_0_, f32[256,128]{1,0:T(8,128)S(1)} %bitcast.15, f32[2,96,192]{2,1,0:T(8,128)S(1)} %copy-done.3, f32[2,192,96]{2,1,0:T(8,128)S(1)} %copy-done.2, f32[128,128]{1,0:T(8,128)S(1)} %copy-done.5, f32[2,96,128]{2,1,0:T(8,128)S(1)} %copy-done.4, ...), custom_call_target="tpu_custom_call" | custom-call | tf_op jit(solution)/shard_map/solve/pallas_call | solution.py:305
  64.4 18.6 %all_to_all.11 = f32[256,1,128]{2,1,0:T(1,128)S(1)} all-to-all(f32[256,1,128]{2,1,0:T(1,128)S(1)} %bitcast.16), channel_id=1, replica_groups=mesh['col'=16,'height'=16] {'col','height'}, dimensions={0} | all-to-all | bytes 262144 | tf_op jit(solution)/shard_map/all_to_all | solution.py:302
  83.0 9.6 %hamiltonian.1 = (f32[96,128]{1,0:T(8,128)}, f32[64,64,128]{2,1,0:T(8,128)S(1)}, bf16[24,64,128]{2,1,0:T(8,128)(2,1)S(1)}, bf16[40,64,128]{2,1,0:T(8,128)(2,1)S(...) custom-call(s32[1536]{0:T(1024)S(1)} %reshape.28.pair_ref, ...), custom_call_target="tpu_custom_call", output_to_operand_aliasing={{4}: (7, {}), {5}: (8, {})} | custom-call | tf_op jit(solution)/shard_map/hamiltonian/pallas_call | solution.py:325
  93.5 1.3 %collective-permute-done.9 = bf16[24,64,128]{2,1,0:T(8,128)(2,1)S(1)} collective-permute-done((bf16[24,64,128]{2,1,0:T(8,128)(2,1)S(1)}, bf16[24,64,128]{2,1,0:T(8,128)(2,1)S(1)}, u32[]{:S(2)}, u32[]{:S(2)}) %collective-permute-start.9) | collective-permute-done | bytes 393248 | tf_op jit(solution)/shard_map/ppermute | solution.py:243
  95.8 1.1 collective-permute-start.14
  97.1 2.2 %collective-permute-done.12 = bf16[8,64,128]{2,1,0:T(8,128)(2,1)S(1)} collective-permute-done((bf16[8,64,128]{2,1,0:T(8,128)(2,1)S(1)}, bf16[8,64,128]{2,1,0:T(8,128)(2,1)S(1)}, u32[]{:S(2)}, u32[]{:S(2)}) %collective-permute-start.12) | collective-permute-done | bytes 131104 | tf_op jit(solution)/shard_map/ppermute | solution.py:250
  99.3 3.7 %collective-permute-done.13 = bf16[8,64,128]{2,1,0:T(8,128)(2,1)S(1)} collective-permute-done((bf16[8,64,128]{2,1,0:T(8,128)(2,1)S(1)}, bf16[8,64,128]{2,1,0:T(8,128)(2,1)S(1)}, u32[]{:S(2)}, u32[]{:S(2)}) %collective-permute-start.13) | collective-permute-done | bytes 131104 | tf_op jit(solution)/shard_map/ppermute | solution.py:250
  104.4 5.5 %collective-permute-start.17 = (bf16[8,64,128]{2,1,0:T(8,128)(2,1)S(1)}, bf16[8,64,128]{2,1,0:T(8,128)(2,1)S(1)}, u32[]{:S(2)}, u32[]{:S(2)}) collective-permute-start(bf16[8,64,128]{2,1,0:T(8,128)(2,1)S(1)} %add_convert_fusion.1), channel_id=1, source_target_pairs={{0,5},{1,12},{2,7},{3,14},{4,9},{5,0},{6,11},{7,2},{8,13},{9,4},{1... | collective-permute-start | bytes 393224 | tf_op jit(solution)/shard_map/ppermute | solution.py:250
  110.0 6.8 %collective-permute-done.17.twin_two_ref = bf16[8,64,128]{2,1,0:T(8,128)(2,1)S(1)} collective-permute-done((bf16[8,64,128]{2,1,0:T(8,128)(2,1)S(1)}, bf16[8,64,128]{2,1,0:T(8,128)(2,1)S(1)}, u32[]{:S(2)}, u32[]{:S(2)}) %collective-permute-start.17) | collective-permute-done | bytes 131104 | tf_op jit(solution)/shard_map/ppermute | solution.py:250
  116.8 1.3 %collective-permute-done.16.twin_one_ref = bf16[8,64,128]{2,1,0:T(8,128)(2,1)S(1)} collective-permute-done((bf16[8,64,128]{2,1,0:T(8,128)(2,1)S(1)}, bf16[8,64,128]{2,1,0:T(8,128)(2,1)S(1)}, u32[]{:S(2)}, u32[]{:S(2)}) %collective-permute-start.16) | collective-permute-done | bytes 131104 | tf_op jit(solution)/shard_map/ppermute | solution.py:250
  (49 shorter events, 9.3 us)
Async XLA Ops:
  1.8 4.3 %collective-permute-start = (bf16[8,64,128]{2,1,0:T(8,128)(2,1)S(1)}, bf16[8,64,128]{2,1,0:T(8,128)(2,1)S(1)}, u32[]{:S(2)}, u32[]{:S(2)}) collective-permute-start(bf16[8,64,128]{2,1,0:T(8,128)(2,1)S(1)} %pad_maximum_fusion.1), channel_id=1, source_target_pairs={{0,1},{1,0},{2,3},{3,2},{4,5},{5,4},{6,7},{7,6},{8,9},{9,8},{10,11... | collective-permute-start | bytes 393224 | tf_op jit(solution)/shard_map/ppermute | solution.py:243
  6.2 11.8 %collective-permute-start.2 = (bf16[16,64,128]{2,1,0:T(8,128)(2,1)S(1)}, bf16[16,64,128]{2,1,0:T(8,128)(2,1)S(1)}, u32[]{:S(2)}, u32[]{:S(2)}) collective-permute-start(bf16[16,64,128]{2,1,0:T(8,128)(2,1)S(1)} %pad_maximum_fusion.refs_0_), channel_id=1, source_target_pairs={{0,2},{1,15},{2,4},{3,1},{4,6},{5,3},{6,8},{7,5},{8,10},{9,7},{10,... | collective-permute-start | bytes 786440 | tf_op jit(solution)/shard_map/ppermute | solution.py:250
  10.1 8.9 %collective-permute-start.1 = (bf16[16,64,128]{2,1,0:T(8,128)(2,1)S(1)}, bf16[16,64,128]{2,1,0:T(8,128)(2,1)S(1)}, u32[]{:S(2)}, u32[]{:S(2)}) collective-permute-start(bf16[16,64,128]{2,1,0:T(8,128)(2,1)S(1)} %pad_maximum_fusion.refs_0_), channel_id=1, source_target_pairs={{0,4},{1,13},{2,6},{3,15},{4,8},{5,1},{6,10},{7,3},{8,12},{9,5},{1... | collective-permute-start | bytes 786440 | tf_op jit(solution)/shard_map/ppermute | solution.py:250
  16.4 46.2 %copy-start.2 = (f32[2,192,96]{2,1,0:T(8,128)S(1)}, f32[2,192,96]{2,1,0:T(8,128)}, u32[]{:S(2)}) copy-start(f32[2,192,96]{2,1,0:T(8,128)} %constant.99.clone.refs_3_) | copy-start | bytes 442372
  16.4 46.2 %copy-start.3 = (f32[2,96,192]{2,1,0:T(8,128)S(1)}, f32[2,96,192]{2,1,0:T(8,128)}, u32[]{:S(2)}) copy-start(f32[2,96,192]{2,1,0:T(8,128)} %constant.98.clone.refs_2_) | copy-start | bytes 442372
  16.4 46.2 %copy-start.4 = (f32[2,96,128]{2,1,0:T(8,128)S(1)}, f32[2,96,128]{2,1,0:T(8,128)}, u32[]{:S(2)}) copy-start(f32[2,96,128]{2,1,0:T(8,128)} %constant.101.clone.refs_5_) | copy-start | bytes 294916
  16.4 46.2 %copy-start.5 = (f32[128,128]{1,0:T(8,128)S(1)}, f32[128,128]{1,0:T(8,128)}, u32[]{:S(2)}) copy-start(f32[128,128]{1,0:T(8,128)} %constant.100.clone.refs_4_) | copy-start | bytes 196612
  16.4 46.2 %copy-start.6 = (f32[128]{0:T(128)S(1)}, f32[128]{0:T(128)}, u32[]{:S(2)}) copy-start(f32[128]{0:T(128)} %constant.103.clone.refs_7_) | copy-start | bytes 1540
  16.4 46.2 %copy-start.7 = (f32[1,128]{1,0:T(1,128)S(1)}, f32[1,128]{1,0:T(1,128)}, u32[]{:S(2)}) copy-start(f32[1,128]{1,0:T(1,128)} %constant.102.clone.refs_6_) | copy-start | bytes 1540
  19.1 5.5 %collective-permute-start.5 = (bf16[16,64,128]{2,1,0:T(8,128)(2,1)S(1)}, bf16[16,64,128]{2,1,0:T(8,128)(2,1)S(1)}, u32[]{:S(2)}, u32[]{:S(2)}) collective-permute-start(bf16[16,64,128]{2,1,0:T(8,128)(2,1)S(1)} %collective-permute-done.1.refs_1_), channel_id=1, source_target_pairs={{0,2},{1,15},{2,4},{3,1},{4,6},{5,3},{6,8},{7,5},{8,10},{9,7},{10,... | collective-permute-start | bytes 786440 | tf_op jit(solution)/shard_map/ppermute | solution.py:250
  21.1 6.4 %collective-permute-start.7 = (bf16[8,64,128]{2,1,0:T(8,128)(2,1)S(1)}, bf16[8,64,128]{2,1,0:T(8,128)(2,1)S(1)}, u32[]{:S(2)}, u32[]{:S(2)}) collective-permute-start(bf16[8,64,128]{2,1,0:T(8,128)(2,1)S(1)} %slice.53), channel_id=1, source_target_pairs={{0,4},{1,13},{2,6},{3,15},{4,8},{5,1},{6,10},{7,3},{8,12},{9,5},{1... | collective-permute-start | bytes 393224 | tf_op jit(solution)/shard_map/ppermute | solution.py:250
  23.2 9.6 %collective-permute-start.3 = (bf16[16,64,128]{2,1,0:T(8,128)(2,1)S(1)}, bf16[16,64,128]{2,1,0:T(8,128)(2,1)S(1)}, u32[]{:S(2)}, u32[]{:S(2)}) collective-permute-start(bf16[16,64,128]{2,1,0:T(8,128)(2,1)S(1)} %collective-permute-done.1.refs_1_), channel_id=1, source_target_pairs={{0,1},{1,0},{2,3},{3,2},{4,5},{5,4},{6,7},{7,6},{8,9},{9,8},{10,11... | collective-permute-start | bytes 786440 | tf_op jit(solution)/shard_map/ppermute | solution.py:243
  23.2 9.6 %collective-permute-start.4 = (bf16[16,64,128]{2,1,0:T(8,128)(2,1)S(1)}, bf16[16,64,128]{2,1,0:T(8,128)(2,1)S(1)}, u32[]{:S(2)}, u32[]{:S(2)}) collective-permute-start(bf16[16,64,128]{2,1,0:T(8,128)(2,1)S(1)} %collective-permute-done.2.refs_3_), channel_id=1, source_target_pairs={{0,1},{1,0},{2,3},{3,2},{4,5},{5,4},{6,7},{7,6},{8,9},{9,8},{10,11... | collective-permute-start | bytes 786440 | tf_op jit(solution)/shard_map/ppermute | solution.py:243
  24.6 8.2 %collective-permute-start.6 = (bf16[16,64,128]{2,1,0:T(8,128)(2,1)S(1)}, bf16[16,64,128]{2,1,0:T(8,128)(2,1)S(1)}, u32[]{:S(2)}, u32[]{:S(2)}) collective-permute-start(bf16[16,64,128]{2,1,0:T(8,128)(2,1)S(1)} %collective-permute-done.5.refs_5_), channel_id=1, source_target_pairs={{0,1},{1,0},{2,3},{3,2},{4,5},{5,4},{6,7},{7,6},{8,9},{9,8},{10,11... | collective-permute-start | bytes 786440 | tf_op jit(solution)/shard_map/ppermute | solution.py:243
  27.6 5.3 %collective-permute-start.8 = (bf16[8,64,128]{2,1,0:T(8,128)(2,1)S(1)}, bf16[8,64,128]{2,1,0:T(8,128)(2,1)S(1)}, u32[]{:S(2)}, u32[]{:S(2)}) collective-permute-start(bf16[8,64,128]{2,1,0:T(8,128)(2,1)S(1)} %collective-permute-done.7.refs_7_), channel_id=1, source_target_pairs={{0,1},{1,0},{2,3},{3,2},{4,5},{5,4},{6,7},{7,6},{8,9},{9,8},{10,11... | collective-permute-start | bytes 393224 | tf_op jit(solution)/shard_map/ppermute | solution.py:243
  92.7 2.2 %collective-permute-start.9 = (bf16[24,64,128]{2,1,0:T(8,128)(2,1)S(1)}, bf16[24,64,128]{2,1,0:T(8,128)(2,1)S(1)}, u32[]{:S(2)}, u32[]{:S(2)}) collective-permute-start(bf16[24,64,128]{2,1,0:T(8,128)(2,1)S(1)} %get-tuple-element.47), channel_id=1, source_target_pairs={{0,1},{1,0},{2,3},{3,2},{4,5},{5,4},{6,7},{7,6},{8,9},{9,8},{10,11... | collective-permute-start | bytes 1179656 | tf_op jit(solution)/shard_map/ppermute | solution.py:243
  94.9 2.1 %collective-permute-start.10 = (bf16[40,64,128]{2,1,0:T(8,128)(2,1)S(1)}, bf16[40,64,128]{2,1,0:T(8,128)(2,1)S(1)}, u32[]{:S(2)}, u32[]{:S(2)}) collective-permute-start(bf16[40,64,128]{2,1,0:T(8,128)(2,1)S(1)} %get-tuple-element.48), channel_id=1, source_target_pairs={{0,1},{1,0},{2,3},{3,2},{4,5},{5,4},{6,7},{7,6},{8,9},{9,8},{10,11... | collective-permute-start | bytes 1966088 | tf_op jit(solution)/shard_map/ppermute | solution.py:243
  95.4 3.9 %collective-permute-start.12 = (bf16[8,64,128]{2,1,0:T(8,128)(2,1)S(1)}, bf16[8,64,128]{2,1,0:T(8,128)(2,1)S(1)}, u32[]{:S(2)}, u32[]{:S(2)}) collective-permute-start(bf16[8,64,128]{2,1,0:T(8,128)(2,1)S(1)} %get-tuple-element.52), channel_id=1, source_target_pairs={{0,2},{1,15},{2,4},{3,1},{4,6},{5,3},{6,8},{7,5},{8,10},{9,7},{10,... | collective-permute-start | bytes 393224 | tf_op jit(solution)/shard_map/ppermute | solution.py:250
  95.5 7.6 %collective-permute-start.13 = (bf16[8,64,128]{2,1,0:T(8,128)(2,1)S(1)}, bf16[8,64,128]{2,1,0:T(8,128)(2,1)S(1)}, u32[]{:S(2)}, u32[]{:S(2)}) collective-permute-start(bf16[8,64,128]{2,1,0:T(8,128)(2,1)S(1)} %get-tuple-element.54), channel_id=1, source_target_pairs={{0,4},{1,13},{2,6},{3,15},{4,8},{5,1},{6,10},{7,3},{8,12},{9,5},{1... | collective-permute-start | bytes 393224 | tf_op jit(solution)/shard_map/ppermute | solution.py:250
  95.8 8.0 %collective-permute-start.14 = (bf16[8,64,128]{2,1,0:T(8,128)(2,1)S(1)}, bf16[8,64,128]{2,1,0:T(8,128)(2,1)S(1)}, u32[]{:S(2)}, u32[]{:S(2)}) collective-permute-start(bf16[8,64,128]{2,1,0:T(8,128)(2,1)S(1)} %get-tuple-element.55), channel_id=1, source_target_pairs={{0,2},{1,15},{2,4},{3,1},{4,6},{5,3},{6,8},{7,5},{8,10},{9,7},{10,... | collective-permute-start | bytes 393224 | tf_op jit(solution)/shard_map/ppermute | solution.py:250
  103.9 6.1 %collective-permute-start.15 = (bf16[8,64,128]{2,1,0:T(8,128)(2,1)S(1)}, bf16[8,64,128]{2,1,0:T(8,128)(2,1)S(1)}, u32[]{:S(2)}, u32[]{:S(2)}) collective-permute-start(bf16[8,64,128]{2,1,0:T(8,128)(2,1)S(1)} %add_convert_fusion), channel_id=1, source_target_pairs={{0,4},{1,13},{2,6},{3,15},{4,8},{5,1},{6,10},{7,3},{8,12},{9,5},{1... | collective-permute-start | bytes 393224 | tf_op jit(solution)/shard_map/ppermute | solution.py:250
  104.4 12.4 %collective-permute-start.17 = (bf16[8,64,128]{2,1,0:T(8,128)(2,1)S(1)}, bf16[8,64,128]{2,1,0:T(8,128)(2,1)S(1)}, u32[]{:S(2)}, u32[]{:S(2)}) collective-permute-start(bf16[8,64,128]{2,1,0:T(8,128)(2,1)S(1)} %add_convert_fusion.1), channel_id=1, source_target_pairs={{0,5},{1,12},{2,7},{3,14},{4,9},{5,0},{6,11},{7,2},{8,13},{9,4},{1... | collective-permute-start | bytes 393224 | tf_op jit(solution)/shard_map/ppermute | solution.py:250
  109.9 6.9 %collective-permute-start.11 = (bf16[8,64,128]{2,1,0:T(8,128)(2,1)S(1)}, bf16[8,64,128]{2,1,0:T(8,128)(2,1)S(1)}, u32[]{:S(2)}, u32[]{:S(2)}) collective-permute-start(bf16[8,64,128]{2,1,0:T(8,128)(2,1)S(1)} %get-tuple-element.50), channel_id=1, source_target_pairs={{0,2},{1,15},{2,4},{3,1},{4,6},{5,3},{6,8},{7,5},{8,10},{9,7},{10,... | collective-permute-start | bytes 393224 | tf_op jit(solution)/shard_map/ppermute | solution.py:250
  109.9 8.2 %collective-permute-start.16 = (bf16[8,64,128]{2,1,0:T(8,128)(2,1)S(1)}, bf16[8,64,128]{2,1,0:T(8,128)(2,1)S(1)}, u32[]{:S(2)}, u32[]{:S(2)}) collective-permute-start(bf16[8,64,128]{2,1,0:T(8,128)(2,1)S(1)} %get-tuple-element.56), channel_id=1, source_target_pairs={{0,3},{1,14},{2,5},{3,0},{4,7},{5,2},{6,9},{7,4},{8,11},{9,6},{10,... | collective-permute-start | bytes 393224 | tf_op jit(solution)/shard_map/ppermute | solution.py:250
  (2 other events, 35.0 us)

commit v5 on v4

--- a/solution.py
+++ b/solution.py
@@ -16,7 +16,8 @@
 BF16 = jnp.bfloat16
 HIGHEST = lax.Precision.HIGHEST
 VMEM_LIMIT = 12 * 1024 * 1024
-STAGE_LIMIT = 12 * 1024 * 1024
+SUMS_LIMIT = 24 * 1024 * 1024
+LINES_AT_ONCE = 8
 
 
 def cas_table(count):
@@ -44,16 +45,23 @@
     return jnp.concatenate(parts, axis=0)
 
 
-def stage_kernel(orb_hbm, orb_ref, left_ref, right_ref, sem):
+def stage_kernel(live_ref, orb_hbm, orb_ref, order_ref, count_ref, sem):
     copy = pltpu.make_async_copy(orb_hbm, orb_ref, sem)
     copy.start()
-
-    def clear(i, carry):
-        left_ref[pl.ds(i * 8, 8)] = jnp.zeros((8, 64, LANES), F32)
-        right_ref[pl.ds(i * 8, 8)] = jnp.zeros((8, 64, LANES), F32)
+    lines = orb_ref.shape[0]
+    for n in range(4):
+        count_ref[n] = 0
+
+    def place(line, carry):
+        n = live_ref[line] - 1
+        order_ref[n, count_ref[n]] = line
+        count_ref[n] += 1
         return carry
 
-    lax.fori_loop(0, left_ref.shape[0] // 8, clear, 0)
+    lax.fori_loop(0, lines, place, 0)
+    for n in range(4):
+        for i in range(LINES_AT_ONCE):
+            order_ref[n, count_ref[n] + i] = lines
     copy.wait()
 
 
@@ -135,48 +143,58 @@
 
 def hamiltonian_kernel(
     pair_ref,
-    live_ref,
+    order_ref,
+    count_ref,
     part_ref,
     orb_ref,
     dens_ref,
     back_ref,
     cas_ref,
-    left_in,
-    right_in,
     pot_ref,
     keep_ref,
     first_ref,
     rest_ref,
     left_ref,
     right_ref,
+    padded_ref,
     *,
-    chunk,
     places,
     chips,
 ):
     lines = dens_ref.shape[0]
 
+    def clear(i, carry):
+        left_ref[pl.ds(i * 8, 8)] = jnp.zeros((8, 64, LANES), F32)
+        right_ref[pl.ds(i * 8, 8)] = jnp.zeros((8, 64, LANES), F32)
+        return carry
+
+    lax.fori_loop(0, left_ref.shape[0] // 8, clear, 0)
     hartree = jnp.dot(cas_ref[...], back_ref[...], precision=HIGHEST, preferred_element_type=F32).T
     dens = dens_ref[...]
-    pot_ref[...] = hartree[:lines] - XC_COEF * jnp.exp(jnp.log(dens * dens + 1.0) * (1.0 / 6.0))
-
-    def body(i, carry):
-        first = i * chunk
-        potential = pot_ref[pl.ds(pl.multiple_of(first, 8), chunk), :]
-        for l in range(chunk):
-            line = first + l
-            phi = masked_line(orb_ref, line, live_ref[line])
-            weighted = (phi.astype(F32) * potential[l : l + 1, :]).astype(BF16)
-            full = lax.dot_general(weighted, phi, (((1,), (1,)), ((), ())), preferred_element_type=F32)
-            for a in range(4):
-                for b in (0, 2):
-                    at = line * 16 + a * 4 + b
-                    both = full[a * 64 : (a + 1) * 64, b * 64 : b * 64 + LANES]
-                    left_ref[pair_ref[at]] += both
-                    right_ref[pair_ref[at + 1]] += both
-        return carry
-
-    lax.fori_loop(0, lines // chunk, body, 0)
+    potential = hartree[:lines] - XC_COEF * jnp.exp(jnp.log(dens * dens + 1.0) * (1.0 / 6.0))
+    pot_ref[...] = potential
+    padded_ref[...] = jnp.concatenate([potential, jnp.zeros((padded_ref.shape[0] - lines, LANES), F32)], axis=0)
+
+    for n in range(1, 5):
+
+        def body(i, carry, n=n):
+            for j in range(LINES_AT_ONCE):
+                entry = order_ref[n - 1, i * LINES_AT_ONCE + j]
+                line = jnp.minimum(entry, lines - 1)
+                rows = orb_ref[line, : n * 64, :]
+                phi = rows if n % 2 == 0 else jnp.concatenate([rows, jnp.zeros((64, LANES), BF16)], axis=0)
+                weighted = (rows.astype(F32) * padded_ref[pl.ds(entry, 1), :]).astype(BF16)
+                full = lax.dot_general(weighted, phi, (((1,), (1,)), ((), ())), preferred_element_type=F32)
+                for a in range(n):
+                    for b in range(0, n, 2):
+                        at = line * 16 + a * 4 + b
+                        both = full[a * 64 : (a + 1) * 64, b * 64 : b * 64 + LANES]
+                        left_ref[pair_ref[at]] += both
+                        if b + 1 < n:
+                            right_ref[pair_ref[at + 1]] += both
+            return carry
+
+        lax.fori_loop(0, (count_ref[n - 1] + LINES_AT_ONCE - 1) // LINES_AT_ONCE, body, 0)
     left_lanes = lax.broadcasted_iota(jnp.int32, (8, 64, LANES), 2) < 64
 
     def emit(base):
@@ -269,18 +287,21 @@
     smem = pl.BlockSpec(memory_space=pltpu.SMEM)
     vmem = pl.BlockSpec(memory_space=pltpu.VMEM)
     params = pltpu.CompilerParams(vmem_limit_bytes=VMEM_LIMIT)
-    sums_shape = jax.ShapeDtypeStruct((2 * block_rows, 64, LANES), F32)
-    orb, left, right = pl.pallas_call(
+    orb, order, count = pl.pallas_call(
         stage_kernel,
-        in_specs=[pl.BlockSpec(memory_space=pl.ANY)],
-        out_specs=[vmem] * 3,
-        out_shape=[jax.ShapeDtypeStruct(orb.shape, BF16), sums_shape, sums_shape],
+        in_specs=[smem, pl.BlockSpec(memory_space=pl.ANY)],
+        out_specs=[vmem, smem, smem],
+        out_shape=[
+            jax.ShapeDtypeStruct(orb.shape, BF16),
+            jax.ShapeDtypeStruct((4, lines + LINES_AT_ONCE), jnp.int32),
+            jax.ShapeDtypeStruct((4,), jnp.int32),
+        ],
         scratch_shapes=[pltpu.SemaphoreType.DMA(())],
-        compiler_params=pltpu.CompilerParams(vmem_limit_bytes=STAGE_LIMIT),
+        compiler_params=params,
         name="stage",
-    )(orb)
-    second, near, table_index, live, part, pairs, orb, left, right = lax.optimization_barrier(
-        (second, near, table_index, live, part, pairs, orb, left, right)
+    )(live, orb)
+    second, near, table_index, live, part, pairs, orb, order, count = lax.optimization_barrier(
+        (second, near, table_index, live, part, pairs, orb, order, count)
     )
     pieces = [whole_chip]
     for piece in (second, near, onward(second, 1), onward(second[:half], 2)):
@@ -322,22 +343,24 @@
     returned = exchange(solved)
 
     half_rows = block_rows // 2
-    potential, keep, give_first, give_rest, _, _ = pl.pallas_call(
-        functools.partial(hamiltonian_kernel, chunk=chunk, places=sum_places, chips=chips),
-        in_specs=[smem] * 3 + [vmem] * 6,
-        out_specs=[vmem] * 6,
+    potential, keep, give_first, give_rest = pl.pallas_call(
+        functools.partial(hamiltonian_kernel, places=sum_places, chips=chips),
+        in_specs=[smem] * 4 + [vmem] * 4,
+        out_specs=[vmem] * 4,
         out_shape=[
             jax.ShapeDtypeStruct((lines, line_cells), F32),
             jax.ShapeDtypeStruct((half_rows, 64, LANES), F32),
             jax.ShapeDtypeStruct((3 * share // 2, 64, LANES), BF16),
             jax.ShapeDtypeStruct((half_rows - 3 * share // 2, 64, LANES), BF16),
-            sums_shape,
-            sums_shape,
         ],
-        input_output_aliases={7: 4, 8: 5},
-        compiler_params=params,
+        scratch_shapes=[
+            pltpu.VMEM((2 * block_rows, 64, LANES), F32),
+            pltpu.VMEM((2 * block_rows, 64, LANES), F32),
+            pltpu.VMEM((lines + 8, LANES), F32),
+        ],
+        compiler_params=pltpu.CompilerParams(vmem_limit_bytes=SUMS_LIMIT),
         name="hamiltonian",
-    )(pairs, live, part, orb, density, returned, jnp.asarray(cas_y2), left, right)
+    )(pairs, order, count, part, orb, density, returned, jnp.asarray(cas_y2))
 
     got_first = across(give_first)
     got_rest = across(lax.optimization_barrier((give_rest, got_first))[0])

time: 119 us -> 120 us (level)
  Pallas kernels: 20.5 us -> 22.7 us
  starting transfers between devices: 29 us -> 27.3 us
    pallas_call x2, Pallas kernels: 11.2 us -> 12.9 us  [the longest x1 9.76 us: per_device(): pl.pallas_call(functools.partial(hamiltonian_kernel, places=sum_places, c...]
    ppermute x11, starting transfers between devices: 16.7 us -> 15.2 us  [onward(): lax.ppermute(values, 'height', [(h, target(h)) for h in range(heights)])]
  transfers between devices with their start and end apart: 18 -> 18, of which waited for: 12 -> 12; matrix products, arithmetic and copies ran while one was open for 2% -> 2% of each run, Pallas kernels for 1% -> 3%
where the time goes in v5:
time: 120 us
  blocking collectives  41.7 us (35%)
  starting transfers between devices  27.3 us (23%)
  Pallas kernels  22.7 us (19%)
  waiting for transfers between devices  20.8 us (17%)
  local copies, waits for them, and re-layouts  6.06 us (5%)
    all_to_all x2, blocking collectives, exchange(): lax.all_to_all(values.reshape(devices, 1, LANES), ('col', 'height'), spli...  41.7 us
    ppermute x11, waiting for transfers between devices, onward(): lax.ppermute(values, 'height', [(h, target(h)) for h in range(heights)])  16.4 us
    ppermute x11, starting transfers between devices, onward(): lax.ppermute(values, 'height', [(h, target(h)) for h in range(heights)])  15.2 us
    ppermute x7, starting transfers between devices, across(): return lax.ppermute(values, 'height', twin)  12.1 us
    pallas_call x1, Pallas kernels, per_device(): pl.pallas_call(functools.partial(hamiltonian_kernel, places=sum_places, c...  9.76 us
    pallas_call x1, Pallas kernels, per_device(): pl.pallas_call(functools.partial(density_kernel, chunk=chunk, places=gath...  7.04 us
    unnamed x18, local copies, waits for them, and re-layouts  4.78 us
    ppermute x7, waiting for transfers between devices, across(): return lax.ppermute(values, 'height', twin)  4.37 us
  transfers between devices with their start and end apart: 18, of which 12 were waited for; matrix products, arithmetic and copies ran while one was open for 2% of the time, Pallas kernels for 3%

profile of v5, /device:TPU:1, one launch (start us, length us, event | category | flops | bytes accessed | tf_op | source)
XLA Modules:
  0.0 120.0 jit_solution(16970508969128379513)
XLA Ops:
  1.7 3.3 %collective-permute-start = (bf16[8,64,128]{2,1,0:T(8,128)(2,1)S(1)}, bf16[8,64,128]{2,1,0:T(8,128)(2,1)S(1)}, u32[]{:S(2)}, u32[]{:S(2)}) collective-permute-start(bf16[8,64,128]{2,1,0:T(8,128)(2,1)S(1)} %pad_maximum_fusion.1), channel_id=1, source_target_pairs={{0,1},{1,0},{2,3},{3,2},{4,5},{5,4},{6,7},{7,6},{8,9},{9,8},{10,11... | collective-permute-start | bytes 393224 | tf_op jit(solution)/shard_map/ppermute | solution.py:261
  6.2 3.9 %collective-permute-start.2 = (bf16[16,64,128]{2,1,0:T(8,128)(2,1)S(1)}, bf16[16,64,128]{2,1,0:T(8,128)(2,1)S(1)}, u32[]{:S(2)}, u32[]{:S(2)}) collective-permute-start(bf16[16,64,128]{2,1,0:T(8,128)(2,1)S(1)} %pad_maximum_fusion.refs_0_), channel_id=1, source_target_pairs={{0,2},{1,15},{2,4},{3,1},{4,6},{5,3},{6,8},{7,5},{8,10},{9,7},{10,... | collective-permute-start | bytes 786440 | tf_op jit(solution)/shard_map/ppermute | solution.py:268
  10.1 1.2 collective-permute-start.1
  12.2 1.2 copy.16
  13.6 2.8 %copy-done = bf16[12,8,256,128]{3,2,1,0:T(8,128)(2,1)S(1)} copy-done((bf16[12,8,256,128]{3,2,1,0:T(8,128)(2,1)S(1)}, bf16[12,8,256,128]{3,2,1,0:T(8,128)(2,1)}, u32[]{:S(2)}) %copy-start) | copy-done | bytes 6291480
  16.4 3.1 %stage.1 = (bf16[96,256,128]{2,1,0:T(8,128)(2,1)S(1)}, s32[4,104]{1,0:T(4,128)S(1)}, s32[4]{0:T(128)S(1)}) custom-call(s32[96]{0:T(128)S(1)} %reshape.29.live_ref, bf16[96,256,128]{2,1,0:T(8,128)(2,1)S(1)} %bitcast.13), custom_call_target="tpu_custom_call" | custom-call | tf_op jit(solution)/shard_map/stage/pallas_call | solution.py:290
  19.5 1.5 %collective-permute-start.5 = (bf16[16,64,128]{2,1,0:T(8,128)(2,1)S(1)}, bf16[16,64,128]{2,1,0:T(8,128)(2,1)S(1)}, u32[]{:S(2)}, u32[]{:S(2)}) collective-permute-start(bf16[16,64,128]{2,1,0:T(8,128)(2,1)S(1)} %collective-permute-done.1.refs_1_), channel_id=1, source_target_pairs={{0,2},{1,15},{2,4},{3,1},{4,6},{5,3},{6,8},{7,5},{8,10},{9,7},{10,... | collective-permute-start | bytes 786440 | tf_op jit(solution)/shard_map/ppermute | solution.py:268
  21.1 2.1 %collective-permute-start.7 = (bf16[8,64,128]{2,1,0:T(8,128)(2,1)S(1)}, bf16[8,64,128]{2,1,0:T(8,128)(2,1)S(1)}, u32[]{:S(2)}, u32[]{:S(2)}) collective-permute-start(bf16[8,64,128]{2,1,0:T(8,128)(2,1)S(1)} %slice.53), channel_id=1, source_target_pairs={{0,4},{1,13},{2,6},{3,15},{4,8},{5,1},{6,10},{7,3},{8,12},{9,5},{1... | collective-permute-start | bytes 393224 | tf_op jit(solution)/shard_map/ppermute | solution.py:268
  23.7 1.4 %collective-permute-done.5.refs_5_ = bf16[16,64,128]{2,1,0:T(8,128)(2,1)S(1)} collective-permute-done((bf16[16,64,128]{2,1,0:T(8,128)(2,1)S(1)}, bf16[16,64,128]{2,1,0:T(8,128)(2,1)S(1)}, u32[]{:S(2)}, u32[]{:S(2)}) %collective-permute-start.5) | collective-permute-done | bytes 262176 | tf_op jit(solution)/shard_map/ppermute | solution.py:268
  25.1 2.4 %collective-permute-start.6 = (bf16[16,64,128]{2,1,0:T(8,128)(2,1)S(1)}, bf16[16,64,128]{2,1,0:T(8,128)(2,1)S(1)}, u32[]{:S(2)}, u32[]{:S(2)}) collective-permute-start(bf16[16,64,128]{2,1,0:T(8,128)(2,1)S(1)} %collective-permute-done.5.refs_5_), channel_id=1, source_target_pairs={{0,1},{1,0},{2,3},{3,2},{4,5},{5,4},{6,7},{7,6},{8,9},{9,8},{10,11... | collective-permute-start | bytes 786440 | tf_op jit(solution)/shard_map/ppermute | solution.py:261
  27.6 4.1 %collective-permute-start.8 = (bf16[8,64,128]{2,1,0:T(8,128)(2,1)S(1)}, bf16[8,64,128]{2,1,0:T(8,128)(2,1)S(1)}, u32[]{:S(2)}, u32[]{:S(2)}) collective-permute-start(bf16[8,64,128]{2,1,0:T(8,128)(2,1)S(1)} %collective-permute-done.7.refs_7_), channel_id=1, source_target_pairs={{0,1},{1,0},{2,3},{3,2},{4,5},{5,4},{6,7},{7,6},{8,9},{9,8},{10,11... | collective-permute-start | bytes 393224 | tf_op jit(solution)/shard_map/ppermute | solution.py:261
  32.8 7.0 %density.1 = (f32[96,128]{1,0:T(8,128)S(1)}, f32[256,128]{1,0:T(8,128)S(1)}) custom-call(s32[1536]{0:T(1024)S(1)} %fusion.3.index_ref, s32[96]{0:T(128)S(1)} %reshape.29.live_ref, s32[3]{0:T(128)S(1)} %pad_add_fusion.part_ref.refs_0_, bf16[96,256,128]{2,1,0:T(8,128)(2,1)S(1)} %get-tuple-element.37.orb_ref, bf16[16,64,128]{2,1,0:T(8,128)(2,1)S(1)} %pad_maximum_fusion.refs_0_, ...), custom_call_target="tpu_custom_call" | custom-call | tf_op jit(solution)/shard_map/density/pallas_call | solution.py:309
  39.8 23.1 %all_to_all.10 = f32[256,1,128]{2,1,0:T(1,128)S(1)} all-to-all(f32[256,1,128]{2,1,0:T(1,128)S(1)} %bitcast.17), channel_id=1, replica_groups=mesh['col'=16,'height'=16] {'col','height'}, dimensions={0} | all-to-all | bytes 262144 | tf_op jit(solution)/shard_map/all_to_all | solution.py:323
  63.0 1.8 %solve.1 = f32[256,128]{1,0:T(8,128)S(1)} custom-call(s32[3]{0:T(128)S(1)} %pad_add_fusion.part_ref.refs_0_, f32[256,128]{1,0:T(8,128)S(1)} %bitcast.15, f32[2,96,192]{2,1,0:T(8,128)S(1)} %copy-done.3, f32[2,192,96]{2,1,0:T(8,128)S(1)} %copy-done.2, f32[128,128]{1,0:T(8,128)S(1)} %copy-done.5, f32[2,96,128]{2,1,0:T(8,128)S(1)} %copy-done.4, ...), custom_call_target="tpu_custom_call" | custom-call | tf_op jit(solution)/shard_map/solve/pallas_call | solution.py:326
  64.8 18.6 %all_to_all.11 = f32[256,1,128]{2,1,0:T(1,128)S(1)} all-to-all(f32[256,1,128]{2,1,0:T(1,128)S(1)} %bitcast.16), channel_id=1, replica_groups=mesh['col'=16,'height'=16] {'col','height'}, dimensions={0} | all-to-all | bytes 262144 | tf_op jit(solution)/shard_map/all_to_all | solution.py:323
  83.4 9.8 %hamiltonian.1 = (f32[96,128]{1,0:T(8,128)}, f32[64,64,128]{2,1,0:T(8,128)S(1)}, bf16[24,64,128]{2,1,0:T(8,128)(2,1)S(1)}, bf16[40,64,128]{2,1,0:T(8,128)(2,1)S(1)}) custom-call(s32[1536]{0:T(1024)S(1)} %reshape.28.pair_ref, s32[4,104]{1,0:T(4,128)S(1)} %get-tuple-element.34.order_ref, s32[4]{0:T(128)S(1)} %get-tuple-element.35.count_ref, ...), custom_call_target="tpu_custom_call" | custom-call | tf_op jit(solution)/shard_map/hamiltonian/pallas_call | solution.py:346
  93.2 1.4 %collective-permute-start.9 = (bf16[24,64,128]{2,1,0:T(8,128)(2,1)S(1)}, bf16[24,64,128]{2,1,0:T(8,128)(2,1)S(1)}, u32[]{:S(2)}, u32[]{:S(2)}) collective-permute-start(bf16[24,64,128]{2,1,0:T(8,128)(2,1)S(1)} %get-tuple-element.47), channel_id=1, source_target_pairs={{0,1},{1,0},{2,3},{3,2},{4,5},{5,4},{6,7},{7,6},{8,9},{9,8},{10,11... | collective-permute-start | bytes 1179656 | tf_op jit(solution)/shard_map/ppermute | solution.py:261
  94.5 1.3 %collective-permute-done.9 = bf16[24,64,128]{2,1,0:T(8,128)(2,1)S(1)} collective-permute-done((bf16[24,64,128]{2,1,0:T(8,128)(2,1)S(1)}, bf16[24,64,128]{2,1,0:T(8,128)(2,1)S(1)}, u32[]{:S(2)}, u32[]{:S(2)}) %collective-permute-start.9) | collective-permute-done | bytes 393248 | tf_op jit(solution)/shard_map/ppermute | solution.py:261
  97.0 1.0 collective-permute-done.10.got_ref
  98.1 2.2 %collective-permute-done.12 = bf16[8,64,128]{2,1,0:T(8,128)(2,1)S(1)} collective-permute-done((bf16[8,64,128]{2,1,0:T(8,128)(2,1)S(1)}, bf16[8,64,128]{2,1,0:T(8,128)(2,1)S(1)}, u32[]{:S(2)}, u32[]{:S(2)}) %collective-permute-start.12) | collective-permute-done | bytes 131104 | tf_op jit(solution)/shard_map/ppermute | solution.py:268
  100.3 3.7 %collective-permute-done.13 = bf16[8,64,128]{2,1,0:T(8,128)(2,1)S(1)} collective-permute-done((bf16[8,64,128]{2,1,0:T(8,128)(2,1)S(1)}, bf16[8,64,128]{2,1,0:T(8,128)(2,1)S(1)}, u32[]{:S(2)}, u32[]{:S(2)}) %collective-permute-start.13) | collective-permute-done | bytes 131104 | tf_op jit(solution)/shard_map/ppermute | solution.py:268
  105.4 5.5 %collective-permute-start.17 = (bf16[8,64,128]{2,1,0:T(8,128)(2,1)S(1)}, bf16[8,64,128]{2,1,0:T(8,128)(2,1)S(1)}, u32[]{:S(2)}, u32[]{:S(2)}) collective-permute-start(bf16[8,64,128]{2,1,0:T(8,128)(2,1)S(1)} %add_convert_fusion.1), channel_id=1, source_target_pairs={{0,5},{1,12},{2,7},{3,14},{4,9},{5,0},{6,11},{7,2},{8,13},{9,4},{1... | collective-permute-start | bytes 393224 | tf_op jit(solution)/shard_map/ppermute | solution.py:268
  111.0 6.8 %collective-permute-done.17.twin_two_ref = bf16[8,64,128]{2,1,0:T(8,128)(2,1)S(1)} collective-permute-done((bf16[8,64,128]{2,1,0:T(8,128)(2,1)S(1)}, bf16[8,64,128]{2,1,0:T(8,128)(2,1)S(1)}, u32[]{:S(2)}, u32[]{:S(2)}) %collective-permute-start.17) | collective-permute-done | bytes 131104 | tf_op jit(solution)/shard_map/ppermute | solution.py:268
  117.8 1.3 %collective-permute-done.16.twin_one_ref = bf16[8,64,128]{2,1,0:T(8,128)(2,1)S(1)} collective-permute-done((bf16[8,64,128]{2,1,0:T(8,128)(2,1)S(1)}, bf16[8,64,128]{2,1,0:T(8,128)(2,1)S(1)}, u32[]{:S(2)}, u32[]{:S(2)}) %collective-permute-start.16) | collective-permute-done | bytes 131104 | tf_op jit(solution)/shard_map/ppermute | solution.py:268
  (49 shorter events, 8.6 us)
Async XLA Ops:
  1.7 4.3 %collective-permute-start = (bf16[8,64,128]{2,1,0:T(8,128)(2,1)S(1)}, bf16[8,64,128]{2,1,0:T(8,128)(2,1)S(1)}, u32[]{:S(2)}, u32[]{:S(2)}) collective-permute-start(bf16[8,64,128]{2,1,0:T(8,128)(2,1)S(1)} %pad_maximum_fusion.1), channel_id=1, source_target_pairs={{0,1},{1,0},{2,3},{3,2},{4,5},{5,4},{6,7},{7,6},{8,9},{9,8},{10,11... | collective-permute-start | bytes 393224 | tf_op jit(solution)/shard_map/ppermute | solution.py:261
  6.2 13.4 %collective-permute-start.2 = (bf16[16,64,128]{2,1,0:T(8,128)(2,1)S(1)}, bf16[16,64,128]{2,1,0:T(8,128)(2,1)S(1)}, u32[]{:S(2)}, u32[]{:S(2)}) collective-permute-start(bf16[16,64,128]{2,1,0:T(8,128)(2,1)S(1)} %pad_maximum_fusion.refs_0_), channel_id=1, source_target_pairs={{0,2},{1,15},{2,4},{3,1},{4,6},{5,3},{6,8},{7,5},{8,10},{9,7},{10,... | collective-permute-start | bytes 786440 | tf_op jit(solution)/shard_map/ppermute | solution.py:268
  10.1 9.5 %collective-permute-start.1 = (bf16[16,64,128]{2,1,0:T(8,128)(2,1)S(1)}, bf16[16,64,128]{2,1,0:T(8,128)(2,1)S(1)}, u32[]{:S(2)}, u32[]{:S(2)}) collective-permute-start(bf16[16,64,128]{2,1,0:T(8,128)(2,1)S(1)} %pad_maximum_fusion.refs_0_), channel_id=1, source_target_pairs={{0,4},{1,13},{2,6},{3,15},{4,8},{5,1},{6,10},{7,3},{8,12},{9,5},{1... | collective-permute-start | bytes 786440 | tf_op jit(solution)/shard_map/ppermute | solution.py:268
  19.5 5.6 %collective-permute-start.5 = (bf16[16,64,128]{2,1,0:T(8,128)(2,1)S(1)}, bf16[16,64,128]{2,1,0:T(8,128)(2,1)S(1)}, u32[]{:S(2)}, u32[]{:S(2)}) collective-permute-start(bf16[16,64,128]{2,1,0:T(8,128)(2,1)S(1)} %collective-permute-done.1.refs_1_), channel_id=1, source_target_pairs={{0,2},{1,15},{2,4},{3,1},{4,6},{5,3},{6,8},{7,5},{8,10},{9,7},{10,... | collective-permute-start | bytes 786440 | tf_op jit(solution)/shard_map/ppermute | solution.py:268
  21.1 41.9 %copy-start.2 = (f32[2,192,96]{2,1,0:T(8,128)S(1)}, f32[2,192,96]{2,1,0:T(8,128)}, u32[]{:S(2)}) copy-start(f32[2,192,96]{2,1,0:T(8,128)} %constant.99.clone.refs_3_) | copy-start | bytes 442372
  21.1 41.9 %copy-start.3 = (f32[2,96,192]{2,1,0:T(8,128)S(1)}, f32[2,96,192]{2,1,0:T(8,128)}, u32[]{:S(2)}) copy-start(f32[2,96,192]{2,1,0:T(8,128)} %constant.98.clone.refs_2_) | copy-start | bytes 442372
  21.1 41.9 %copy-start.4 = (f32[2,96,128]{2,1,0:T(8,128)S(1)}, f32[2,96,128]{2,1,0:T(8,128)}, u32[]{:S(2)}) copy-start(f32[2,96,128]{2,1,0:T(8,128)} %constant.101.clone.refs_5_) | copy-start | bytes 294916
  21.1 41.9 %copy-start.5 = (f32[128,128]{1,0:T(8,128)S(1)}, f32[128,128]{1,0:T(8,128)}, u32[]{:S(2)}) copy-start(f32[128,128]{1,0:T(8,128)} %constant.100.clone.refs_4_) | copy-start | bytes 196612
  21.1 41.8 %copy-start.6 = (f32[128]{0:T(128)S(1)}, f32[128]{0:T(128)}, u32[]{:S(2)}) copy-start(f32[128]{0:T(128)} %constant.103.clone.refs_7_) | copy-start | bytes 1540
  21.1 41.8 %copy-start.7 = (f32[1,128]{1,0:T(1,128)S(1)}, f32[1,128]{1,0:T(1,128)}, u32[]{:S(2)}) copy-start(f32[1,128]{1,0:T(1,128)} %constant.102.clone.refs_6_) | copy-start | bytes 1540
  21.1 6.5 %collective-permute-start.7 = (bf16[8,64,128]{2,1,0:T(8,128)(2,1)S(1)}, bf16[8,64,128]{2,1,0:T(8,128)(2,1)S(1)}, u32[]{:S(2)}, u32[]{:S(2)}) collective-permute-start(bf16[8,64,128]{2,1,0:T(8,128)(2,1)S(1)} %slice.53), channel_id=1, source_target_pairs={{0,4},{1,13},{2,6},{3,15},{4,8},{5,1},{6,10},{7,3},{8,12},{9,5},{1... | collective-permute-start | bytes 393224 | tf_op jit(solution)/shard_map/ppermute | solution.py:268
  23.2 9.6 %collective-permute-start.3 = (bf16[16,64,128]{2,1,0:T(8,128)(2,1)S(1)}, bf16[16,64,128]{2,1,0:T(8,128)(2,1)S(1)}, u32[]{:S(2)}, u32[]{:S(2)}) collective-permute-start(bf16[16,64,128]{2,1,0:T(8,128)(2,1)S(1)} %collective-permute-done.1.refs_1_), channel_id=1, source_target_pairs={{0,1},{1,0},{2,3},{3,2},{4,5},{5,4},{6,7},{7,6},{8,9},{9,8},{10,11... | collective-permute-start | bytes 786440 | tf_op jit(solution)/shard_map/ppermute | solution.py:261
  23.2 9.6 %collective-permute-start.4 = (bf16[16,64,128]{2,1,0:T(8,128)(2,1)S(1)}, bf16[16,64,128]{2,1,0:T(8,128)(2,1)S(1)}, u32[]{:S(2)}, u32[]{:S(2)}) collective-permute-start(bf16[16,64,128]{2,1,0:T(8,128)(2,1)S(1)} %collective-permute-done.2.refs_3_), channel_id=1, source_target_pairs={{0,1},{1,0},{2,3},{3,2},{4,5},{5,4},{6,7},{7,6},{8,9},{9,8},{10,11... | collective-permute-start | bytes 786440 | tf_op jit(solution)/shard_map/ppermute | solution.py:261
  25.1 7.6 %collective-permute-start.6 = (bf16[16,64,128]{2,1,0:T(8,128)(2,1)S(1)}, bf16[16,64,128]{2,1,0:T(8,128)(2,1)S(1)}, u32[]{:S(2)}, u32[]{:S(2)}) collective-permute-start(bf16[16,64,128]{2,1,0:T(8,128)(2,1)S(1)} %collective-permute-done.5.refs_5_), channel_id=1, source_target_pairs={{0,1},{1,0},{2,3},{3,2},{4,5},{5,4},{6,7},{7,6},{8,9},{9,8},{10,11... | collective-permute-start | bytes 786440 | tf_op jit(solution)/shard_map/ppermute | solution.py:261
  27.6 5.1 %collective-permute-start.8 = (bf16[8,64,128]{2,1,0:T(8,128)(2,1)S(1)}, bf16[8,64,128]{2,1,0:T(8,128)(2,1)S(1)}, u32[]{:S(2)}, u32[]{:S(2)}) collective-permute-start(bf16[8,64,128]{2,1,0:T(8,128)(2,1)S(1)} %collective-permute-done.7.refs_7_), channel_id=1, source_target_pairs={{0,1},{1,0},{2,3},{3,2},{4,5},{5,4},{6,7},{7,6},{8,9},{9,8},{10,11... | collective-permute-start | bytes 393224 | tf_op jit(solution)/shard_map/ppermute | solution.py:261
  93.2 2.7 %collective-permute-start.9 = (bf16[24,64,128]{2,1,0:T(8,128)(2,1)S(1)}, bf16[24,64,128]{2,1,0:T(8,128)(2,1)S(1)}, u32[]{:S(2)}, u32[]{:S(2)}) collective-permute-start(bf16[24,64,128]{2,1,0:T(8,128)(2,1)S(1)} %get-tuple-element.47), channel_id=1, source_target_pairs={{0,1},{1,0},{2,3},{3,2},{4,5},{5,4},{6,7},{7,6},{8,9},{9,8},{10,11... | collective-permute-start | bytes 1179656 | tf_op jit(solution)/shard_map/ppermute | solution.py:261
  95.9 2.1 %collective-permute-start.10 = (bf16[40,64,128]{2,1,0:T(8,128)(2,1)S(1)}, bf16[40,64,128]{2,1,0:T(8,128)(2,1)S(1)}, u32[]{:S(2)}, u32[]{:S(2)}) collective-permute-start(bf16[40,64,128]{2,1,0:T(8,128)(2,1)S(1)} %get-tuple-element.48), channel_id=1, source_target_pairs={{0,1},{1,0},{2,3},{3,2},{4,5},{5,4},{6,7},{7,6},{8,9},{9,8},{10,11... | collective-permute-start | bytes 1966088 | tf_op jit(solution)/shard_map/ppermute | solution.py:261
  96.4 3.9 %collective-permute-start.12 = (bf16[8,64,128]{2,1,0:T(8,128)(2,1)S(1)}, bf16[8,64,128]{2,1,0:T(8,128)(2,1)S(1)}, u32[]{:S(2)}, u32[]{:S(2)}) collective-permute-start(bf16[8,64,128]{2,1,0:T(8,128)(2,1)S(1)} %get-tuple-element.52), channel_id=1, source_target_pairs={{0,2},{1,15},{2,4},{3,1},{4,6},{5,3},{6,8},{7,5},{8,10},{9,7},{10,... | collective-permute-start | bytes 393224 | tf_op jit(solution)/shard_map/ppermute | solution.py:268
  96.5 7.6 %collective-permute-start.13 = (bf16[8,64,128]{2,1,0:T(8,128)(2,1)S(1)}, bf16[8,64,128]{2,1,0:T(8,128)(2,1)S(1)}, u32[]{:S(2)}, u32[]{:S(2)}) collective-permute-start(bf16[8,64,128]{2,1,0:T(8,128)(2,1)S(1)} %get-tuple-element.54), channel_id=1, source_target_pairs={{0,4},{1,13},{2,6},{3,15},{4,8},{5,1},{6,10},{7,3},{8,12},{9,5},{1... | collective-permute-start | bytes 393224 | tf_op jit(solution)/shard_map/ppermute | solution.py:268
  96.6 8.2 %collective-permute-start.14 = (bf16[8,64,128]{2,1,0:T(8,128)(2,1)S(1)}, bf16[8,64,128]{2,1,0:T(8,128)(2,1)S(1)}, u32[]{:S(2)}, u32[]{:S(2)}) collective-permute-start(bf16[8,64,128]{2,1,0:T(8,128)(2,1)S(1)} %get-tuple-element.55), channel_id=1, source_target_pairs={{0,2},{1,15},{2,4},{3,1},{4,6},{5,3},{6,8},{7,5},{8,10},{9,7},{10,... | collective-permute-start | bytes 393224 | tf_op jit(solution)/shard_map/ppermute | solution.py:268
  104.9 6.1 %collective-permute-start.15 = (bf16[8,64,128]{2,1,0:T(8,128)(2,1)S(1)}, bf16[8,64,128]{2,1,0:T(8,128)(2,1)S(1)}, u32[]{:S(2)}, u32[]{:S(2)}) collective-permute-start(bf16[8,64,128]{2,1,0:T(8,128)(2,1)S(1)} %add_convert_fusion), channel_id=1, source_target_pairs={{0,4},{1,13},{2,6},{3,15},{4,8},{5,1},{6,10},{7,3},{8,12},{9,5},{1... | collective-permute-start | bytes 393224 | tf_op jit(solution)/shard_map/ppermute | solution.py:268
  105.4 12.4 %collective-permute-start.17 = (bf16[8,64,128]{2,1,0:T(8,128)(2,1)S(1)}, bf16[8,64,128]{2,1,0:T(8,128)(2,1)S(1)}, u32[]{:S(2)}, u32[]{:S(2)}) collective-permute-start(bf16[8,64,128]{2,1,0:T(8,128)(2,1)S(1)} %add_convert_fusion.1), channel_id=1, source_target_pairs={{0,5},{1,12},{2,7},{3,14},{4,9},{5,0},{6,11},{7,2},{8,13},{9,4},{1... | collective-permute-start | bytes 393224 | tf_op jit(solution)/shard_map/ppermute | solution.py:268
  110.9 6.9 %collective-permute-start.11 = (bf16[8,64,128]{2,1,0:T(8,128)(2,1)S(1)}, bf16[8,64,128]{2,1,0:T(8,128)(2,1)S(1)}, u32[]{:S(2)}, u32[]{:S(2)}) collective-permute-start(bf16[8,64,128]{2,1,0:T(8,128)(2,1)S(1)} %get-tuple-element.50), channel_id=1, source_target_pairs={{0,2},{1,15},{2,4},{3,1},{4,6},{5,3},{6,8},{7,5},{8,10},{9,7},{10,... | collective-permute-start | bytes 393224 | tf_op jit(solution)/shard_map/ppermute | solution.py:268
  110.9 8.2 %collective-permute-start.16 = (bf16[8,64,128]{2,1,0:T(8,128)(2,1)S(1)}, bf16[8,64,128]{2,1,0:T(8,128)(2,1)S(1)}, u32[]{:S(2)}, u32[]{:S(2)}) collective-permute-start(bf16[8,64,128]{2,1,0:T(8,128)(2,1)S(1)} %get-tuple-element.56), channel_id=1, source_target_pairs={{0,3},{1,14},{2,5},{3,0},{4,7},{5,2},{6,9},{7,4},{8,11},{9,6},{10,... | collective-permute-start | bytes 393224 | tf_op jit(solution)/shard_map/ppermute | solution.py:268
  (2 other events, 19.2 us)

commit v6 on v5

--- a/solution.py
+++ b/solution.py
@@ -16,6 +16,7 @@
 BF16 = jnp.bfloat16
 HIGHEST = lax.Precision.HIGHEST
 VMEM_LIMIT = 12 * 1024 * 1024
+STAGE_LIMIT = 44 * 1024 * 1024
 SUMS_LIMIT = 24 * 1024 * 1024
 LINES_AT_ONCE = 8
 
@@ -269,8 +270,8 @@
 
     half = share // 2
     gather_places = [(0, 0), (0, 1)]
-    for d in (2, 1, 3):
-        gather_places += [(-d, 0), (-d, 1), (d, 1), (d, 0)]
+    gather_places += [(-2, 0), (2, 1), (-2, 1), (2, 0), (-1, 0), (-1, 1), (1, 1), (1, 0)]
+    gather_places += [(-3, 0), (3, 1), (-3, 1), (3, 0)]
     gather_places += [(far, 0), (far, 1)]
     keep_places, give_places = [(far, 0)], [(far, 1)]
     for d in (3, 1, 2):
@@ -281,8 +282,10 @@
     side = jnp.arange(lines * 16, dtype=jnp.int32) % 2
     table_index = (pairs // share) * half + pairs % half
     table_index = table_index + jnp.where((pairs // half) % 2 == side, 0, block_rows)
-    whole_chip = jnp.concatenate([packed, across(packed)], axis=0)
-    second = onward(whole_chip, 2)
+    twin_packed = across(packed)
+    second = onward(packed, 2)
+    second_twin = onward(twin_packed, 2)
+    whole_chip = jnp.concatenate([packed, twin_packed], axis=0)
     near = onward(whole_chip, 1)
     smem = pl.BlockSpec(memory_space=pltpu.SMEM)
     vmem = pl.BlockSpec(memory_space=pltpu.VMEM)
@@ -297,14 +300,16 @@
             jax.ShapeDtypeStruct((4,), jnp.int32),
         ],
         scratch_shapes=[pltpu.SemaphoreType.DMA(())],
-        compiler_params=params,
+        compiler_params=pltpu.CompilerParams(vmem_limit_bytes=STAGE_LIMIT),
         name="stage",
     )(live, orb)
-    second, near, table_index, live, part, pairs, orb, order, count = lax.optimization_barrier(
-        (second, near, table_index, live, part, pairs, orb, order, count)
+    second_twin, near, table_index, live, part, pairs, orb, order, count = lax.optimization_barrier(
+        (second_twin, near, table_index, live, part, pairs, orb, order, count)
     )
+    fourth = onward(second, 2)
+    rest = [onward(second, 1), onward(second_twin, 1)]
     pieces = [whole_chip]
-    for piece in (second, near, onward(second, 1), onward(second[:half], 2)):
+    for piece in (second, second_twin, near, *rest, fourth):
         pieces += [piece, across(piece)]
     density, spectrum = pl.pallas_call(
         functools.partial(density_kernel, chunk=chunk, places=gather_places, chips=chips),

time: 120 us -> 116 us (0.967)
  local copies, waits for them, and re-layouts: 6.06 us -> 2.59 us
  waiting for transfers between devices: 20.8 us -> 17.9 us
  Pallas kernels: 22.7 us -> 24.4 us
  blocking collectives: 41.7 us -> 40.2 us
  starting transfers between devices: 27.3 us -> 28.8 us
    unnamed x18, local copies, waits for them, and re-layouts: 4.78 us -> 1.31 us
    ppermute x11 -> x13, waiting for transfers between devices: 16.4 us -> 14.5 us  [onward(): lax.ppermute(values, 'height', [(h, target(h)) for h in range(heights)])]
    all_to_all x2, blocking collectives: 41.7 us -> 40.2 us  [exchange(): lax.all_to_all(values.reshape(devices, 1, LANES), ('col', 'height'), spli...]
    ppermute x11 -> x13, starting transfers between devices: 15.2 us -> 16.6 us  [onward(): lax.ppermute(values, 'height', [(h, target(h)) for h in range(heights)])]
    ppermute x7 -> x9, waiting for transfers between devices: 4.37 us -> 3.43 us  [across(): return lax.ppermute(values, 'height', twin)]
    ppermute x7 -> x9, starting transfers between devices: 12.1 us -> 12.1 us  [across(): return lax.ppermute(values, 'height', twin)]
  transfers between devices with their start and end apart: 18 -> 22, of which waited for: 12 -> 9; matrix products, arithmetic and copies ran while one was open for 2% -> 2% of each run, Pallas kernels for 3% -> 3%
where the time goes in v6:
time: 116 us; the launch traced here: 115 us
  blocking collectives  40.2 us (35%)
  starting transfers between devices  28.8 us (25%)
  Pallas kernels  24.4 us (21%)
  waiting for transfers between devices  17.9 us (15%)
  local copies, waits for them, and re-layouts  2.59 us (2%)
    all_to_all x2, blocking collectives, exchange(): lax.all_to_all(values.reshape(devices, 1, LANES), ('col', 'height'), spli...  40.2 us
    ppermute x13, starting transfers between devices, onward(): lax.ppermute(values, 'height', [(h, target(h)) for h in range(heights)])  16.6 us
    ppermute x13, waiting for transfers between devices, onward(): lax.ppermute(values, 'height', [(h, target(h)) for h in range(heights)])  14.5 us
    ppermute x9, starting transfers between devices, across(): return lax.ppermute(values, 'height', twin)  12.1 us
    pallas_call x1, Pallas kernels, per_device(): pl.pallas_call(functools.partial(hamiltonian_kernel, places=sum_places, c...  10.7 us
    pallas_call x1, Pallas kernels, per_device(): pl.pallas_call(functools.partial(density_kernel, chunk=chunk, places=gath...  6.99 us
    pallas_call x1, Pallas kernels, per_device(): pl.pallas_call(stage_kernel, in_specs=[smem, pl.BlockSpec(memory_space=pl...  3.96 us
    ppermute x9, waiting for transfers between devices, across(): return lax.ppermute(values, 'height', twin)  3.43 us
  transfers between devices with their start and end apart: 22, of which 9 were waited for; matrix products, arithmetic and copies ran while one was open for 2% of the time, Pallas kernels for 3%

profile of v6, /device:TPU:1, one launch (start us, length us, event | category | flops | bytes accessed | tf_op | source)
XLA Modules:
  0.0 115.4 jit_solution(12881096798978250125)
XLA Ops:
  0.6 1.0 fusion.11
  1.7 3.3 %collective-permute-start = (bf16[8,64,128]{2,1,0:T(8,128)(2,1)S(1)}, bf16[8,64,128]{2,1,0:T(8,128)(2,1)S(1)}, u32[]{:S(2)}, u32[]{:S(2)}) collective-permute-start(bf16[8,64,128]{2,1,0:T(8,128)(2,1)S(1)} %pad_maximum_fusion.1), channel_id=1, source_target_pairs={{0,1},{1,0},{2,3},{3,2},{4,5},{5,4},{6,7},{7,6},{8,9},{9,8},{10,11... | collective-permute-start | bytes 393224 | tf_op jit(solution)/shard_map/ppermute | solution.py:262
  5.1 4.3 %collective-permute-start.3 = (bf16[8,64,128]{2,1,0:T(8,128)(2,1)S(1)}, bf16[8,64,128]{2,1,0:T(8,128)(2,1)S(1)}, u32[]{:S(2)}, u32[]{:S(2)}) collective-permute-start(bf16[8,64,128]{2,1,0:T(8,128)(2,1)S(1)} %pad_maximum_fusion.1), channel_id=1, source_target_pairs={{0,4},{1,13},{2,6},{3,15},{4,8},{5,1},{6,10},{7,3},{8,12},{9,5},{1... | collective-permute-start | bytes 393224 | tf_op jit(solution)/shard_map/ppermute | solution.py:269
  9.4 1.2 %copy.16 = s32[12,8,4,4]{3,2,1,0:T(4,128)S(1)} copy(s32[12,8,4,4]{0,3,2,1:T(4,128)} %param.13) | data formatting | bytes 12288 | tf_op args[2]
  12.5 4.0 %stage.1 = (bf16[96,256,128]{2,1,0:T(8,128)(2,1)S(1)}, s32[4,104]{1,0:T(4,128)S(1)}, s32[4]{0:T(128)S(1)}) custom-call(s32[96]{0:T(128)S(1)} %reshape.29.live_ref, bf16[96,256,128]{2,1,0:T(8,128)(2,1)} %bitcast.17), custom_call_target="tpu_custom_call" | custom-call | tf_op jit(solution)/shard_map/stage/pallas_call | solution.py:293
  17.2 2.5 %collective-permute-start.4 = (bf16[8,64,128]{2,1,0:T(8,128)(2,1)S(1)}, bf16[8,64,128]{2,1,0:T(8,128)(2,1)S(1)}, u32[]{:S(2)}, u32[]{:S(2)}) collective-permute-start(bf16[8,64,128]{2,1,0:T(8,128)(2,1)S(1)} %collective-permute-done.3.refs_1_), channel_id=1, source_target_pairs={{0,1},{1,0},{2,3},{3,2},{4,5},{5,4},{6,7},{7,6},{8,9},{9,8},{10,11... | collective-permute-start | bytes 393224 | tf_op jit(solution)/shard_map/ppermute | solution.py:262
  19.8 2.9 %collective-permute-start.9 = (bf16[8,64,128]{2,1,0:T(8,128)(2,1)S(1)}, bf16[8,64,128]{2,1,0:T(8,128)(2,1)S(1)}, u32[]{:S(2)}, u32[]{:S(2)}) collective-permute-start(bf16[8,64,128]{2,1,0:T(8,128)(2,1)S(1)} %collective-permute-done.1.refs_3_), channel_id=1, source_target_pairs={{0,2},{1,15},{2,4},{3,1},{4,6},{5,3},{6,8},{7,5},{8,10},{9,7},{10,... | collective-permute-start | bytes 393224 | tf_op jit(solution)/shard_map/ppermute | solution.py:269
  22.8 3.6 %collective-permute-start.12 = (bf16[8,64,128]{2,1,0:T(8,128)(2,1)S(1)}, bf16[8,64,128]{2,1,0:T(8,128)(2,1)S(1)}, u32[]{:S(2)}, u32[]{:S(2)}) collective-permute-start(bf16[8,64,128]{2,1,0:T(8,128)(2,1)S(1)} %collective-permute-done.11.refs_11_), channel_id=1, source_target_pairs={{0,1},{1,0},{2,3},{3,2},{4,5},{5,4},{6,7},{7,6},{8,9},{9,8},{10,11... | collective-permute-start | bytes 393224 | tf_op jit(solution)/shard_map/ppermute | solution.py:262
  26.3 1.2 %collective-permute-start.8 = (bf16[8,64,128]{2,1,0:T(8,128)(2,1)S(1)}, bf16[8,64,128]{2,1,0:T(8,128)(2,1)S(1)}, u32[]{:S(2)}, u32[]{:S(2)}) collective-permute-start(bf16[8,64,128]{2,1,0:T(8,128)(2,1)S(1)} %collective-permute-done.7.refs_7_), channel_id=1, source_target_pairs={{0,1},{1,0},{2,3},{3,2},{4,5},{5,4},{6,7},{7,6},{8,9},{9,8},{10,11... | collective-permute-start | bytes 393224 | tf_op jit(solution)/shard_map/ppermute | solution.py:262
  27.6 1.4 %collective-permute-start.10 = (bf16[8,64,128]{2,1,0:T(8,128)(2,1)S(1)}, bf16[8,64,128]{2,1,0:T(8,128)(2,1)S(1)}, u32[]{:S(2)}, u32[]{:S(2)}) collective-permute-start(bf16[8,64,128]{2,1,0:T(8,128)(2,1)S(1)} %collective-permute-done.9.refs_9_), channel_id=1, source_target_pairs={{0,1},{1,0},{2,3},{3,2},{4,5},{5,4},{6,7},{7,6},{8,9},{9,8},{10,11... | collective-permute-start | bytes 393224 | tf_op jit(solution)/shard_map/ppermute | solution.py:262
  29.0 1.0 collective-permute-done.10.refs_10_
  30.0 7.0 %density.1 = (f32[96,128]{1,0:T(8,128)S(1)}, f32[256,128]{1,0:T(8,128)S(1)}) custom-call(s32[1536]{0:T(1024)S(1)} %fusion.3.index_ref, s32[96]{0:T(128)S(1)} %reshape.29.live_ref, s32[3]{0:T(128)S(1)} %pad_add_fusion.part_ref.refs_0_, bf16[96,256,128]{2,1,0:T(8,128)(2,1)S(1)} %get-tuple-element.37.orb_ref, bf16[16,64,128]{2,1,0:T(8,128)(2,1)S(1)} %pad_maximum_fusion.refs_0_, ...), custom_call_target="tpu_custom_call" | custom-call | tf_op jit(solution)/shard_map/density/pallas_call | solution.py:314
  37.0 21.6 %all_to_all.10 = f32[256,1,128]{2,1,0:T(1,128)S(1)} all-to-all(f32[256,1,128]{2,1,0:T(1,128)S(1)} %bitcast.16), channel_id=1, replica_groups=mesh['col'=16,'height'=16] {'col','height'}, dimensions={0} | all-to-all | bytes 262144 | tf_op jit(solution)/shard_map/all_to_all | solution.py:328
  58.6 1.8 %solve.1 = f32[256,128]{1,0:T(8,128)S(1)} custom-call(s32[3]{0:T(128)S(1)} %pad_add_fusion.part_ref.refs_0_, f32[256,128]{1,0:T(8,128)S(1)} %bitcast.14, f32[2,96,192]{2,1,0:T(8,128)S(1)} %copy-done.2, f32[2,192,96]{2,1,0:T(8,128)S(1)} %copy-done.1, f32[128,128]{1,0:T(8,128)S(1)} %copy-done.4, f32[2,96,128]{2,1,0:T(8,128)S(1)} %copy-done.3, ...), custom_call_target="tpu_custom_call" | custom-call | tf_op jit(solution)/shard_map/solve/pallas_call | solution.py:331
  60.4 18.6 %all_to_all.11 = f32[256,1,128]{2,1,0:T(1,128)S(1)} all-to-all(f32[256,1,128]{2,1,0:T(1,128)S(1)} %bitcast.15), channel_id=1, replica_groups=mesh['col'=16,'height'=16] {'col','height'}, dimensions={0} | all-to-all | bytes 262144 | tf_op jit(solution)/shard_map/all_to_all | solution.py:328
  79.0 10.7 %hamiltonian.1 = (f32[96,128]{1,0:T(8,128)}, f32[64,64,128]{2,1,0:T(8,128)S(1)}, bf16[24,64,128]{2,1,0:T(8,128)(2,1)S(1)}, bf16[40,64,128]{2,1,0:T(8,128)(2,1)S(1)}) custom-call(s32[1536]{0:T(1024)S(1)} %reshape.28.pair_ref, s32[4,104]{1,0:T(4,128)S(1)} %get-tuple-element.34.order_ref, s32[4]{0:T(128)S(1)} %get-tuple-element.35.count_ref, ...), custom_call_target="tpu_custom_call" | custom-call | tf_op jit(solution)/shard_map/hamiltonian/pallas_call | solution.py:351
  89.7 1.7 %collective-permute-done.13 = bf16[24,64,128]{2,1,0:T(8,128)(2,1)S(1)} collective-permute-done((bf16[24,64,128]{2,1,0:T(8,128)(2,1)S(1)}, bf16[24,64,128]{2,1,0:T(8,128)(2,1)S(1)}, u32[]{:S(2)}, u32[]{:S(2)}) %collective-permute-start.13) | collective-permute-done | bytes 393248 | tf_op jit(solution)/shard_map/ppermute | solution.py:262
  93.6 2.0 %collective-permute-done.16 = bf16[8,64,128]{2,1,0:T(8,128)(2,1)S(1)} collective-permute-done((bf16[8,64,128]{2,1,0:T(8,128)(2,1)S(1)}, bf16[8,64,128]{2,1,0:T(8,128)(2,1)S(1)}, u32[]{:S(2)}, u32[]{:S(2)}) %collective-permute-start.16) | collective-permute-done | bytes 131104 | tf_op jit(solution)/shard_map/ppermute | solution.py:269
  95.6 3.1 %collective-permute-done.17 = bf16[8,64,128]{2,1,0:T(8,128)(2,1)S(1)} collective-permute-done((bf16[8,64,128]{2,1,0:T(8,128)(2,1)S(1)}, bf16[8,64,128]{2,1,0:T(8,128)(2,1)S(1)}, u32[]{:S(2)}, u32[]{:S(2)}) %collective-permute-start.17) | collective-permute-done | bytes 131104 | tf_op jit(solution)/shard_map/ppermute | solution.py:269
  98.7 1.4 %collective-permute-done.18 = bf16[8,64,128]{2,1,0:T(8,128)(2,1)S(1)} collective-permute-done((bf16[8,64,128]{2,1,0:T(8,128)(2,1)S(1)}, bf16[8,64,128]{2,1,0:T(8,128)(2,1)S(1)}, u32[]{:S(2)}, u32[]{:S(2)}) %collective-permute-start.18) | collective-permute-done | bytes 131104 | tf_op jit(solution)/shard_map/ppermute | solution.py:269
  100.9 5.5 %collective-permute-start.21 = (bf16[8,64,128]{2,1,0:T(8,128)(2,1)S(1)}, bf16[8,64,128]{2,1,0:T(8,128)(2,1)S(1)}, u32[]{:S(2)}, u32[]{:S(2)}) collective-permute-start(bf16[8,64,128]{2,1,0:T(8,128)(2,1)S(1)} %add_convert_fusion.1), channel_id=1, source_target_pairs={{0,5},{1,12},{2,7},{3,14},{4,9},{5,0},{6,11},{7,2},{8,13},{9,4},{1... | collective-permute-start | bytes 393224 | tf_op jit(solution)/shard_map/ppermute | solution.py:269
  106.4 6.9 %collective-permute-done.21.twin_two_ref = bf16[8,64,128]{2,1,0:T(8,128)(2,1)S(1)} collective-permute-done((bf16[8,64,128]{2,1,0:T(8,128)(2,1)S(1)}, bf16[8,64,128]{2,1,0:T(8,128)(2,1)S(1)}, u32[]{:S(2)}, u32[]{:S(2)}) %collective-permute-start.21) | collective-permute-done | bytes 131104 | tf_op jit(solution)/shard_map/ppermute | solution.py:269
  113.3 1.1 collective-permute-done.20.twin_one_ref
  114.4 1.0 finish.1
  (56 shorter events, 6.0 us)
Async XLA Ops:
  1.7 9.0 %collective-permute-start = (bf16[8,64,128]{2,1,0:T(8,128)(2,1)S(1)}, bf16[8,64,128]{2,1,0:T(8,128)(2,1)S(1)}, u32[]{:S(2)}, u32[]{:S(2)}) collective-permute-start(bf16[8,64,128]{2,1,0:T(8,128)(2,1)S(1)} %pad_maximum_fusion.1), channel_id=1, source_target_pairs={{0,1},{1,0},{2,3},{3,2},{4,5},{5,4},{6,7},{7,6},{8,9},{9,8},{10,11... | collective-permute-start | bytes 393224 | tf_op jit(solution)/shard_map/ppermute | solution.py:262
  5.1 11.4 %collective-permute-start.3 = (bf16[8,64,128]{2,1,0:T(8,128)(2,1)S(1)}, bf16[8,64,128]{2,1,0:T(8,128)(2,1)S(1)}, u32[]{:S(2)}, u32[]{:S(2)}) collective-permute-start(bf16[8,64,128]{2,1,0:T(8,128)(2,1)S(1)} %pad_maximum_fusion.1), channel_id=1, source_target_pairs={{0,4},{1,13},{2,6},{3,15},{4,8},{5,1},{6,10},{7,3},{8,12},{9,5},{1... | collective-permute-start | bytes 393224 | tf_op jit(solution)/shard_map/ppermute | solution.py:269
  10.9 8.8 %collective-permute-start.2 = (bf16[16,64,128]{2,1,0:T(8,128)(2,1)S(1)}, bf16[16,64,128]{2,1,0:T(8,128)(2,1)S(1)}, u32[]{:S(2)}, u32[]{:S(2)}) collective-permute-start(bf16[16,64,128]{2,1,0:T(8,128)(2,1)S(1)} %pad_maximum_fusion.refs_0_), channel_id=1, source_target_pairs={{0,2},{1,15},{2,4},{3,1},{4,6},{5,3},{6,8},{7,5},{8,10},{9,7},{10,... | collective-permute-start | bytes 786440 | tf_op jit(solution)/shard_map/ppermute | solution.py:269
  11.7 8.0 %collective-permute-start.1 = (bf16[8,64,128]{2,1,0:T(8,128)(2,1)S(1)}, bf16[8,64,128]{2,1,0:T(8,128)(2,1)S(1)}, u32[]{:S(2)}, u32[]{:S(2)}) collective-permute-start(bf16[8,64,128]{2,1,0:T(8,128)(2,1)S(1)} %collective-permute-done), channel_id=1, source_target_pairs={{0,4},{1,13},{2,6},{3,15},{4,8},{5,1},{6,10},{7,3},{8,12},{9,5},{1... | collective-permute-start | bytes 393224 | tf_op jit(solution)/shard_map/ppermute | solution.py:269
  16.5 6.3 %collective-permute-start.11 = (bf16[8,64,128]{2,1,0:T(8,128)(2,1)S(1)}, bf16[8,64,128]{2,1,0:T(8,128)(2,1)S(1)}, u32[]{:S(2)}, u32[]{:S(2)}) collective-permute-start(bf16[8,64,128]{2,1,0:T(8,128)(2,1)S(1)} %collective-permute-done.3.refs_1_), channel_id=1, source_target_pairs={{0,4},{1,13},{2,6},{3,15},{4,8},{5,1},{6,10},{7,3},{8,12},{9,5},{1... | collective-permute-start | bytes 393224 | tf_op jit(solution)/shard_map/ppermute | solution.py:269
  16.8 9.5 %collective-permute-start.7 = (bf16[8,64,128]{2,1,0:T(8,128)(2,1)S(1)}, bf16[8,64,128]{2,1,0:T(8,128)(2,1)S(1)}, u32[]{:S(2)}, u32[]{:S(2)}) collective-permute-start(bf16[8,64,128]{2,1,0:T(8,128)(2,1)S(1)} %collective-permute-done.3.refs_1_), channel_id=1, source_target_pairs={{0,2},{1,15},{2,4},{3,1},{4,6},{5,3},{6,8},{7,5},{8,10},{9,7},{10,... | collective-permute-start | bytes 393224 | tf_op jit(solution)/shard_map/ppermute | solution.py:269
  17.2 10.3 %collective-permute-start.4 = (bf16[8,64,128]{2,1,0:T(8,128)(2,1)S(1)}, bf16[8,64,128]{2,1,0:T(8,128)(2,1)S(1)}, u32[]{:S(2)}, u32[]{:S(2)}) collective-permute-start(bf16[8,64,128]{2,1,0:T(8,128)(2,1)S(1)} %collective-permute-done.3.refs_1_), channel_id=1, source_target_pairs={{0,1},{1,0},{2,3},{3,2},{4,5},{5,4},{6,7},{7,6},{8,9},{9,8},{10,11... | collective-permute-start | bytes 393224 | tf_op jit(solution)/shard_map/ppermute | solution.py:262
  19.7 38.8 %copy-start.1 = (f32[2,192,96]{2,1,0:T(8,128)S(1)}, f32[2,192,96]{2,1,0:T(8,128)}, u32[]{:S(2)}) copy-start(f32[2,192,96]{2,1,0:T(8,128)} %constant.99.clone.refs_3_) | copy-start | bytes 442372
  19.7 38.8 %copy-start.2 = (f32[2,96,192]{2,1,0:T(8,128)S(1)}, f32[2,96,192]{2,1,0:T(8,128)}, u32[]{:S(2)}) copy-start(f32[2,96,192]{2,1,0:T(8,128)} %constant.98.clone.refs_2_) | copy-start | bytes 442372
  19.8 7.8 %collective-permute-start.9 = (bf16[8,64,128]{2,1,0:T(8,128)(2,1)S(1)}, bf16[8,64,128]{2,1,0:T(8,128)(2,1)S(1)}, u32[]{:S(2)}, u32[]{:S(2)}) collective-permute-start(bf16[8,64,128]{2,1,0:T(8,128)(2,1)S(1)} %collective-permute-done.1.refs_3_), channel_id=1, source_target_pairs={{0,2},{1,15},{2,4},{3,1},{4,6},{5,3},{6,8},{7,5},{8,10},{9,7},{10,... | collective-permute-start | bytes 393224 | tf_op jit(solution)/shard_map/ppermute | solution.py:269
  22.7 7.3 %collective-permute-start.6 = (bf16[16,64,128]{2,1,0:T(8,128)(2,1)S(1)}, bf16[16,64,128]{2,1,0:T(8,128)(2,1)S(1)}, u32[]{:S(2)}, u32[]{:S(2)}) collective-permute-start(bf16[16,64,128]{2,1,0:T(8,128)(2,1)S(1)} %collective-permute-done.2.refs_5_), channel_id=1, source_target_pairs={{0,1},{1,0},{2,3},{3,2},{4,5},{5,4},{6,7},{7,6},{8,9},{9,8},{10,11... | collective-permute-start | bytes 786440 | tf_op jit(solution)/shard_map/ppermute | solution.py:262
  22.8 6.2 %collective-permute-start.12 = (bf16[8,64,128]{2,1,0:T(8,128)(2,1)S(1)}, bf16[8,64,128]{2,1,0:T(8,128)(2,1)S(1)}, u32[]{:S(2)}, u32[]{:S(2)}) collective-permute-start(bf16[8,64,128]{2,1,0:T(8,128)(2,1)S(1)} %collective-permute-done.11.refs_11_), channel_id=1, source_target_pairs={{0,1},{1,0},{2,3},{3,2},{4,5},{5,4},{6,7},{7,6},{8,9},{9,8},{10,11... | collective-permute-start | bytes 393224 | tf_op jit(solution)/shard_map/ppermute | solution.py:262
  26.3 2.6 %collective-permute-start.8 = (bf16[8,64,128]{2,1,0:T(8,128)(2,1)S(1)}, bf16[8,64,128]{2,1,0:T(8,128)(2,1)S(1)}, u32[]{:S(2)}, u32[]{:S(2)}) collective-permute-start(bf16[8,64,128]{2,1,0:T(8,128)(2,1)S(1)} %collective-permute-done.7.refs_7_), channel_id=1, source_target_pairs={{0,1},{1,0},{2,3},{3,2},{4,5},{5,4},{6,7},{7,6},{8,9},{9,8},{10,11... | collective-permute-start | bytes 393224 | tf_op jit(solution)/shard_map/ppermute | solution.py:262
  27.6 1.4 %collective-permute-start.5 = (bf16[8,64,128]{2,1,0:T(8,128)(2,1)S(1)}, bf16[8,64,128]{2,1,0:T(8,128)(2,1)S(1)}, u32[]{:S(2)}, u32[]{:S(2)}) collective-permute-start(bf16[8,64,128]{2,1,0:T(8,128)(2,1)S(1)} %collective-permute-done.1.refs_3_), channel_id=1, source_target_pairs={{0,1},{1,0},{2,3},{3,2},{4,5},{5,4},{6,7},{7,6},{8,9},{9,8},{10,11... | collective-permute-start | bytes 393224 | tf_op jit(solution)/shard_map/ppermute | solution.py:262
  27.6 2.4 %collective-permute-start.10 = (bf16[8,64,128]{2,1,0:T(8,128)(2,1)S(1)}, bf16[8,64,128]{2,1,0:T(8,128)(2,1)S(1)}, u32[]{:S(2)}, u32[]{:S(2)}) collective-permute-start(bf16[8,64,128]{2,1,0:T(8,128)(2,1)S(1)} %collective-permute-done.9.refs_9_), channel_id=1, source_target_pairs={{0,1},{1,0},{2,3},{3,2},{4,5},{5,4},{6,7},{7,6},{8,9},{9,8},{10,11... | collective-permute-start | bytes 393224 | tf_op jit(solution)/shard_map/ppermute | solution.py:262
  89.7 1.7 %collective-permute-start.13 = (bf16[24,64,128]{2,1,0:T(8,128)(2,1)S(1)}, bf16[24,64,128]{2,1,0:T(8,128)(2,1)S(1)}, u32[]{:S(2)}, u32[]{:S(2)}) collective-permute-start(bf16[24,64,128]{2,1,0:T(8,128)(2,1)S(1)} %get-tuple-element.47), channel_id=1, source_target_pairs={{0,1},{1,0},{2,3},{3,2},{4,5},{5,4},{6,7},{7,6},{8,9},{9,8},{10,11... | collective-permute-start | bytes 1179656 | tf_op jit(solution)/shard_map/ppermute | solution.py:262
  91.4 2.1 %collective-permute-start.14 = (bf16[40,64,128]{2,1,0:T(8,128)(2,1)S(1)}, bf16[40,64,128]{2,1,0:T(8,128)(2,1)S(1)}, u32[]{:S(2)}, u32[]{:S(2)}) collective-permute-start(bf16[40,64,128]{2,1,0:T(8,128)(2,1)S(1)} %get-tuple-element.48), channel_id=1, source_target_pairs={{0,1},{1,0},{2,3},{3,2},{4,5},{5,4},{6,7},{7,6},{8,9},{9,8},{10,11... | collective-permute-start | bytes 1966088 | tf_op jit(solution)/shard_map/ppermute | solution.py:262
  91.7 3.9 %collective-permute-start.16 = (bf16[8,64,128]{2,1,0:T(8,128)(2,1)S(1)}, bf16[8,64,128]{2,1,0:T(8,128)(2,1)S(1)}, u32[]{:S(2)}, u32[]{:S(2)}) collective-permute-start(bf16[8,64,128]{2,1,0:T(8,128)(2,1)S(1)} %get-tuple-element.52), channel_id=1, source_target_pairs={{0,2},{1,15},{2,4},{3,1},{4,6},{5,3},{6,8},{7,5},{8,10},{9,7},{10,... | collective-permute-start | bytes 393224 | tf_op jit(solution)/shard_map/ppermute | solution.py:269
  91.7 6.9 %collective-permute-start.17 = (bf16[8,64,128]{2,1,0:T(8,128)(2,1)S(1)}, bf16[8,64,128]{2,1,0:T(8,128)(2,1)S(1)}, u32[]{:S(2)}, u32[]{:S(2)}) collective-permute-start(bf16[8,64,128]{2,1,0:T(8,128)(2,1)S(1)} %get-tuple-element.54), channel_id=1, source_target_pairs={{0,4},{1,13},{2,6},{3,15},{4,8},{5,1},{6,10},{7,3},{8,12},{9,5},{1... | collective-permute-start | bytes 393224 | tf_op jit(solution)/shard_map/ppermute | solution.py:269
  92.2 7.9 %collective-permute-start.18 = (bf16[8,64,128]{2,1,0:T(8,128)(2,1)S(1)}, bf16[8,64,128]{2,1,0:T(8,128)(2,1)S(1)}, u32[]{:S(2)}, u32[]{:S(2)}) collective-permute-start(bf16[8,64,128]{2,1,0:T(8,128)(2,1)S(1)} %get-tuple-element.55), channel_id=1, source_target_pairs={{0,2},{1,15},{2,4},{3,1},{4,6},{5,3},{6,8},{7,5},{8,10},{9,7},{10,... | collective-permute-start | bytes 393224 | tf_op jit(solution)/shard_map/ppermute | solution.py:269
  100.1 6.3 %collective-permute-start.19 = (bf16[8,64,128]{2,1,0:T(8,128)(2,1)S(1)}, bf16[8,64,128]{2,1,0:T(8,128)(2,1)S(1)}, u32[]{:S(2)}, u32[]{:S(2)}) collective-permute-start(bf16[8,64,128]{2,1,0:T(8,128)(2,1)S(1)} %add_convert_fusion), channel_id=1, source_target_pairs={{0,4},{1,13},{2,6},{3,15},{4,8},{5,1},{6,10},{7,3},{8,12},{9,5},{1... | collective-permute-start | bytes 393224 | tf_op jit(solution)/shard_map/ppermute | solution.py:269
  100.9 12.3 %collective-permute-start.21 = (bf16[8,64,128]{2,1,0:T(8,128)(2,1)S(1)}, bf16[8,64,128]{2,1,0:T(8,128)(2,1)S(1)}, u32[]{:S(2)}, u32[]{:S(2)}) collective-permute-start(bf16[8,64,128]{2,1,0:T(8,128)(2,1)S(1)} %add_convert_fusion.1), channel_id=1, source_target_pairs={{0,5},{1,12},{2,7},{3,14},{4,9},{5,0},{6,11},{7,2},{8,13},{9,4},{1... | collective-permute-start | bytes 393224 | tf_op jit(solution)/shard_map/ppermute | solution.py:269
  106.4 6.9 %collective-permute-start.15 = (bf16[8,64,128]{2,1,0:T(8,128)(2,1)S(1)}, bf16[8,64,128]{2,1,0:T(8,128)(2,1)S(1)}, u32[]{:S(2)}, u32[]{:S(2)}) collective-permute-start(bf16[8,64,128]{2,1,0:T(8,128)(2,1)S(1)} %get-tuple-element.50), channel_id=1, source_target_pairs={{0,2},{1,15},{2,4},{3,1},{4,6},{5,3},{6,8},{7,5},{8,10},{9,7},{10,... | collective-permute-start | bytes 393224 | tf_op jit(solution)/shard_map/ppermute | solution.py:269
  106.4 8.0 %collective-permute-start.20 = (bf16[8,64,128]{2,1,0:T(8,128)(2,1)S(1)}, bf16[8,64,128]{2,1,0:T(8,128)(2,1)S(1)}, u32[]{:S(2)}, u32[]{:S(2)}) collective-permute-start(bf16[8,64,128]{2,1,0:T(8,128)(2,1)S(1)} %get-tuple-element.56), channel_id=1, source_target_pairs={{0,3},{1,14},{2,5},{3,0},{4,7},{5,2},{6,9},{7,4},{8,11},{9,6},{10,... | collective-permute-start | bytes 393224 | tf_op jit(solution)/shard_map/ppermute | solution.py:269
  (6 other events, 184.4 us)

commit v7 on v6

--- a/solution.py
+++ b/solution.py
@@ -214,7 +214,7 @@
     rows = out_ref.shape[0] // 2
     for i in range(rows):
         total = keep_ref[keep_ref.shape[0] - rows + i] + got_ref[got_ref.shape[0] - rows + i].astype(F32)
-        total = total + one_ref[i].astype(F32) + two_ref[i].astype(F32)
+        total = total + one_ref[rows + i].astype(F32) + two_ref[i].astype(F32)
         total = total + twin_one_ref[i].astype(F32) + twin_two_ref[i].astype(F32)
         out_ref[i] = total[:, :64]
         out_ref[rows + i] = total[:, 64:]
@@ -273,11 +273,8 @@
     gather_places += [(-2, 0), (2, 1), (-2, 1), (2, 0), (-1, 0), (-1, 1), (1, 1), (1, 0)]
     gather_places += [(-3, 0), (3, 1), (-3, 1), (3, 0)]
     gather_places += [(far, 0), (far, 1)]
-    keep_places, give_places = [(far, 0)], [(far, 1)]
-    for d in (3, 1, 2):
-        keep_places += [(d, 0), (d, 1)]
-        give_places += [(-d, 1), (-d, 0)]
-    sum_places = keep_places + [(0, 0)] + give_places + [(0, 1)]
+    keep_places = [(far, 0), (3, 0), (1, 0), (3, 1), (1, 1), (2, 0), (2, 1), (0, 0)]
+    sum_places = keep_places + [(-d, 1 - flip) for d, flip in keep_places]
 
     side = jnp.arange(lines * 16, dtype=jnp.int32) % 2
     table_index = (pairs // share) * half + pairs % half
@@ -355,8 +352,8 @@
         out_shape=[
             jax.ShapeDtypeStruct((lines, line_cells), F32),
             jax.ShapeDtypeStruct((half_rows, 64, LANES), F32),
-            jax.ShapeDtypeStruct((3 * share // 2, 64, LANES), BF16),
-            jax.ShapeDtypeStruct((half_rows - 3 * share // 2, 64, LANES), BF16),
+            jax.ShapeDtypeStruct((2 * share, 64, LANES), BF16),
+            jax.ShapeDtypeStruct((half_rows - 2 * share, 64, LANES), BF16),
         ],
         scratch_shapes=[
             pltpu.VMEM((2 * block_rows, 64, LANES), F32),
@@ -370,20 +367,21 @@
     got_first = across(give_first)
     got_rest = across(lax.optimization_barrier((give_rest, got_first))[0])
 
-    def local(kept, i):
-        got = got_first[i * half : (i + 1) * half] if i < 3 else got_rest[(i - 3) * half : (i - 2) * half]
-        return kept[i * half : (i + 1) * half] + got.astype(F32)
-
-    begin = lax.optimization_barrier((keep, *[local(keep, i).astype(BF16) for i in range(3)]))
+    def local(kept, i, count=1):
+        got = got_first[i * half : (i + count) * half] if i < 4 else got_rest[(i - 4) * half : (i - 4 + count) * half]
+        return kept[i * half : (i + count) * half] + got.astype(F32)
+
+    begin = lax.optimization_barrier(
+        (keep, local(keep, 0).astype(BF16), local(keep, 1, 2).astype(BF16), local(keep, 3).astype(BF16))
+    )
     far_sum = onward(begin[1], 2)
-    third = onward(begin[2], 1)
+    ahead = onward(begin[2], 1)
     third_twin = onward(begin[3], 1)
-    ones = lax.optimization_barrier((begin[0], local(begin[0], 3).astype(BF16), local(begin[0], 4).astype(BF16)))
-    by_one = onward(ones[1], 1)
-    by_one_twin = onward(ones[2], 1, 1, 1)
+    ones = lax.optimization_barrier((begin[0], local(begin[0], 4).astype(BF16)))
+    by_one_twin = onward(ones[1], 1, 1, 1)
     twos = lax.optimization_barrier((ones[0], (local(ones[0], 6) + third_twin.astype(F32)).astype(BF16)))
     by_two_twin = onward(twos[1], 2, 1, 1)
-    by_two = onward((local(twos[0], 5) + far_sum.astype(F32) + third.astype(F32)).astype(BF16), 2)
+    by_two = onward((local(twos[0], 5) + far_sum.astype(F32) + ahead[:half].astype(F32)).astype(BF16), 2)
     hamiltonian = pl.pallas_call(
         finish_kernel,
         in_specs=[vmem] * 6,
@@ -391,7 +389,7 @@
         out_shape=jax.ShapeDtypeStruct(density_blocks.shape, F32),
         compiler_params=params,
         name="finish",
-    )(keep, got_rest, by_one, by_two, by_one_twin, by_two_twin)
+    )(keep, got_rest, ahead, by_two, by_one_twin, by_two_twin)
     return potential.reshape(cells_x, cells_z, line_cells), hamiltonian
 
 

time: 116 us -> 116 us (level)
  starting transfers between devices: 28.8 us -> 30.9 us
  Pallas kernels: 24.4 us -> 22.8 us
    pallas_call x1, Pallas kernels: 10.7 us -> 9.04 us  [per_device(): pl.pallas_call(functools.partial(hamiltonian_kernel, places=sum_places, c...]
    ppermute x9, starting transfers between devices: 12.1 us -> 13.6 us  [across(): return lax.ppermute(values, 'height', twin)]
    ppermute x13 -> x12, waiting for transfers between devices: 14.5 us -> 15.2 us  [onward(): lax.ppermute(values, 'height', [(h, target(h)) for h in range(heights)])]
    ppermute x13 -> x12, starting transfers between devices: 16.6 us -> 17.3 us  [onward(): lax.ppermute(values, 'height', [(h, target(h)) for h in range(heights)])]
  transfers between devices with their start and end apart: 22 -> 21, of which waited for: 9 -> 8; matrix products, arithmetic and copies ran while one was open for 2% -> 2% of each run, Pallas kernels for 3% -> 3%
where the time goes in v7:
time: 116 us
  blocking collectives  40.2 us (35%)
  starting transfers between devices  30.9 us (27%)
  Pallas kernels  22.8 us (20%)
  waiting for transfers between devices  17.7 us (15%)
  local copies, waits for them, and re-layouts  2.59 us (2%)
    all_to_all x2, blocking collectives, exchange(): lax.all_to_all(values.reshape(devices, 1, LANES), ('col', 'height'), spli...  40.2 us
    ppermute x12, starting transfers between devices, onward(): lax.ppermute(values, 'height', [(h, target(h)) for h in range(heights)])  17.3 us
    ppermute x12, waiting for transfers between devices, onward(): lax.ppermute(values, 'height', [(h, target(h)) for h in range(heights)])  15.2 us
    ppermute x9, starting transfers between devices, across(): return lax.ppermute(values, 'height', twin)  13.6 us
    pallas_call x1, Pallas kernels, per_device(): pl.pallas_call(functools.partial(hamiltonian_kernel, places=sum_places, c...  9.04 us
    pallas_call x1, Pallas kernels, per_device(): pl.pallas_call(functools.partial(density_kernel, chunk=chunk, places=gath...  6.99 us
    pallas_call x1, Pallas kernels, per_device(): pl.pallas_call(stage_kernel, in_specs=[smem, pl.BlockSpec(memory_space=pl...  3.96 us
    ppermute x9, waiting for transfers between devices, across(): return lax.ppermute(values, 'height', twin)  2.53 us
  transfers between devices with their start and end apart: 21, of which 8 were waited for; matrix products, arithmetic and copies ran while one was open for 2% of the time, Pallas kernels for 3%

profile of v7, /device:TPU:1, one launch (start us, length us, event | category | flops | bytes accessed | tf_op | source)
XLA Modules:
  0.0 115.6 jit_solution(9074427413182054088)
XLA Ops:
  0.6 1.0 fusion.11
  1.7 3.3 %collective-permute-start = (bf16[8,64,128]{2,1,0:T(8,128)(2,1)S(1)}, bf16[8,64,128]{2,1,0:T(8,128)(2,1)S(1)}, u32[]{:S(2)}, u32[]{:S(2)}) collective-permute-start(bf16[8,64,128]{2,1,0:T(8,128)(2,1)S(1)} %pad_maximum_fusion.1), channel_id=1, source_target_pairs={{0,1},{1,0},{2,3},{3,2},{4,5},{5,4},{6,7},{7,6},{8,9},{9,8},{10,11... | collective-permute-start | bytes 393224 | tf_op jit(solution)/shard_map/ppermute | solution.py:262
  5.1 4.3 %collective-permute-start.3 = (bf16[8,64,128]{2,1,0:T(8,128)(2,1)S(1)}, bf16[8,64,128]{2,1,0:T(8,128)(2,1)S(1)}, u32[]{:S(2)}, u32[]{:S(2)}) collective-permute-start(bf16[8,64,128]{2,1,0:T(8,128)(2,1)S(1)} %pad_maximum_fusion.1), channel_id=1, source_target_pairs={{0,4},{1,13},{2,6},{3,15},{4,8},{5,1},{6,10},{7,3},{8,12},{9,5},{1... | collective-permute-start | bytes 393224 | tf_op jit(solution)/shard_map/ppermute | solution.py:269
  9.4 1.2 %copy.16 = s32[12,8,4,4]{3,2,1,0:T(4,128)S(1)} copy(s32[12,8,4,4]{0,3,2,1:T(4,128)} %param.13) | data formatting | bytes 12288 | tf_op args[2]
  12.5 4.0 %stage.1 = (bf16[96,256,128]{2,1,0:T(8,128)(2,1)S(1)}, s32[4,104]{1,0:T(4,128)S(1)}, s32[4]{0:T(128)S(1)}) custom-call(s32[96]{0:T(128)S(1)} %reshape.29.live_ref, bf16[96,256,128]{2,1,0:T(8,128)(2,1)} %bitcast.17), custom_call_target="tpu_custom_call" | custom-call | tf_op jit(solution)/shard_map/stage/pallas_call | solution.py:290
  17.2 2.5 %collective-permute-start.4 = (bf16[8,64,128]{2,1,0:T(8,128)(2,1)S(1)}, bf16[8,64,128]{2,1,0:T(8,128)(2,1)S(1)}, u32[]{:S(2)}, u32[]{:S(2)}) collective-permute-start(bf16[8,64,128]{2,1,0:T(8,128)(2,1)S(1)} %collective-permute-done.3.refs_1_), channel_id=1, source_target_pairs={{0,1},{1,0},{2,3},{3,2},{4,5},{5,4},{6,7},{7,6},{8,9},{9,8},{10,11... | collective-permute-start | bytes 393224 | tf_op jit(solution)/shard_map/ppermute | solution.py:262
  19.8 2.9 %collective-permute-start.9 = (bf16[8,64,128]{2,1,0:T(8,128)(2,1)S(1)}, bf16[8,64,128]{2,1,0:T(8,128)(2,1)S(1)}, u32[]{:S(2)}, u32[]{:S(2)}) collective-permute-start(bf16[8,64,128]{2,1,0:T(8,128)(2,1)S(1)} %collective-permute-done.1.refs_3_), channel_id=1, source_target_pairs={{0,2},{1,15},{2,4},{3,1},{4,6},{5,3},{6,8},{7,5},{8,10},{9,7},{10,... | collective-permute-start | bytes 393224 | tf_op jit(solution)/shard_map/ppermute | solution.py:269
  22.8 3.6 %collective-permute-start.12 = (bf16[8,64,128]{2,1,0:T(8,128)(2,1)S(1)}, bf16[8,64,128]{2,1,0:T(8,128)(2,1)S(1)}, u32[]{:S(2)}, u32[]{:S(2)}) collective-permute-start(bf16[8,64,128]{2,1,0:T(8,128)(2,1)S(1)} %collective-permute-done.11.refs_11_), channel_id=1, source_target_pairs={{0,1},{1,0},{2,3},{3,2},{4,5},{5,4},{6,7},{7,6},{8,9},{9,8},{10,11... | collective-permute-start | bytes 393224 | tf_op jit(solution)/shard_map/ppermute | solution.py:262
  26.3 1.2 %collective-permute-start.8 = (bf16[8,64,128]{2,1,0:T(8,128)(2,1)S(1)}, bf16[8,64,128]{2,1,0:T(8,128)(2,1)S(1)}, u32[]{:S(2)}, u32[]{:S(2)}) collective-permute-start(bf16[8,64,128]{2,1,0:T(8,128)(2,1)S(1)} %collective-permute-done.7.refs_7_), channel_id=1, source_target_pairs={{0,1},{1,0},{2,3},{3,2},{4,5},{5,4},{6,7},{7,6},{8,9},{9,8},{10,11... | collective-permute-start | bytes 393224 | tf_op jit(solution)/shard_map/ppermute | solution.py:262
  27.6 1.4 %collective-permute-start.10 = (bf16[8,64,128]{2,1,0:T(8,128)(2,1)S(1)}, bf16[8,64,128]{2,1,0:T(8,128)(2,1)S(1)}, u32[]{:S(2)}, u32[]{:S(2)}) collective-permute-start(bf16[8,64,128]{2,1,0:T(8,128)(2,1)S(1)} %collective-permute-done.9.refs_9_), channel_id=1, source_target_pairs={{0,1},{1,0},{2,3},{3,2},{4,5},{5,4},{6,7},{7,6},{8,9},{9,8},{10,11... | collective-permute-start | bytes 393224 | tf_op jit(solution)/shard_map/ppermute | solution.py:262
  29.0 1.0 collective-permute-done.10.refs_10_
  30.0 7.0 %density.1 = (f32[96,128]{1,0:T(8,128)S(1)}, f32[256,128]{1,0:T(8,128)S(1)}) custom-call(s32[1536]{0:T(1024)S(1)} %fusion.3.index_ref, s32[96]{0:T(128)S(1)} %reshape.29.live_ref, s32[3]{0:T(128)S(1)} %pad_add_fusion.part_ref.refs_0_, bf16[96,256,128]{2,1,0:T(8,128)(2,1)S(1)} %get-tuple-element.36.orb_ref, bf16[16,64,128]{2,1,0:T(8,128)(2,1)S(1)} %pad_maximum_fusion.refs_0_, ...), custom_call_target="tpu_custom_call" | custom-call | tf_op jit(solution)/shard_map/density/pallas_call | solution.py:311
  37.0 21.6 %all_to_all.10 = f32[256,1,128]{2,1,0:T(1,128)S(1)} all-to-all(f32[256,1,128]{2,1,0:T(1,128)S(1)} %bitcast.16), channel_id=1, replica_groups=mesh['col'=16,'height'=16] {'col','height'}, dimensions={0} | all-to-all | bytes 262144 | tf_op jit(solution)/shard_map/all_to_all | solution.py:325
  58.6 1.8 %solve.1 = f32[256,128]{1,0:T(8,128)S(1)} custom-call(s32[3]{0:T(128)S(1)} %pad_add_fusion.part_ref.refs_0_, f32[256,128]{1,0:T(8,128)S(1)} %bitcast.14, f32[2,96,192]{2,1,0:T(8,128)S(1)} %copy-done.2, f32[2,192,96]{2,1,0:T(8,128)S(1)} %copy-done.1, f32[128,128]{1,0:T(8,128)S(1)} %copy-done.4, f32[2,96,128]{2,1,0:T(8,128)S(1)} %copy-done.3, ...), custom_call_target="tpu_custom_call" | custom-call | tf_op jit(solution)/shard_map/solve/pallas_call | solution.py:328
  60.4 18.6 %all_to_all.11 = f32[256,1,128]{2,1,0:T(1,128)S(1)} all-to-all(f32[256,1,128]{2,1,0:T(1,128)S(1)} %bitcast.15), channel_id=1, replica_groups=mesh['col'=16,'height'=16] {'col','height'}, dimensions={0} | all-to-all | bytes 262144 | tf_op jit(solution)/shard_map/all_to_all | solution.py:325
  79.0 9.0 %hamiltonian.1 = (f32[96,128]{1,0:T(8,128)}, f32[64,64,128]{2,1,0:T(8,128)S(1)}, bf16[32,64,128]{2,1,0:T(8,128)(2,1)S(1)}, bf16[32,64,128]{2,1,0:T(8,128)(2,1)S(1)}) custom-call(s32[1536]{0:T(1024)S(1)} %reshape.28.pair_ref, s32[4,104]{1,0:T(4,128)S(1)} %get-tuple-element.33.order_ref, s32[4]{0:T(128)S(1)} %get-tuple-element.34.count_ref, ...), custom_call_target="tpu_custom_call" | custom-call | tf_op jit(solution)/shard_map/hamiltonian/pallas_call | solution.py:348
  88.0 1.3 %collective-permute-start.13 = (bf16[32,64,128]{2,1,0:T(8,128)(2,1)S(1)}, bf16[32,64,128]{2,1,0:T(8,128)(2,1)S(1)}, u32[]{:S(2)}, u32[]{:S(2)}) collective-permute-start(bf16[32,64,128]{2,1,0:T(8,128)(2,1)S(1)} %get-tuple-element.46), channel_id=1, source_target_pairs={{0,1},{1,0},{2,3},{3,2},{4,5},{5,4},{6,7},{7,6},{8,9},{9,8},{10,11... | collective-permute-start | bytes 1572872 | tf_op jit(solution)/shard_map/ppermute | solution.py:262
  89.3 1.5 %collective-permute-done.13 = bf16[32,64,128]{2,1,0:T(8,128)(2,1)S(1)} collective-permute-done((bf16[32,64,128]{2,1,0:T(8,128)(2,1)S(1)}, bf16[32,64,128]{2,1,0:T(8,128)(2,1)S(1)}, u32[]{:S(2)}, u32[]{:S(2)}) %collective-permute-start.13) | collective-permute-done | bytes 524320 | tf_op jit(solution)/shard_map/ppermute | solution.py:262
  92.3 1.2 %collective-permute-start.15 = (bf16[16,64,128]{2,1,0:T(8,128)(2,1)S(1)}, bf16[16,64,128]{2,1,0:T(8,128)(2,1)S(1)}, u32[]{:S(2)}, u32[]{:S(2)}) collective-permute-start(bf16[16,64,128]{2,1,0:T(8,128)(2,1)S(1)} %add_convert_fusion), channel_id=1, source_target_pairs={{0,2},{1,15},{2,4},{3,1},{4,6},{5,3},{6,8},{7,5},{8,10},{9,7},{10,... | collective-permute-start | bytes 786440 | tf_op jit(solution)/shard_map/ppermute | solution.py:269
  93.5 1.8 %collective-permute-done.16 = bf16[8,64,128]{2,1,0:T(8,128)(2,1)S(1)} collective-permute-done((bf16[8,64,128]{2,1,0:T(8,128)(2,1)S(1)}, bf16[8,64,128]{2,1,0:T(8,128)(2,1)S(1)}, u32[]{:S(2)}, u32[]{:S(2)}) %collective-permute-start.16) | collective-permute-done | bytes 131104 | tf_op jit(solution)/shard_map/ppermute | solution.py:269
  95.4 4.3 %collective-permute-done.17 = bf16[8,64,128]{2,1,0:T(8,128)(2,1)S(1)} collective-permute-done((bf16[8,64,128]{2,1,0:T(8,128)(2,1)S(1)}, bf16[8,64,128]{2,1,0:T(8,128)(2,1)S(1)}, u32[]{:S(2)}, u32[]{:S(2)}) %collective-permute-start.17) | collective-permute-done | bytes 131104 | tf_op jit(solution)/shard_map/ppermute | solution.py:269
  99.6 1.6 %collective-permute-done.15.one_ref = bf16[16,64,128]{2,1,0:T(8,128)(2,1)S(1)} collective-permute-done((bf16[16,64,128]{2,1,0:T(8,128)(2,1)S(1)}, bf16[16,64,128]{2,1,0:T(8,128)(2,1)S(1)}, u32[]{:S(2)}, u32[]{:S(2)}) %collective-permute-start.15) | collective-permute-done | bytes 262176 | tf_op jit(solution)/shard_map/ppermute | solution.py:269
  101.7 5.6 %collective-permute-start.20 = (bf16[8,64,128]{2,1,0:T(8,128)(2,1)S(1)}, bf16[8,64,128]{2,1,0:T(8,128)(2,1)S(1)}, u32[]{:S(2)}, u32[]{:S(2)}) collective-permute-start(bf16[8,64,128]{2,1,0:T(8,128)(2,1)S(1)} %add_convert_fusion.2), channel_id=1, source_target_pairs={{0,5},{1,12},{2,7},{3,14},{4,9},{5,0},{6,11},{7,2},{8,13},{9,4},{1... | collective-permute-start | bytes 393224 | tf_op jit(solution)/shard_map/ppermute | solution.py:269
  107.3 7.0 %collective-permute-done.20.twin_two_ref = bf16[8,64,128]{2,1,0:T(8,128)(2,1)S(1)} collective-permute-done((bf16[8,64,128]{2,1,0:T(8,128)(2,1)S(1)}, bf16[8,64,128]{2,1,0:T(8,128)(2,1)S(1)}, u32[]{:S(2)}, u32[]{:S(2)}) %collective-permute-start.20) | collective-permute-done | bytes 131104 | tf_op jit(solution)/shard_map/ppermute | solution.py:269
  (55 shorter events, 6.2 us)
Async XLA Ops:
  1.7 9.0 %collective-permute-start = (bf16[8,64,128]{2,1,0:T(8,128)(2,1)S(1)}, bf16[8,64,128]{2,1,0:T(8,128)(2,1)S(1)}, u32[]{:S(2)}, u32[]{:S(2)}) collective-permute-start(bf16[8,64,128]{2,1,0:T(8,128)(2,1)S(1)} %pad_maximum_fusion.1), channel_id=1, source_target_pairs={{0,1},{1,0},{2,3},{3,2},{4,5},{5,4},{6,7},{7,6},{8,9},{9,8},{10,11... | collective-permute-start | bytes 393224 | tf_op jit(solution)/shard_map/ppermute | solution.py:262
  5.1 11.4 %collective-permute-start.3 = (bf16[8,64,128]{2,1,0:T(8,128)(2,1)S(1)}, bf16[8,64,128]{2,1,0:T(8,128)(2,1)S(1)}, u32[]{:S(2)}, u32[]{:S(2)}) collective-permute-start(bf16[8,64,128]{2,1,0:T(8,128)(2,1)S(1)} %pad_maximum_fusion.1), channel_id=1, source_target_pairs={{0,4},{1,13},{2,6},{3,15},{4,8},{5,1},{6,10},{7,3},{8,12},{9,5},{1... | collective-permute-start | bytes 393224 | tf_op jit(solution)/shard_map/ppermute | solution.py:269
  10.9 8.8 %collective-permute-start.2 = (bf16[16,64,128]{2,1,0:T(8,128)(2,1)S(1)}, bf16[16,64,128]{2,1,0:T(8,128)(2,1)S(1)}, u32[]{:S(2)}, u32[]{:S(2)}) collective-permute-start(bf16[16,64,128]{2,1,0:T(8,128)(2,1)S(1)} %pad_maximum_fusion.refs_0_), channel_id=1, source_target_pairs={{0,2},{1,15},{2,4},{3,1},{4,6},{5,3},{6,8},{7,5},{8,10},{9,7},{10,... | collective-permute-start | bytes 786440 | tf_op jit(solution)/shard_map/ppermute | solution.py:269
  11.7 8.0 %collective-permute-start.1 = (bf16[8,64,128]{2,1,0:T(8,128)(2,1)S(1)}, bf16[8,64,128]{2,1,0:T(8,128)(2,1)S(1)}, u32[]{:S(2)}, u32[]{:S(2)}) collective-permute-start(bf16[8,64,128]{2,1,0:T(8,128)(2,1)S(1)} %collective-permute-done), channel_id=1, source_target_pairs={{0,4},{1,13},{2,6},{3,15},{4,8},{5,1},{6,10},{7,3},{8,12},{9,5},{1... | collective-permute-start | bytes 393224 | tf_op jit(solution)/shard_map/ppermute | solution.py:269
  16.5 6.3 %collective-permute-start.11 = (bf16[8,64,128]{2,1,0:T(8,128)(2,1)S(1)}, bf16[8,64,128]{2,1,0:T(8,128)(2,1)S(1)}, u32[]{:S(2)}, u32[]{:S(2)}) collective-permute-start(bf16[8,64,128]{2,1,0:T(8,128)(2,1)S(1)} %collective-permute-done.3.refs_1_), channel_id=1, source_target_pairs={{0,4},{1,13},{2,6},{3,15},{4,8},{5,1},{6,10},{7,3},{8,12},{9,5},{1... | collective-permute-start | bytes 393224 | tf_op jit(solution)/shard_map/ppermute | solution.py:269
  16.8 9.5 %collective-permute-start.7 = (bf16[8,64,128]{2,1,0:T(8,128)(2,1)S(1)}, bf16[8,64,128]{2,1,0:T(8,128)(2,1)S(1)}, u32[]{:S(2)}, u32[]{:S(2)}) collective-permute-start(bf16[8,64,128]{2,1,0:T(8,128)(2,1)S(1)} %collective-permute-done.3.refs_1_), channel_id=1, source_target_pairs={{0,2},{1,15},{2,4},{3,1},{4,6},{5,3},{6,8},{7,5},{8,10},{9,7},{10,... | collective-permute-start | bytes 393224 | tf_op jit(solution)/shard_map/ppermute | solution.py:269
  17.2 10.3 %collective-permute-start.4 = (bf16[8,64,128]{2,1,0:T(8,128)(2,1)S(1)}, bf16[8,64,128]{2,1,0:T(8,128)(2,1)S(1)}, u32[]{:S(2)}, u32[]{:S(2)}) collective-permute-start(bf16[8,64,128]{2,1,0:T(8,128)(2,1)S(1)} %collective-permute-done.3.refs_1_), channel_id=1, source_target_pairs={{0,1},{1,0},{2,3},{3,2},{4,5},{5,4},{6,7},{7,6},{8,9},{9,8},{10,11... | collective-permute-start | bytes 393224 | tf_op jit(solution)/shard_map/ppermute | solution.py:262
  19.7 38.8 %copy-start.1 = (f32[2,192,96]{2,1,0:T(8,128)S(1)}, f32[2,192,96]{2,1,0:T(8,128)}, u32[]{:S(2)}) copy-start(f32[2,192,96]{2,1,0:T(8,128)} %constant.99.clone.refs_3_) | copy-start | bytes 442372
  19.7 38.8 %copy-start.2 = (f32[2,96,192]{2,1,0:T(8,128)S(1)}, f32[2,96,192]{2,1,0:T(8,128)}, u32[]{:S(2)}) copy-start(f32[2,96,192]{2,1,0:T(8,128)} %constant.98.clone.refs_2_) | copy-start | bytes 442372
  19.7 38.8 %copy-start.3 = (f32[2,96,128]{2,1,0:T(8,128)S(1)}, f32[2,96,128]{2,1,0:T(8,128)}, u32[]{:S(2)}) copy-start(f32[2,96,128]{2,1,0:T(8,128)} %constant.101.clone.refs_5_) | copy-start | bytes 294916
  19.8 7.8 %collective-permute-start.9 = (bf16[8,64,128]{2,1,0:T(8,128)(2,1)S(1)}, bf16[8,64,128]{2,1,0:T(8,128)(2,1)S(1)}, u32[]{:S(2)}, u32[]{:S(2)}) collective-permute-start(bf16[8,64,128]{2,1,0:T(8,128)(2,1)S(1)} %collective-permute-done.1.refs_3_), channel_id=1, source_target_pairs={{0,2},{1,15},{2,4},{3,1},{4,6},{5,3},{6,8},{7,5},{8,10},{9,7},{10,... | collective-permute-start | bytes 393224 | tf_op jit(solution)/shard_map/ppermute | solution.py:269
  22.7 7.3 %collective-permute-start.6 = (bf16[16,64,128]{2,1,0:T(8,128)(2,1)S(1)}, bf16[16,64,128]{2,1,0:T(8,128)(2,1)S(1)}, u32[]{:S(2)}, u32[]{:S(2)}) collective-permute-start(bf16[16,64,128]{2,1,0:T(8,128)(2,1)S(1)} %collective-permute-done.2.refs_5_), channel_id=1, source_target_pairs={{0,1},{1,0},{2,3},{3,2},{4,5},{5,4},{6,7},{7,6},{8,9},{9,8},{10,11... | collective-permute-start | bytes 786440 | tf_op jit(solution)/shard_map/ppermute | solution.py:262
  22.8 6.2 %collective-permute-start.12 = (bf16[8,64,128]{2,1,0:T(8,128)(2,1)S(1)}, bf16[8,64,128]{2,1,0:T(8,128)(2,1)S(1)}, u32[]{:S(2)}, u32[]{:S(2)}) collective-permute-start(bf16[8,64,128]{2,1,0:T(8,128)(2,1)S(1)} %collective-permute-done.11.refs_11_), channel_id=1, source_target_pairs={{0,1},{1,0},{2,3},{3,2},{4,5},{5,4},{6,7},{7,6},{8,9},{9,8},{10,11... | collective-permute-start | bytes 393224 | tf_op jit(solution)/shard_map/ppermute | solution.py:262
  26.3 2.6 %collective-permute-start.8 = (bf16[8,64,128]{2,1,0:T(8,128)(2,1)S(1)}, bf16[8,64,128]{2,1,0:T(8,128)(2,1)S(1)}, u32[]{:S(2)}, u32[]{:S(2)}) collective-permute-start(bf16[8,64,128]{2,1,0:T(8,128)(2,1)S(1)} %collective-permute-done.7.refs_7_), channel_id=1, source_target_pairs={{0,1},{1,0},{2,3},{3,2},{4,5},{5,4},{6,7},{7,6},{8,9},{9,8},{10,11... | collective-permute-start | bytes 393224 | tf_op jit(solution)/shard_map/ppermute | solution.py:262
  27.6 1.4 %collective-permute-start.5 = (bf16[8,64,128]{2,1,0:T(8,128)(2,1)S(1)}, bf16[8,64,128]{2,1,0:T(8,128)(2,1)S(1)}, u32[]{:S(2)}, u32[]{:S(2)}) collective-permute-start(bf16[8,64,128]{2,1,0:T(8,128)(2,1)S(1)} %collective-permute-done.1.refs_3_), channel_id=1, source_target_pairs={{0,1},{1,0},{2,3},{3,2},{4,5},{5,4},{6,7},{7,6},{8,9},{9,8},{10,11... | collective-permute-start | bytes 393224 | tf_op jit(solution)/shard_map/ppermute | solution.py:262
  27.6 2.4 %collective-permute-start.10 = (bf16[8,64,128]{2,1,0:T(8,128)(2,1)S(1)}, bf16[8,64,128]{2,1,0:T(8,128)(2,1)S(1)}, u32[]{:S(2)}, u32[]{:S(2)}) collective-permute-start(bf16[8,64,128]{2,1,0:T(8,128)(2,1)S(1)} %collective-permute-done.9.refs_9_), channel_id=1, source_target_pairs={{0,1},{1,0},{2,3},{3,2},{4,5},{5,4},{6,7},{7,6},{8,9},{9,8},{10,11... | collective-permute-start | bytes 393224 | tf_op jit(solution)/shard_map/ppermute | solution.py:262
  88.0 2.8 %collective-permute-start.13 = (bf16[32,64,128]{2,1,0:T(8,128)(2,1)S(1)}, bf16[32,64,128]{2,1,0:T(8,128)(2,1)S(1)}, u32[]{:S(2)}, u32[]{:S(2)}) collective-permute-start(bf16[32,64,128]{2,1,0:T(8,128)(2,1)S(1)} %get-tuple-element.46), channel_id=1, source_target_pairs={{0,1},{1,0},{2,3},{3,2},{4,5},{5,4},{6,7},{7,6},{8,9},{9,8},{10,11... | collective-permute-start | bytes 1572872 | tf_op jit(solution)/shard_map/ppermute | solution.py:262
  90.8 2.6 %collective-permute-start.14 = (bf16[32,64,128]{2,1,0:T(8,128)(2,1)S(1)}, bf16[32,64,128]{2,1,0:T(8,128)(2,1)S(1)}, u32[]{:S(2)}, u32[]{:S(2)}) collective-permute-start(bf16[32,64,128]{2,1,0:T(8,128)(2,1)S(1)} %get-tuple-element.47), channel_id=1, source_target_pairs={{0,1},{1,0},{2,3},{3,2},{4,5},{5,4},{6,7},{7,6},{8,9},{9,8},{10,11... | collective-permute-start | bytes 1572872 | tf_op jit(solution)/shard_map/ppermute | solution.py:262
  91.4 3.9 %collective-permute-start.16 = (bf16[8,64,128]{2,1,0:T(8,128)(2,1)S(1)}, bf16[8,64,128]{2,1,0:T(8,128)(2,1)S(1)}, u32[]{:S(2)}, u32[]{:S(2)}) collective-permute-start(bf16[8,64,128]{2,1,0:T(8,128)(2,1)S(1)} %get-tuple-element.51), channel_id=1, source_target_pairs={{0,2},{1,15},{2,4},{3,1},{4,6},{5,3},{6,8},{7,5},{8,10},{9,7},{10,... | collective-permute-start | bytes 393224 | tf_op jit(solution)/shard_map/ppermute | solution.py:269
  91.6 8.1 %collective-permute-start.17 = (bf16[8,64,128]{2,1,0:T(8,128)(2,1)S(1)}, bf16[8,64,128]{2,1,0:T(8,128)(2,1)S(1)}, u32[]{:S(2)}, u32[]{:S(2)}) collective-permute-start(bf16[8,64,128]{2,1,0:T(8,128)(2,1)S(1)} %get-tuple-element.53), channel_id=1, source_target_pairs={{0,4},{1,13},{2,6},{3,15},{4,8},{5,1},{6,10},{7,3},{8,12},{9,5},{1... | collective-permute-start | bytes 393224 | tf_op jit(solution)/shard_map/ppermute | solution.py:269
  92.3 9.0 %collective-permute-start.15 = (bf16[16,64,128]{2,1,0:T(8,128)(2,1)S(1)}, bf16[16,64,128]{2,1,0:T(8,128)(2,1)S(1)}, u32[]{:S(2)}, u32[]{:S(2)}) collective-permute-start(bf16[16,64,128]{2,1,0:T(8,128)(2,1)S(1)} %add_convert_fusion), channel_id=1, source_target_pairs={{0,2},{1,15},{2,4},{3,1},{4,6},{5,3},{6,8},{7,5},{8,10},{9,7},{10,... | collective-permute-start | bytes 786440 | tf_op jit(solution)/shard_map/ppermute | solution.py:269
  101.3 5.9 %collective-permute-start.18 = (bf16[8,64,128]{2,1,0:T(8,128)(2,1)S(1)}, bf16[8,64,128]{2,1,0:T(8,128)(2,1)S(1)}, u32[]{:S(2)}, u32[]{:S(2)}) collective-permute-start(bf16[8,64,128]{2,1,0:T(8,128)(2,1)S(1)} %add_convert_fusion.1), channel_id=1, source_target_pairs={{0,4},{1,13},{2,6},{3,15},{4,8},{5,1},{6,10},{7,3},{8,12},{9,5},{1... | collective-permute-start | bytes 393224 | tf_op jit(solution)/shard_map/ppermute | solution.py:269
  101.7 12.6 %collective-permute-start.20 = (bf16[8,64,128]{2,1,0:T(8,128)(2,1)S(1)}, bf16[8,64,128]{2,1,0:T(8,128)(2,1)S(1)}, u32[]{:S(2)}, u32[]{:S(2)}) collective-permute-start(bf16[8,64,128]{2,1,0:T(8,128)(2,1)S(1)} %add_convert_fusion.2), channel_id=1, source_target_pairs={{0,5},{1,12},{2,7},{3,14},{4,9},{5,0},{6,11},{7,2},{8,13},{9,4},{1... | collective-permute-start | bytes 393224 | tf_op jit(solution)/shard_map/ppermute | solution.py:269
  107.3 7.4 %collective-permute-start.19 = (bf16[8,64,128]{2,1,0:T(8,128)(2,1)S(1)}, bf16[8,64,128]{2,1,0:T(8,128)(2,1)S(1)}, u32[]{:S(2)}, u32[]{:S(2)}) collective-permute-start(bf16[8,64,128]{2,1,0:T(8,128)(2,1)S(1)} %add_convert_fusion.3), channel_id=1, source_target_pairs={{0,3},{1,14},{2,5},{3,0},{4,7},{5,2},{6,9},{7,4},{8,11},{9,6},{10,... | collective-permute-start | bytes 393224 | tf_op jit(solution)/shard_map/ppermute | solution.py:269
  (5 other events, 145.6 us)

commit v8 on v7

--- a/solution.py
+++ b/solution.py
@@ -371,12 +371,10 @@
         got = got_first[i * half : (i + count) * half] if i < 4 else got_rest[(i - 4) * half : (i - 4 + count) * half]
         return kept[i * half : (i + count) * half] + got.astype(F32)
 
-    begin = lax.optimization_barrier(
-        (keep, local(keep, 0).astype(BF16), local(keep, 1, 2).astype(BF16), local(keep, 3).astype(BF16))
-    )
+    begin = lax.optimization_barrier((keep, local(keep, 0).astype(BF16), local(keep, 1, 3).astype(BF16)))
     far_sum = onward(begin[1], 2)
     ahead = onward(begin[2], 1)
-    third_twin = onward(begin[3], 1)
+    third_twin = ahead[2 * half :]
     ones = lax.optimization_barrier((begin[0], local(begin[0], 4).astype(BF16)))
     by_one_twin = onward(ones[1], 1, 1, 1)
     twos = lax.optimization_barrier((ones[0], (local(ones[0], 6) + third_twin.astype(F32)).astype(BF16)))

time: 116 us -> 116 us (level)
  waiting for transfers between devices: 17.7 us -> 19.8 us
  starting transfers between devices: 30.9 us -> 28.8 us
    ppermute x12 -> x11, waiting for transfers between devices: 15.2 us -> 17.2 us  [onward(): lax.ppermute(values, 'height', [(h, target(h)) for h in range(heights)])]
    ppermute x12 -> x11, starting transfers between devices: 17.3 us -> 15.4 us  [onward(): lax.ppermute(values, 'height', [(h, target(h)) for h in range(heights)])]
  transfers between devices with their start and end apart: 21 -> 20, of which waited for: 8 -> 9; matrix products, arithmetic and copies ran while one was open for 2% -> 2% of each run, Pallas kernels for 3% -> 3%
where the time goes in v8:
time: 116 us
  blocking collectives  40.2 us (35%)
  starting transfers between devices  28.8 us (25%)
  Pallas kernels  23 us (20%)
  waiting for transfers between devices  19.8 us (17%)
  local copies, waits for them, and re-layouts  2.59 us (2%)
    all_to_all x2, blocking collectives, exchange(): lax.all_to_all(values.reshape(devices, 1, LANES), ('col', 'height'), spli...  40.2 us
    ppermute x11, waiting for transfers between devices, onward(): lax.ppermute(values, 'height', [(h, target(h)) for h in range(heights)])  17.2 us
    ppermute x11, starting transfers between devices, onward(): lax.ppermute(values, 'height', [(h, target(h)) for h in range(heights)])  15.4 us
    ppermute x9, starting transfers between devices, across(): return lax.ppermute(values, 'height', twin)  13.4 us
    pallas_call x1, Pallas kernels, per_device(): pl.pallas_call(functools.partial(hamiltonian_kernel, places=sum_places, c...  9.24 us
    pallas_call x1, Pallas kernels, per_device(): pl.pallas_call(functools.partial(density_kernel, chunk=chunk, places=gath...  6.99 us
    pallas_call x1, Pallas kernels, per_device(): pl.pallas_call(stage_kernel, in_specs=[smem, pl.BlockSpec(memory_space=pl...  3.96 us
    ppermute x9, waiting for transfers between devices, across(): return lax.ppermute(values, 'height', twin)  2.64 us
  transfers between devices with their start and end apart: 20, of which 9 were waited for; matrix products, arithmetic and copies ran while one was open for 2% of the time, Pallas kernels for 3%

profile of v8, /device:TPU:1, one launch (start us, length us, event | category | flops | bytes accessed | tf_op | source)
XLA Modules:
  0.0 115.8 jit_solution(14908591659706395580)
XLA Ops:
  0.6 1.0 fusion.11
  1.7 3.3 %collective-permute-start = (bf16[8,64,128]{2,1,0:T(8,128)(2,1)S(1)}, bf16[8,64,128]{2,1,0:T(8,128)(2,1)S(1)}, u32[]{:S(2)}, u32[]{:S(2)}) collective-permute-start(bf16[8,64,128]{2,1,0:T(8,128)(2,1)S(1)} %pad_maximum_fusion.1), channel_id=1, source_target_pairs={{0,1},{1,0},{2,3},{3,2},{4,5},{5,4},{6,7},{7,6},{8,9},{9,8},{10,11... | collective-permute-start | bytes 393224 | tf_op jit(solution)/shard_map/ppermute | solution.py:262
  5.1 4.3 %collective-permute-start.3 = (bf16[8,64,128]{2,1,0:T(8,128)(2,1)S(1)}, bf16[8,64,128]{2,1,0:T(8,128)(2,1)S(1)}, u32[]{:S(2)}, u32[]{:S(2)}) collective-permute-start(bf16[8,64,128]{2,1,0:T(8,128)(2,1)S(1)} %pad_maximum_fusion.1), channel_id=1, source_target_pairs={{0,4},{1,13},{2,6},{3,15},{4,8},{5,1},{6,10},{7,3},{8,12},{9,5},{1... | collective-permute-start | bytes 393224 | tf_op jit(solution)/shard_map/ppermute | solution.py:269
  9.4 1.2 %copy.16 = s32[12,8,4,4]{3,2,1,0:T(4,128)S(1)} copy(s32[12,8,4,4]{0,3,2,1:T(4,128)} %param.13) | data formatting | bytes 12288 | tf_op args[2]
  12.5 4.0 %stage.1 = (bf16[96,256,128]{2,1,0:T(8,128)(2,1)S(1)}, s32[4,104]{1,0:T(4,128)S(1)}, s32[4]{0:T(128)S(1)}) custom-call(s32[96]{0:T(128)S(1)} %reshape.29.live_ref, bf16[96,256,128]{2,1,0:T(8,128)(2,1)} %bitcast.17), custom_call_target="tpu_custom_call" | custom-call | tf_op jit(solution)/shard_map/stage/pallas_call | solution.py:290
  17.2 2.5 %collective-permute-start.4 = (bf16[8,64,128]{2,1,0:T(8,128)(2,1)S(1)}, bf16[8,64,128]{2,1,0:T(8,128)(2,1)S(1)}, u32[]{:S(2)}, u32[]{:S(2)}) collective-permute-start(bf16[8,64,128]{2,1,0:T(8,128)(2,1)S(1)} %collective-permute-done.3.refs_1_), channel_id=1, source_target_pairs={{0,1},{1,0},{2,3},{3,2},{4,5},{5,4},{6,7},{7,6},{8,9},{9,8},{10,11... | collective-permute-start | bytes 393224 | tf_op jit(solution)/shard_map/ppermute | solution.py:262
  19.8 2.9 %collective-permute-start.9 = (bf16[8,64,128]{2,1,0:T(8,128)(2,1)S(1)}, bf16[8,64,128]{2,1,0:T(8,128)(2,1)S(1)}, u32[]{:S(2)}, u32[]{:S(2)}) collective-permute-start(bf16[8,64,128]{2,1,0:T(8,128)(2,1)S(1)} %collective-permute-done.1.refs_3_), channel_id=1, source_target_pairs={{0,2},{1,15},{2,4},{3,1},{4,6},{5,3},{6,8},{7,5},{8,10},{9,7},{10,... | collective-permute-start | bytes 393224 | tf_op jit(solution)/shard_map/ppermute | solution.py:269
  22.8 3.6 %collective-permute-start.12 = (bf16[8,64,128]{2,1,0:T(8,128)(2,1)S(1)}, bf16[8,64,128]{2,1,0:T(8,128)(2,1)S(1)}, u32[]{:S(2)}, u32[]{:S(2)}) collective-permute-start(bf16[8,64,128]{2,1,0:T(8,128)(2,1)S(1)} %collective-permute-done.11.refs_11_), channel_id=1, source_target_pairs={{0,1},{1,0},{2,3},{3,2},{4,5},{5,4},{6,7},{7,6},{8,9},{9,8},{10,11... | collective-permute-start | bytes 393224 | tf_op jit(solution)/shard_map/ppermute | solution.py:262
  26.3 1.2 %collective-permute-start.8 = (bf16[8,64,128]{2,1,0:T(8,128)(2,1)S(1)}, bf16[8,64,128]{2,1,0:T(8,128)(2,1)S(1)}, u32[]{:S(2)}, u32[]{:S(2)}) collective-permute-start(bf16[8,64,128]{2,1,0:T(8,128)(2,1)S(1)} %collective-permute-done.7.refs_7_), channel_id=1, source_target_pairs={{0,1},{1,0},{2,3},{3,2},{4,5},{5,4},{6,7},{7,6},{8,9},{9,8},{10,11... | collective-permute-start | bytes 393224 | tf_op jit(solution)/shard_map/ppermute | solution.py:262
  27.6 1.4 %collective-permute-start.10 = (bf16[8,64,128]{2,1,0:T(8,128)(2,1)S(1)}, bf16[8,64,128]{2,1,0:T(8,128)(2,1)S(1)}, u32[]{:S(2)}, u32[]{:S(2)}) collective-permute-start(bf16[8,64,128]{2,1,0:T(8,128)(2,1)S(1)} %collective-permute-done.9.refs_9_), channel_id=1, source_target_pairs={{0,1},{1,0},{2,3},{3,2},{4,5},{5,4},{6,7},{7,6},{8,9},{9,8},{10,11... | collective-permute-start | bytes 393224 | tf_op jit(solution)/shard_map/ppermute | solution.py:262
  30.0 7.0 %density.1 = (f32[96,128]{1,0:T(8,128)S(1)}, f32[256,128]{1,0:T(8,128)S(1)}) custom-call(s32[1536]{0:T(1024)S(1)} %fusion.3.index_ref, s32[96]{0:T(128)S(1)} %reshape.29.live_ref, s32[3]{0:T(128)S(1)} %pad_add_fusion.part_ref.refs_0_, bf16[96,256,128]{2,1,0:T(8,128)(2,1)S(1)} %get-tuple-element.35.orb_ref, bf16[16,64,128]{2,1,0:T(8,128)(2,1)S(1)} %pad_maximum_fusion.refs_0_, ...), custom_call_target="tpu_custom_call" | custom-call | tf_op jit(solution)/shard_map/density/pallas_call | solution.py:311
  37.0 21.6 %all_to_all.10 = f32[256,1,128]{2,1,0:T(1,128)S(1)} all-to-all(f32[256,1,128]{2,1,0:T(1,128)S(1)} %bitcast.16), channel_id=1, replica_groups=mesh['col'=16,'height'=16] {'col','height'}, dimensions={0} | all-to-all | bytes 262144 | tf_op jit(solution)/shard_map/all_to_all | solution.py:325
  58.6 1.8 %solve.1 = f32[256,128]{1,0:T(8,128)S(1)} custom-call(s32[3]{0:T(128)S(1)} %pad_add_fusion.part_ref.refs_0_, f32[256,128]{1,0:T(8,128)S(1)} %bitcast.14, f32[2,96,192]{2,1,0:T(8,128)S(1)} %copy-done.2, f32[2,192,96]{2,1,0:T(8,128)S(1)} %copy-done.1, f32[128,128]{1,0:T(8,128)S(1)} %copy-done.4, f32[2,96,128]{2,1,0:T(8,128)S(1)} %copy-done.3, ...), custom_call_target="tpu_custom_call" | custom-call | tf_op jit(solution)/shard_map/solve/pallas_call | solution.py:328
  60.4 18.6 %all_to_all.11 = f32[256,1,128]{2,1,0:T(1,128)S(1)} all-to-all(f32[256,1,128]{2,1,0:T(1,128)S(1)} %bitcast.15), channel_id=1, replica_groups=mesh['col'=16,'height'=16] {'col','height'}, dimensions={0} | all-to-all | bytes 262144 | tf_op jit(solution)/shard_map/all_to_all | solution.py:325
  79.0 9.2 %hamiltonian.1 = (f32[96,128]{1,0:T(8,128)}, f32[64,64,128]{2,1,0:T(8,128)S(1)}, bf16[32,64,128]{2,1,0:T(8,128)(2,1)S(1)}, bf16[32,64,128]{2,1,0:T(8,128)(2,1)S(1)}) custom-call(s32[1536]{0:T(1024)S(1)} %reshape.28.pair_ref, s32[4,104]{1,0:T(4,128)S(1)} %get-tuple-element.32.order_ref, s32[4]{0:T(128)S(1)} %get-tuple-element.33.count_ref, ...), custom_call_target="tpu_custom_call" | custom-call | tf_op jit(solution)/shard_map/hamiltonian/pallas_call | solution.py:348
  88.2 1.0 collective-permute-start.13
  89.3 1.5 %collective-permute-done.13 = bf16[32,64,128]{2,1,0:T(8,128)(2,1)S(1)} collective-permute-done((bf16[32,64,128]{2,1,0:T(8,128)(2,1)S(1)}, bf16[32,64,128]{2,1,0:T(8,128)(2,1)S(1)}, u32[]{:S(2)}, u32[]{:S(2)}) %collective-permute-start.13) | collective-permute-done | bytes 524320 | tf_op jit(solution)/shard_map/ppermute | solution.py:262
  92.7 5.9 %collective-permute-done.15.one_ref = bf16[24,64,128]{2,1,0:T(8,128)(2,1)S(1)} collective-permute-done((bf16[24,64,128]{2,1,0:T(8,128)(2,1)S(1)}, bf16[24,64,128]{2,1,0:T(8,128)(2,1)S(1)}, u32[]{:S(2)}, u32[]{:S(2)}) %collective-permute-start.15) | collective-permute-done | bytes 393248 | tf_op jit(solution)/shard_map/ppermute | solution.py:269
  98.7 3.6 %collective-permute-done.16 = bf16[8,64,128]{2,1,0:T(8,128)(2,1)S(1)} collective-permute-done((bf16[8,64,128]{2,1,0:T(8,128)(2,1)S(1)}, bf16[8,64,128]{2,1,0:T(8,128)(2,1)S(1)}, u32[]{:S(2)}, u32[]{:S(2)}) %collective-permute-start.16) | collective-permute-done | bytes 131104 | tf_op jit(solution)/shard_map/ppermute | solution.py:269
  102.4 1.6 %collective-permute-start.17 = (bf16[8,64,128]{2,1,0:T(8,128)(2,1)S(1)}, bf16[8,64,128]{2,1,0:T(8,128)(2,1)S(1)}, u32[]{:S(2)}, u32[]{:S(2)}) collective-permute-start(bf16[8,64,128]{2,1,0:T(8,128)(2,1)S(1)} %add_convert_fusion.1), channel_id=1, source_target_pairs={{0,4},{1,13},{2,6},{3,15},{4,8},{5,1},{6,10},{7,3},{8,12},{9,5},{1... | collective-permute-start | bytes 393224 | tf_op jit(solution)/shard_map/ppermute | solution.py:269
  104.0 1.9 %collective-permute-start.19 = (bf16[8,64,128]{2,1,0:T(8,128)(2,1)S(1)}, bf16[8,64,128]{2,1,0:T(8,128)(2,1)S(1)}, u32[]{:S(2)}, u32[]{:S(2)}) collective-permute-start(bf16[8,64,128]{2,1,0:T(8,128)(2,1)S(1)} %add_convert_fusion.2), channel_id=1, source_target_pairs={{0,5},{1,12},{2,7},{3,14},{4,9},{5,0},{6,11},{7,2},{8,13},{9,4},{1... | collective-permute-start | bytes 393224 | tf_op jit(solution)/shard_map/ppermute | solution.py:269
  105.9 1.3 %collective-permute-start.18 = (bf16[8,64,128]{2,1,0:T(8,128)(2,1)S(1)}, bf16[8,64,128]{2,1,0:T(8,128)(2,1)S(1)}, u32[]{:S(2)}, u32[]{:S(2)}) collective-permute-start(bf16[8,64,128]{2,1,0:T(8,128)(2,1)S(1)} %add_convert_fusion.3), channel_id=1, source_target_pairs={{0,3},{1,14},{2,5},{3,0},{4,7},{5,2},{6,9},{7,4},{8,11},{9,6},{10,... | collective-permute-start | bytes 393224 | tf_op jit(solution)/shard_map/ppermute | solution.py:269
  108.2 4.3 %collective-permute-done.19.twin_two_ref = bf16[8,64,128]{2,1,0:T(8,128)(2,1)S(1)} collective-permute-done((bf16[8,64,128]{2,1,0:T(8,128)(2,1)S(1)}, bf16[8,64,128]{2,1,0:T(8,128)(2,1)S(1)}, u32[]{:S(2)}, u32[]{:S(2)}) %collective-permute-start.19) | collective-permute-done | bytes 131104 | tf_op jit(solution)/shard_map/ppermute | solution.py:269
  112.5 2.3 %collective-permute-done.18.twin_one_ref = bf16[8,64,128]{2,1,0:T(8,128)(2,1)S(1)} collective-permute-done((bf16[8,64,128]{2,1,0:T(8,128)(2,1)S(1)}, bf16[8,64,128]{2,1,0:T(8,128)(2,1)S(1)}, u32[]{:S(2)}, u32[]{:S(2)}) %collective-permute-start.18) | collective-permute-done | bytes 131104 | tf_op jit(solution)/shard_map/ppermute | solution.py:269
  (53 shorter events, 7.8 us)
Async XLA Ops:
  1.7 9.0 %collective-permute-start = (bf16[8,64,128]{2,1,0:T(8,128)(2,1)S(1)}, bf16[8,64,128]{2,1,0:T(8,128)(2,1)S(1)}, u32[]{:S(2)}, u32[]{:S(2)}) collective-permute-start(bf16[8,64,128]{2,1,0:T(8,128)(2,1)S(1)} %pad_maximum_fusion.1), channel_id=1, source_target_pairs={{0,1},{1,0},{2,3},{3,2},{4,5},{5,4},{6,7},{7,6},{8,9},{9,8},{10,11... | collective-permute-start | bytes 393224 | tf_op jit(solution)/shard_map/ppermute | solution.py:262
  5.1 11.4 %collective-permute-start.3 = (bf16[8,64,128]{2,1,0:T(8,128)(2,1)S(1)}, bf16[8,64,128]{2,1,0:T(8,128)(2,1)S(1)}, u32[]{:S(2)}, u32[]{:S(2)}) collective-permute-start(bf16[8,64,128]{2,1,0:T(8,128)(2,1)S(1)} %pad_maximum_fusion.1), channel_id=1, source_target_pairs={{0,4},{1,13},{2,6},{3,15},{4,8},{5,1},{6,10},{7,3},{8,12},{9,5},{1... | collective-permute-start | bytes 393224 | tf_op jit(solution)/shard_map/ppermute | solution.py:269
  10.9 8.8 %collective-permute-start.2 = (bf16[16,64,128]{2,1,0:T(8,128)(2,1)S(1)}, bf16[16,64,128]{2,1,0:T(8,128)(2,1)S(1)}, u32[]{:S(2)}, u32[]{:S(2)}) collective-permute-start(bf16[16,64,128]{2,1,0:T(8,128)(2,1)S(1)} %pad_maximum_fusion.refs_0_), channel_id=1, source_target_pairs={{0,2},{1,15},{2,4},{3,1},{4,6},{5,3},{6,8},{7,5},{8,10},{9,7},{10,... | collective-permute-start | bytes 786440 | tf_op jit(solution)/shard_map/ppermute | solution.py:269
  11.7 8.0 %collective-permute-start.1 = (bf16[8,64,128]{2,1,0:T(8,128)(2,1)S(1)}, bf16[8,64,128]{2,1,0:T(8,128)(2,1)S(1)}, u32[]{:S(2)}, u32[]{:S(2)}) collective-permute-start(bf16[8,64,128]{2,1,0:T(8,128)(2,1)S(1)} %collective-permute-done), channel_id=1, source_target_pairs={{0,4},{1,13},{2,6},{3,15},{4,8},{5,1},{6,10},{7,3},{8,12},{9,5},{1... | collective-permute-start | bytes 393224 | tf_op jit(solution)/shard_map/ppermute | solution.py:269
  16.5 6.3 %collective-permute-start.11 = (bf16[8,64,128]{2,1,0:T(8,128)(2,1)S(1)}, bf16[8,64,128]{2,1,0:T(8,128)(2,1)S(1)}, u32[]{:S(2)}, u32[]{:S(2)}) collective-permute-start(bf16[8,64,128]{2,1,0:T(8,128)(2,1)S(1)} %collective-permute-done.3.refs_1_), channel_id=1, source_target_pairs={{0,4},{1,13},{2,6},{3,15},{4,8},{5,1},{6,10},{7,3},{8,12},{9,5},{1... | collective-permute-start | bytes 393224 | tf_op jit(solution)/shard_map/ppermute | solution.py:269
  16.8 9.5 %collective-permute-start.7 = (bf16[8,64,128]{2,1,0:T(8,128)(2,1)S(1)}, bf16[8,64,128]{2,1,0:T(8,128)(2,1)S(1)}, u32[]{:S(2)}, u32[]{:S(2)}) collective-permute-start(bf16[8,64,128]{2,1,0:T(8,128)(2,1)S(1)} %collective-permute-done.3.refs_1_), channel_id=1, source_target_pairs={{0,2},{1,15},{2,4},{3,1},{4,6},{5,3},{6,8},{7,5},{8,10},{9,7},{10,... | collective-permute-start | bytes 393224 | tf_op jit(solution)/shard_map/ppermute | solution.py:269
  17.2 10.3 %collective-permute-start.4 = (bf16[8,64,128]{2,1,0:T(8,128)(2,1)S(1)}, bf16[8,64,128]{2,1,0:T(8,128)(2,1)S(1)}, u32[]{:S(2)}, u32[]{:S(2)}) collective-permute-start(bf16[8,64,128]{2,1,0:T(8,128)(2,1)S(1)} %collective-permute-done.3.refs_1_), channel_id=1, source_target_pairs={{0,1},{1,0},{2,3},{3,2},{4,5},{5,4},{6,7},{7,6},{8,9},{9,8},{10,11... | collective-permute-start | bytes 393224 | tf_op jit(solution)/shard_map/ppermute | solution.py:262
  19.7 38.8 %copy-start.1 = (f32[2,192,96]{2,1,0:T(8,128)S(1)}, f32[2,192,96]{2,1,0:T(8,128)}, u32[]{:S(2)}) copy-start(f32[2,192,96]{2,1,0:T(8,128)} %constant.99.clone.refs_3_) | copy-start | bytes 442372
  19.7 38.8 %copy-start.2 = (f32[2,96,192]{2,1,0:T(8,128)S(1)}, f32[2,96,192]{2,1,0:T(8,128)}, u32[]{:S(2)}) copy-start(f32[2,96,192]{2,1,0:T(8,128)} %constant.98.clone.refs_2_) | copy-start | bytes 442372
  19.7 38.8 %copy-start.3 = (f32[2,96,128]{2,1,0:T(8,128)S(1)}, f32[2,96,128]{2,1,0:T(8,128)}, u32[]{:S(2)}) copy-start(f32[2,96,128]{2,1,0:T(8,128)} %constant.101.clone.refs_5_) | copy-start | bytes 294916
  19.7 38.8 %copy-start.4 = (f32[128,128]{1,0:T(8,128)S(1)}, f32[128,128]{1,0:T(8,128)}, u32[]{:S(2)}) copy-start(f32[128,128]{1,0:T(8,128)} %constant.100.clone.refs_4_) | copy-start | bytes 196612
  19.8 7.8 %collective-permute-start.9 = (bf16[8,64,128]{2,1,0:T(8,128)(2,1)S(1)}, bf16[8,64,128]{2,1,0:T(8,128)(2,1)S(1)}, u32[]{:S(2)}, u32[]{:S(2)}) collective-permute-start(bf16[8,64,128]{2,1,0:T(8,128)(2,1)S(1)} %collective-permute-done.1.refs_3_), channel_id=1, source_target_pairs={{0,2},{1,15},{2,4},{3,1},{4,6},{5,3},{6,8},{7,5},{8,10},{9,7},{10,... | collective-permute-start | bytes 393224 | tf_op jit(solution)/shard_map/ppermute | solution.py:269
  22.7 7.3 %collective-permute-start.6 = (bf16[16,64,128]{2,1,0:T(8,128)(2,1)S(1)}, bf16[16,64,128]{2,1,0:T(8,128)(2,1)S(1)}, u32[]{:S(2)}, u32[]{:S(2)}) collective-permute-start(bf16[16,64,128]{2,1,0:T(8,128)(2,1)S(1)} %collective-permute-done.2.refs_5_), channel_id=1, source_target_pairs={{0,1},{1,0},{2,3},{3,2},{4,5},{5,4},{6,7},{7,6},{8,9},{9,8},{10,11... | collective-permute-start | bytes 786440 | tf_op jit(solution)/shard_map/ppermute | solution.py:262
  22.8 6.2 %collective-permute-start.12 = (bf16[8,64,128]{2,1,0:T(8,128)(2,1)S(1)}, bf16[8,64,128]{2,1,0:T(8,128)(2,1)S(1)}, u32[]{:S(2)}, u32[]{:S(2)}) collective-permute-start(bf16[8,64,128]{2,1,0:T(8,128)(2,1)S(1)} %collective-permute-done.11.refs_11_), channel_id=1, source_target_pairs={{0,1},{1,0},{2,3},{3,2},{4,5},{5,4},{6,7},{7,6},{8,9},{9,8},{10,11... | collective-permute-start | bytes 393224 | tf_op jit(solution)/shard_map/ppermute | solution.py:262
  26.3 2.6 %collective-permute-start.8 = (bf16[8,64,128]{2,1,0:T(8,128)(2,1)S(1)}, bf16[8,64,128]{2,1,0:T(8,128)(2,1)S(1)}, u32[]{:S(2)}, u32[]{:S(2)}) collective-permute-start(bf16[8,64,128]{2,1,0:T(8,128)(2,1)S(1)} %collective-permute-done.7.refs_7_), channel_id=1, source_target_pairs={{0,1},{1,0},{2,3},{3,2},{4,5},{5,4},{6,7},{7,6},{8,9},{9,8},{10,11... | collective-permute-start | bytes 393224 | tf_op jit(solution)/shard_map/ppermute | solution.py:262
  27.6 1.4 %collective-permute-start.5 = (bf16[8,64,128]{2,1,0:T(8,128)(2,1)S(1)}, bf16[8,64,128]{2,1,0:T(8,128)(2,1)S(1)}, u32[]{:S(2)}, u32[]{:S(2)}) collective-permute-start(bf16[8,64,128]{2,1,0:T(8,128)(2,1)S(1)} %collective-permute-done.1.refs_3_), channel_id=1, source_target_pairs={{0,1},{1,0},{2,3},{3,2},{4,5},{5,4},{6,7},{7,6},{8,9},{9,8},{10,11... | collective-permute-start | bytes 393224 | tf_op jit(solution)/shard_map/ppermute | solution.py:262
  27.6 2.4 %collective-permute-start.10 = (bf16[8,64,128]{2,1,0:T(8,128)(2,1)S(1)}, bf16[8,64,128]{2,1,0:T(8,128)(2,1)S(1)}, u32[]{:S(2)}, u32[]{:S(2)}) collective-permute-start(bf16[8,64,128]{2,1,0:T(8,128)(2,1)S(1)} %collective-permute-done.9.refs_9_), channel_id=1, source_target_pairs={{0,1},{1,0},{2,3},{3,2},{4,5},{5,4},{6,7},{7,6},{8,9},{9,8},{10,11... | collective-permute-start | bytes 393224 | tf_op jit(solution)/shard_map/ppermute | solution.py:262
  88.2 2.5 %collective-permute-start.13 = (bf16[32,64,128]{2,1,0:T(8,128)(2,1)S(1)}, bf16[32,64,128]{2,1,0:T(8,128)(2,1)S(1)}, u32[]{:S(2)}, u32[]{:S(2)}) collective-permute-start(bf16[32,64,128]{2,1,0:T(8,128)(2,1)S(1)} %get-tuple-element.45), channel_id=1, source_target_pairs={{0,1},{1,0},{2,3},{3,2},{4,5},{5,4},{6,7},{7,6},{8,9},{9,8},{10,11... | collective-permute-start | bytes 1572872 | tf_op jit(solution)/shard_map/ppermute | solution.py:262
  90.8 1.9 %collective-permute-start.14 = (bf16[32,64,128]{2,1,0:T(8,128)(2,1)S(1)}, bf16[32,64,128]{2,1,0:T(8,128)(2,1)S(1)}, u32[]{:S(2)}, u32[]{:S(2)}) collective-permute-start(bf16[32,64,128]{2,1,0:T(8,128)(2,1)S(1)} %get-tuple-element.46), channel_id=1, source_target_pairs={{0,1},{1,0},{2,3},{3,2},{4,5},{5,4},{6,7},{7,6},{8,9},{9,8},{10,11... | collective-permute-start | bytes 1572872 | tf_op jit(solution)/shard_map/ppermute | solution.py:262
  91.3 7.3 %collective-permute-start.15 = (bf16[24,64,128]{2,1,0:T(8,128)(2,1)S(1)}, bf16[24,64,128]{2,1,0:T(8,128)(2,1)S(1)}, u32[]{:S(2)}, u32[]{:S(2)}) collective-permute-start(bf16[24,64,128]{2,1,0:T(8,128)(2,1)S(1)} %add_convert_fusion), channel_id=1, source_target_pairs={{0,2},{1,15},{2,4},{3,1},{4,6},{5,3},{6,8},{7,5},{8,10},{9,7},{10,... | collective-permute-start | bytes 1179656 | tf_op jit(solution)/shard_map/ppermute | solution.py:269
  92.3 10.0 %collective-permute-start.16 = (bf16[8,64,128]{2,1,0:T(8,128)(2,1)S(1)}, bf16[8,64,128]{2,1,0:T(8,128)(2,1)S(1)}, u32[]{:S(2)}, u32[]{:S(2)}) collective-permute-start(bf16[8,64,128]{2,1,0:T(8,128)(2,1)S(1)} %add_convert_fusion.4), channel_id=1, source_target_pairs={{0,4},{1,13},{2,6},{3,15},{4,8},{5,1},{6,10},{7,3},{8,12},{9,5},{1... | collective-permute-start | bytes 393224 | tf_op jit(solution)/shard_map/ppermute | solution.py:269
  102.4 5.8 %collective-permute-start.17 = (bf16[8,64,128]{2,1,0:T(8,128)(2,1)S(1)}, bf16[8,64,128]{2,1,0:T(8,128)(2,1)S(1)}, u32[]{:S(2)}, u32[]{:S(2)}) collective-permute-start(bf16[8,64,128]{2,1,0:T(8,128)(2,1)S(1)} %add_convert_fusion.1), channel_id=1, source_target_pairs={{0,4},{1,13},{2,6},{3,15},{4,8},{5,1},{6,10},{7,3},{8,12},{9,5},{1... | collective-permute-start | bytes 393224 | tf_op jit(solution)/shard_map/ppermute | solution.py:269
  104.0 8.5 %collective-permute-start.19 = (bf16[8,64,128]{2,1,0:T(8,128)(2,1)S(1)}, bf16[8,64,128]{2,1,0:T(8,128)(2,1)S(1)}, u32[]{:S(2)}, u32[]{:S(2)}) collective-permute-start(bf16[8,64,128]{2,1,0:T(8,128)(2,1)S(1)} %add_convert_fusion.2), channel_id=1, source_target_pairs={{0,5},{1,12},{2,7},{3,14},{4,9},{5,0},{6,11},{7,2},{8,13},{9,4},{1... | collective-permute-start | bytes 393224 | tf_op jit(solution)/shard_map/ppermute | solution.py:269
  105.9 8.9 %collective-permute-start.18 = (bf16[8,64,128]{2,1,0:T(8,128)(2,1)S(1)}, bf16[8,64,128]{2,1,0:T(8,128)(2,1)S(1)}, u32[]{:S(2)}, u32[]{:S(2)}) collective-permute-start(bf16[8,64,128]{2,1,0:T(8,128)(2,1)S(1)} %add_convert_fusion.3), channel_id=1, source_target_pairs={{0,3},{1,14},{2,5},{3,0},{4,7},{5,2},{6,9},{7,4},{8,11},{9,6},{10,... | collective-permute-start | bytes 393224 | tf_op jit(solution)/shard_map/ppermute | solution.py:269
  (4 other events, 106.7 us)
